TPU v7x, 128 devices: a whole 4x4x4 slice. The times are simulated.
128 devices in a mesh: dp: 16 (over z, x_hi, core), seq: 8 (over x_lo, y).
Axes of the slice: x: 4 (x_hi: 2, x_lo: 2; x = x_hi * 2 + x_lo), y: 4, z: 4, core: 2. Of those that a mesh axis runs over, the one named last changes fastest.
Arguments:
- tokens: bfloat16 [32768, 1152], P(('dp', 'seq')), may hold values from -6 to 6
- cotangent: bfloat16 [32768, 1152], P(('dp', 'seq')), may hold values from -6 to 6
- lengths: int32 [16], P('dp'), may hold values from 1793 to 2048, as said below
- query_weight: bfloat16 [1152, 1024], P('dp'), may hold values from -0.1875 to 0.1875
- key_weight: bfloat16 [1152, 256], P('dp'), may hold values from -0.1875 to 0.1875
- value_weight: bfloat16 [1152, 256], P('dp'), may hold values from -0.1875 to 0.1875
- out_weight: bfloat16 [1152, 1024], P('dp'), may hold values from -0.1875 to 0.1875
- gate_weight: bfloat16 [1152, 6912], P('dp'), may hold values from -0.1875 to 0.1875
- up_weight: bfloat16 [1152, 6912], P('dp'), may hold values from -0.1875 to 0.1875
- down_weight: bfloat16 [1152, 6912], P('dp'), may hold values from -0.078125 to 0.078125
- input_gain: bfloat16 [1152], P('dp'), may hold values from -0.5 to 0.5
- query_gain: bfloat16 [256], P('dp'), may hold values from -0.5 to 0.5
- key_gain: bfloat16 [256], P('dp'), may hold values from -0.5 to 0.5
- attention_gain: bfloat16 [1152], P('dp'), may hold values from -0.5 to 0.5
- feedforward_gain: bfloat16 [1152], P('dp'), may hold values from -0.5 to 0.5
- output_gain: bfloat16 [1152], P('dp'), may hold values from -0.5 to 0.5
Outputs:
- layer_output: bfloat16 [32768, 1152], P(('dp', 'seq'))
- tokens_grad: bfloat16 [32768, 1152], P(('dp', 'seq'))
- query_weight_grad: float32 [1152, 1024], P('dp')
- key_weight_grad: float32 [1152, 256], P('dp')
- value_weight_grad: float32 [1152, 256], P('dp')
- out_weight_grad: float32 [1152, 1024], P('dp')
- gate_weight_grad: float32 [1152, 6912], P('dp')
- up_weight_grad: float32 [1152, 6912], P('dp')
- down_weight_grad: float32 [1152, 6912], P('dp')
- input_gain_grad: float32 [1152], P('dp')
- query_gain_grad: float32 [256], P('dp')
- key_gain_grad: float32 [256], P('dp')
- attention_gain_grad: float32 [1152], P('dp')
- feedforward_gain_grad: float32 [1152], P('dp')
- output_gain_grad: float32 [1152], P('dp')
Inputs may be any that keep to these rules, and one draw needn't show every extreme that they name: lengths[g] counts the true tokens of sequence g, which fill the first rows of its 2048; the rest are padding. In every draw some sequence is full.
All inputs are finite; a program needn't handle non-finite values.
Results may differ from a plain program's by a relative error of at most 0.033.
Values may be sent and summed in bfloat16 or wider, within the bound.
No kernel may reach another device: no remote copies, remote signals or barrier semaphores. Data moves between devices by JAX's collectives and lax.ppermute only.
A program may use at most 256 MiB of HBM per device.

v0:
```python
import math

import jax
import jax.numpy as jnp
from jax import lax
from jax.sharding import PartitionSpec as P

WINDOW = 512


EPSILON = 1e-06
GELU_COEFF = 0.044715


def from_behind(array, axis, by):
    devices = lax.axis_size(axis)
    pairs = [(i, i + by) for i in range(devices) if 0 <= i + by < devices]
    return lax.ppermute(array, axis, pairs)


def inverse_rms(values):
    return lax.rsqrt(jnp.mean(values * values, axis=-1, keepdims=True) + EPSILON)


def rms_backward(values, scaling, upstream):
    inner = jnp.mean(upstream * values, axis=-1, keepdims=True)
    return scaling * (upstream - values * (scaling * scaling) * inner)


def rotary_tables(positions, head_size):
    half_size = head_size // 2
    exponents = lax.iota(jnp.float32, half_size) * (2.0 / head_size)
    frequency = jnp.power(10000.0, -exponents)
    angles = positions.astype(jnp.float32)[:, None] * frequency[None, :]
    return (jnp.cos(angles), jnp.sin(angles))


def rotate(values, cosine_table, sine_table):
    half_size = values.shape[-1] // 2
    first_half = values[..., :half_size]
    second_half = values[..., half_size:]
    return jnp.concatenate(
        [
            first_half * cosine_table - second_half * sine_table,
            second_half * cosine_table + first_half * sine_table,
        ],
        axis=-1,
    )


def rotate_back(upstream, cosine_table, sine_table):
    half_size = upstream.shape[-1] // 2
    first_half = upstream[..., :half_size]
    second_half = upstream[..., half_size:]
    return jnp.concatenate(
        [
            first_half * cosine_table + second_half * sine_table,
            second_half * cosine_table - first_half * sine_table,
        ],
        axis=-1,
    )


def gelu_parts(values):
    root_coeff = math.sqrt(2.0 / math.pi)
    bend = jnp.tanh(root_coeff * (values + GELU_COEFF * values * values * values))
    gelu_value = 0.5 * values * (1.0 + bend)
    gelu_slope = 0.5 * (1.0 + bend) + 0.5 * values * (1.0 - bend * bend) * root_coeff * (
        1.0 + 3.0 * GELU_COEFF * values * values
    )
    return (gelu_value, gelu_slope)


def local(
    tokens,
    cotangent,
    lengths,
    query_weight,
    key_weight,
    value_weight,
    out_weight,
    gate_weight,
    up_weight,
    down_weight,
    input_gain,
    query_gain,
    key_gain,
    attention_gain,
    feedforward_gain,
    output_gain,
):
    row_count, model_width = tokens.shape
    head_size = key_weight.shape[1]
    head_count = query_weight.shape[1] // head_size
    query_width = head_count * head_size
    feed_width = gate_weight.shape[1]
    scaling_factor = head_size ** (-0.5)
    seq_count = lax.axis_size("seq")
    data_count = lax.axis_size("dp")
    seq_index = lax.axis_index("seq")
    positions = seq_index * row_count + lax.iota(jnp.int32, row_count)
    valid_rows = (positions < lengths[0]).astype(jnp.float32)[:, None]
    cosine_table, sine_table = rotary_tables(positions, head_size)
    hop_total = min((WINDOW + row_count - 2) // row_count, seq_count - 1)
    gathered = (
        lax.all_gather(query_weight, "dp", axis=0, tiled=True),
        lax.all_gather(key_weight, "dp", axis=0, tiled=True),
        lax.all_gather(value_weight, "dp", axis=0, tiled=True),
        lax.all_gather(out_weight, "dp", axis=0, tiled=True),
        lax.all_gather(input_gain, "dp", axis=0, tiled=True),
        lax.all_gather(query_gain, "dp", axis=0, tiled=True),
        lax.all_gather(key_gain, "dp", axis=0, tiled=True),
        lax.all_gather(attention_gain, "dp", axis=0, tiled=True),
        lax.all_gather(feedforward_gain, "dp", axis=0, tiled=True),
        lax.all_gather(output_gain, "dp", axis=0, tiled=True),
    )
    full_query, full_key, full_value, full_out = (
        gathered[0],
        gathered[1],
        gathered[2],
        gathered[3],
    )
    one_input = 1.0 + gathered[4].astype(jnp.float32)
    one_query = 1.0 + gathered[5].astype(jnp.float32)
    one_key = 1.0 + gathered[6].astype(jnp.float32)
    one_attention = 1.0 + gathered[7].astype(jnp.float32)
    one_feed = 1.0 + gathered[8].astype(jnp.float32)
    one_output = 1.0 + gathered[9].astype(jnp.float32)
    residual = tokens.astype(jnp.float32)
    input_scale = inverse_rms(residual)
    normed_input = residual * input_scale
    attention_input = (normed_input * one_input).astype(jnp.bfloat16)
    query_raw = jnp.dot(attention_input, full_query, preferred_element_type=jnp.float32)
    key_raw = jnp.dot(attention_input, full_key, preferred_element_type=jnp.float32)
    value_raw = jnp.dot(attention_input, full_value, preferred_element_type=jnp.float32)
    query_heads = query_raw.reshape(row_count, head_count, head_size)
    query_scale = inverse_rms(query_heads)
    query_hat = query_heads * query_scale
    query_low = rotate(
        query_hat * one_query, cosine_table[:, None, :], sine_table[:, None, :]
    ).astype(jnp.bfloat16)
    key_scale = inverse_rms(key_raw)
    key_hat = key_raw * key_scale
    key_low = rotate(key_hat * one_key, cosine_table, sine_table).astype(jnp.bfloat16)
    value_low = value_raw.astype(jnp.bfloat16)
    local_pair = jnp.concatenate([key_low, value_low], axis=1)
    rim_blocks = []
    for distance in range(1, hop_total + 1):
        rim_blocks.append(from_behind(local_pair, "seq", distance))
    key_rows = jnp.concatenate(rim_blocks[::-1] + [local_pair], axis=0)
    key_count = key_rows.shape[0]
    key_positions = (seq_index - hop_total) * row_count + lax.iota(jnp.int32, key_count)
    offsets = positions[:, None] - key_positions[None, :]
    allowed = (offsets >= 0) & (offsets < WINDOW) & (key_positions[None, :] >= 0)
    keys_only = key_rows[:, :head_size]
    values_only = key_rows[:, head_size:]

    def masked_scores():
        raw_scores = (
            jnp.einsum("thd,kd->htk", query_low, keys_only, preferred_element_type=jnp.float32)
            * scaling_factor
        )
        return jnp.where(allowed[None], raw_scores, -1e30)

    masked = masked_scores()
    row_top = jnp.max(masked, axis=-1, keepdims=True)
    exponent_terms = jnp.exp(masked - row_top)
    row_total = jnp.sum(exponent_terms, axis=-1, keepdims=True)
    log_total = row_top + jnp.log(row_total)
    probs_low = (exponent_terms / row_total).astype(jnp.bfloat16)
    context = jnp.einsum("htk,kd->thd", probs_low, values_only, preferred_element_type=jnp.float32)
    context_low = context.reshape(row_count, query_width).astype(jnp.bfloat16)
    attention_raw = jnp.einsum(
        "tq,dq->td", context_low, full_out, preferred_element_type=jnp.float32
    )
    attention_scale = inverse_rms(attention_raw)
    attention_hat = attention_raw * attention_scale
    hidden_state = residual + attention_hat * one_attention
    state_scale = inverse_rms(hidden_state)
    state_hat = hidden_state * state_scale
    feed_input = (state_hat * one_feed).astype(jnp.bfloat16)
    pieces = (
        lax.all_gather(gate_weight, "dp", axis=0, tiled=True),
        lax.all_gather(up_weight, "dp", axis=0, tiled=True),
    )
    columns = feed_input
    gate_raw = jnp.dot(columns, pieces[0], preferred_element_type=jnp.float32)
    up_raw = jnp.dot(columns, pieces[1], preferred_element_type=jnp.float32)
    gelu_value, gelu_slope = gelu_parts(gate_raw)
    hidden_low = (gelu_value * up_raw).astype(jnp.bfloat16)
    down_raw = jnp.einsum(
        "tf,df->td",
        hidden_low,
        lax.all_gather(down_weight, "dp", axis=0, tiled=True),
        preferred_element_type=jnp.float32,
    )
    down_scale = inverse_rms(down_raw)
    down_hat = down_raw * down_scale
    layer_value = hidden_state + down_hat * one_output
    layer_output = (valid_rows * layer_value).astype(jnp.bfloat16)
    upstream = cotangent.astype(jnp.float32) * valid_rows
    output_gain_vec = jnp.sum(upstream * down_hat, axis=0)
    down_grad_low = rms_backward(down_raw, down_scale, upstream * one_output).astype(jnp.bfloat16)
    columns = down_grad_low
    hidden_grad = jnp.dot(
        columns,
        lax.all_gather(down_weight, "dp", axis=0, tiled=True),
        preferred_element_type=jnp.float32,
    )
    gate_grad_low = (hidden_grad * up_raw * gelu_slope).astype(jnp.bfloat16)
    up_grad_low = (hidden_grad * gelu_value).astype(jnp.bfloat16)
    pieces = (
        lax.all_gather(gate_weight, "dp", axis=0, tiled=True),
        lax.all_gather(up_weight, "dp", axis=0, tiled=True),
    )
    block_part = jnp.einsum(
        "tf,df->td", gate_grad_low, pieces[0], preferred_element_type=jnp.float32
    )
    block_part = block_part + jnp.einsum(
        "tf,df->td", up_grad_low, pieces[1], preferred_element_type=jnp.float32
    )
    feed_gain_vec = jnp.sum(block_part * state_hat, axis=0)
    state_grad = upstream + rms_backward(hidden_state, state_scale, block_part * one_feed)
    attention_gain_vec = jnp.sum(state_grad * attention_hat, axis=0)
    attention_grad_low = rms_backward(
        attention_raw, attention_scale, state_grad * one_attention
    ).astype(jnp.bfloat16)
    regathered = (
        lax.all_gather(query_weight, "dp", axis=0, tiled=True),
        lax.all_gather(key_weight, "dp", axis=0, tiled=True),
        lax.all_gather(value_weight, "dp", axis=0, tiled=True),
        lax.all_gather(out_weight, "dp", axis=0, tiled=True),
    )
    back_query, back_key, back_value, back_out = (
        regathered[0],
        regathered[1],
        regathered[2],
        regathered[3],
    )
    context_grad = jnp.einsum(
        "td,dq->tq", attention_grad_low, back_out, preferred_element_type=jnp.float32
    )
    context_grad_low = context_grad.reshape(row_count, head_count, head_size).astype(jnp.bfloat16)
    probs_again = jnp.exp(masked_scores() - log_total)
    probs_again_low = probs_again.astype(jnp.bfloat16)
    prob_grad = jnp.einsum(
        "thd,kd->htk", context_grad_low, values_only, preferred_element_type=jnp.float32
    )
    score_grad = probs_again * (
        prob_grad - jnp.sum(probs_again * prob_grad, axis=-1, keepdims=True)
    )
    score_grad_low = score_grad.astype(jnp.bfloat16)
    query_rot_grad = (
        jnp.einsum("htk,kd->thd", score_grad_low, keys_only, preferred_element_type=jnp.float32)
        * scaling_factor
    )
    key_rot_rows = (
        jnp.einsum("htk,thd->kd", score_grad_low, query_low, preferred_element_type=jnp.float32)
        * scaling_factor
    )
    value_rows = jnp.einsum(
        "htk,thd->kd", probs_again_low, context_grad_low, preferred_element_type=jnp.float32
    )
    pair_grad = jnp.concatenate([key_rot_rows, value_rows], axis=1)
    local_grad = pair_grad[hop_total * row_count :]
    for distance in range(1, hop_total + 1):
        begin_row = (hop_total - distance) * row_count
        local_grad = local_grad + from_behind(
            pair_grad[begin_row : begin_row + row_count].astype(jnp.bfloat16), "seq", -distance
        ).astype(jnp.float32)
    key_norm_grad = rotate_back(local_grad[:, :head_size], cosine_table, sine_table)
    key_gain_vec = jnp.sum(key_norm_grad * key_hat, axis=0)
    key_raw_low = rms_backward(key_raw, key_scale, key_norm_grad * one_key).astype(jnp.bfloat16)
    value_raw_low = local_grad[:, head_size:].astype(jnp.bfloat16)
    query_norm_grad = rotate_back(query_rot_grad, cosine_table[:, None, :], sine_table[:, None, :])
    query_gain_vec = jnp.sum(query_norm_grad * query_hat, axis=(0, 1))
    query_raw_low = (
        rms_backward(query_heads, query_scale, query_norm_grad * one_query)
        .reshape(row_count, query_width)
        .astype(jnp.bfloat16)
    )
    input_grad = jnp.einsum(
        "tq,dq->td", query_raw_low, back_query, preferred_element_type=jnp.float32
    )
    input_grad = input_grad + jnp.einsum(
        "tq,dq->td", key_raw_low, back_key, preferred_element_type=jnp.float32
    )
    input_grad = input_grad + jnp.einsum(
        "tq,dq->td", value_raw_low, back_value, preferred_element_type=jnp.float32
    )
    input_gain_vec = jnp.sum(input_grad * normed_input, axis=0)
    tokens_grad = (state_grad + rms_backward(residual, input_scale, input_grad * one_input)).astype(
        jnp.bfloat16
    )
    gain_shard = input_gain.shape[0]
    head_shard = query_gain.shape[0]

    def spread_head(vector):
        return jnp.pad(
            vector.reshape(data_count, head_shard), ((0, 0), (0, gain_shard - head_shard))
        ).reshape(model_width)

    gain_columns = jnp.stack(
        [
            input_gain_vec,
            attention_gain_vec,
            feed_gain_vec,
            output_gain_vec,
            spread_head(query_gain_vec),
            spread_head(key_gain_vec),
        ],
        axis=1,
    )
    gain_block = jnp.pad(gain_columns, ((0, 0), (0, 122)))
    grad_part = lax.psum_scatter(
        jnp.concatenate(
            [
                jnp.einsum(
                    "tc,tf->cf", feed_input, gate_grad_low, preferred_element_type=jnp.float32
                ),
                jnp.einsum(
                    "tc,tf->cf", feed_input, up_grad_low, preferred_element_type=jnp.float32
                ),
                jnp.einsum(
                    "tc,tf->cf", down_grad_low, hidden_low, preferred_element_type=jnp.float32
                ),
                jnp.einsum(
                    "tc,tq->cq", attention_input, query_raw_low, preferred_element_type=jnp.float32
                ),
                jnp.einsum(
                    "tc,tq->cq", attention_input, key_raw_low, preferred_element_type=jnp.float32
                ),
                jnp.einsum(
                    "tc,tq->cq", attention_input, value_raw_low, preferred_element_type=jnp.float32
                ),
                jnp.einsum(
                    "tc,tq->cq", attention_grad_low, context_low, preferred_element_type=jnp.float32
                ),
                gain_block,
            ],
            axis=1,
        ).astype(jnp.bfloat16),
        "dp",
        scatter_dimension=0,
        tiled=True,
    ).astype(jnp.float32)
    grad_part = lax.psum(grad_part.astype(jnp.bfloat16), "seq").astype(jnp.float32)
    feed_part = grad_part[:, : 3 * feed_width]
    attention_part = grad_part[:, 3 * feed_width :]
    value_start = query_width + head_size
    out_start = query_width + 2 * head_size
    tail_start = 2 * query_width + 2 * head_size
    gain_tail = attention_part[:, tail_start:]
    return (
        layer_output,
        tokens_grad,
        attention_part[:, :query_width],
        attention_part[:, query_width:value_start],
        attention_part[:, value_start:out_start],
        attention_part[:, out_start:tail_start],
        feed_part[:, :feed_width],
        feed_part[:, feed_width : 2 * feed_width],
        feed_part[:, 2 * feed_width :],
        gain_tail[:, 0],
        gain_tail[:head_shard, 4],
        gain_tail[:head_shard, 5],
        gain_tail[:, 1],
        gain_tail[:, 2],
        gain_tail[:, 3],
    )


def solution(mesh):
    return jax.shard_map(
        local,
        mesh=mesh,
        in_specs=(
            P(("dp", "seq"), None),
            P(("dp", "seq"), None),
            P("dp"),
            P("dp", None),
            P("dp", None),
            P("dp", None),
            P("dp", None),
            P("dp", None),
            P("dp", None),
            P("dp", None),
            P("dp"),
            P("dp"),
            P("dp"),
            P("dp"),
            P("dp"),
            P("dp"),
        ),
        out_specs=(
            P(("dp", "seq"), None),
            P(("dp", "seq"), None),
            P("dp", None),
            P("dp", None),
            P("dp", None),
            P("dp", None),
            P("dp", None),
            P("dp", None),
            P("dp", None),
            P("dp"),
            P("dp"),
            P("dp"),
            P("dp"),
            P("dp"),
            P("dp"),
        ),
        check_vma=False,
    )
```

profile of v0, /device:TPU:0, one launch (start us, length us, event | category | flops | bytes accessed | tf_op | source)
XLA Modules:
  0.0 1242.0 jit_solution(9089543273622509428)
XLA Ops:
  14.1 71.1 %all-reduce.10 = (bf16[1152]{0:T(1024)(128)(2,1)S(1)}, bf16[256]{0:T(256)(128)(2,1)S(1)}, bf16[256]{0:T(256)(128)(2,1)S(1)}, bf16[1152]{0:T(1024)(128)(2,1)S(1)}...) all-reduce(bf16[1152]{0:T(1024)(128)(2,1)S(1)} %dynamic-update-slic, ...), channel_id=1, replica_groups=mesh['dp'=16,'seq'=8] {'dp'}, use_global_device_ids=true, to_apply=%add.3 | all-reduce | flops 5120 | bytes 20480
  86.0 24.4 %all_gather.47 = bf16[1152,256]{1,0:T(8,128)(2,1)S(1)} all-gather(bf16[72,256]{1,0:T(8,128)(2,1)S(1)} %copy-done.36), channel_id=1, replica_groups=mesh['dp'=16,'seq'=8] {'dp'}, dimensions={0}, use_global_device_ids=true | all-gather | bytes 626688 | tf_op jit(solution)/shard_map/all_gather | solution.py:107
  111.7 26.2 %all_gather.49 = bf16[1152,256]{1,0:T(8,128)(2,1)S(1)} all-gather(bf16[72,256]{1,0:T(8,128)(2,1)S(1)} %copy-done.37), channel_id=1, replica_groups=mesh['dp'=16,'seq'=8] {'dp'}, dimensions={0}, use_global_device_ids=true | all-gather | bytes 626688 | tf_op jit(solution)/shard_map/all_gather | solution.py:108
  138.8 3.5 collective-permute-start.1
  142.2 4.8 collective-permute-start
  149.0 4.9 collective-permute-done
  154.8 2.6 fusion.77
  165.6 2.9 multiply_reduce_fusion.8
  171.8 48.8 %all-gather.10.cloned.1.call-done = bf16[1152,6912]{1,0:T(8,128)(2,1)} async-done(((bf16[72,6912]{1,0:T(8,128)(2,1)}), bf16[1152,6912]{1,0:T(8,128)(2,1)}) %all-gather.10.cloned.1.call-update) | async-done | bytes 15925264 | tf_op jit(solution)/shard_map/all_gather | solution.py:183
  220.6 13.4 %fusion.88 = f32[256,6912]{1,0:T(8,128)} fusion(bf16[256,1152]{1,0:T(8,128)(2,1)} %multiply_convert_fusion.5, bf16[1152,6912]{1,0:T(8,128)(2,1)} %all-gather.10.cloned.1.call-done), kind=kOutput, calls=%fused_computation.185 | convolution fusion | flops 4076863488 | bytes 23592960 | tf_op jit(solution)/shard_map/dot_general | solution.py:187
  234.0 92.0 %all-gather.12.cloned.1.call-done = bf16[1152,6912]{1,0:T(8,128)(2,1)} async-done(((bf16[72,6912]{1,0:T(8,128)(2,1)}), bf16[1152,6912]{1,0:T(8,128)(2,1)}) %all-gather.12.cloned.1.call-update) | async-done | bytes 15925264 | tf_op jit(solution)/shard_map/all_gather | solution.py:184
  326.0 13.1 %multiply_convert_fusion.1 = (bf16[256,6912]{1,0:T(8,128)(2,1)}, f32[256,6912]{1,0:T(8,128)}) fusion(f32[256,6912]{1,0:T(8,128)} %fusion.88, bf16[256,1152]{1,0:T(8,128)(2,1)} %multiply_convert_fusion.5, bf16[1152,6912]{1,0:T(8,128)(2,1)} %all-gather.12.cloned.1.call-done), kind=kOutput, calls=%fused_computation.16 | convolution fusion | flops 4094558208 | bytes 34209792 | tf_op jit(solution)/shard_map/dot_general | solution.py:188
  339.2 92.2 %all-gather.14.cloned.1.call-done = bf16[1152,6912]{1,0:T(8,128)(2,1)} async-done(((bf16[72,6912]{1,0:T(8,128)(2,1)}), bf16[1152,6912]{1,0:T(8,128)(2,1)}) %all-gather.14.cloned.1.call-update) | async-done | bytes 15925264 | tf_op jit(solution)/shard_map/all_gather | solution.py:194
  431.4 12.4 multiply_reduce_fusion.6
  443.8 3.3 multiply_reduce_fusion
  447.1 18.6 %multiply_convert_fusion = (bf16[256,6912]{1,0:T(8,128)(2,1)}, bf16[256,6912]{1,0:T(8,128)(2,1)}) fusion(f32[256,6912]{1,0:T(8,128)} %fusion.88, f32[256,6912]{1,0:T(8,128)} %get-tuple-element.85, bf16[1152,6912]{1,0:T(8,128)(2,1)} %all-gather.14.cloned.1.call-done, f32[256,1152]{1,0:T(8,128)S(1)} %copy-done.30, bf16[256,1152]{1,0:T(8,128)(2,1)S(1)} %copy-done.17, ...), kind=kOutput, calls=%fused_computation.15 | convolution fusion | flops 4119920640 | bytes 38937088 | tf_op jit(solution)/shard_map/dot_general | solution.py:205
  465.6 12.4 fusion.89
  478.0 13.0 %multiply_reduce_fusion.1 = (bf16[1152]{0:T(1024)(128)(2,1)S(1)}, f32[256]{0:T(256)S(1)}, f32[256,1152]{1,0:T(8,128)}) fusion(f32[256,1152]{1,0:T(8,128)} %copy-done.3, f32[256]{0:T(256)S(1)} %get-tuple-element.75, f32[1152]{0:T(1024)S(1)} %convert_add_fusion.2, f32[256,1152]{1,0:T(8,128)} %fusion.89, bf16[256,6912]{1,0:T(8,128)(2,1)} %get-tuple-element.40, ...), kind=kOutput, calls=%fused_computation.71 | convolution fusion | flops 4078926592 | bytes 23012096 | tf_op jit(solution)/shard_map/tf,df->td/dot_general | solution.py:219
  491.1 3.0 multiply_reduce_fusion.2
  498.0 2.0 copy.191
  500.1 1.9 fusion.12
  508.1 12.3 fusion
  528.4 12.2 fusion.1
  540.6 12.8 %fusion.2 = bf16[1152,23424]{1,0:T(8,128)(2,1)} fusion(bf16[1152,23424]{1,0:T(8,128)(2,1)} %fusion.1, bf16[256,6912]{1,0:T(8,128)(2,1)} %get-tuple-element.84, f32[256,1152]{1,0:T(8,128)} %get-tuple-element.87, bf16[256,1152]{1,0:T(8,128)(2,1)S(1)} %copy-done.18, f32[256]{0:T(256)S(1)} %broadcast_multiply_fusion.5, f32[256]{0:T(256)S(1)} %get-tuple-element.76, ...), kind=kOutput, calls=%fused_computation.5 | convolution fusion | flops 4087185408 | bytes 21242368 | tf_op jit(solution)/shard_map/tc,tf->cf/dot_general | solution.py:324
  553.4 3.6 multiply_reduce_fusion.9
  557.3 2.8 fusion.90
  560.1 2.4 fusion.11
  568.9 2.3 fusion.10
  572.6 561.1 %reduce-scatter.5.cloned.1.call-done = bf16[72,23424]{1,0:T(8,128)(2,1)} async-done(((bf16[1152,23424]{1,0:T(8,128)(2,1)}), bf16[72,23424]{1,0:T(8,128)(2,1)}) %reduce-scatter.5.cloned.1.call-update) | async-done | bytes 3373072
  1136.2 90.2 %all-reduce.13.cloned.1.call-done = bf16[72,23424]{1,0:T(8,128)(2,1)} async-done(((bf16[72,23424]{1,0:T(8,128)(2,1)}), bf16[72,23424]{1,0:T(8,128)(2,1)}) %all-reduce.13.cloned.1.call-update) | async-done | bytes 3373072 | tf_op jit(solution)/shard_map/psum | solution.py:347
  1226.4 2.5 convert_element_type.152
  1231.9 2.7 fusion.83
  (221 shorter events, 53.3 us)
Async XLA Ops:
  7.2 147.7 %all-gather.6.cloned.1.call-start = ((), (), s32[]{:S(2)}) async-start(), calls=%async_computation.1 | async-start | bytes 2506752 | tf_op jit(solution)/shard_map/all_gather | solution.py:106
  7.9 2.8 copy-start.45
  7.9 4.7 copy-start.39
  7.9 4.9 copy-start.40
  7.9 5.2 copy-start.41
  8.0 5.4 copy-start.42
  8.0 5.7 copy-start.43
  8.0 5.9 copy-start.44
  8.0 77.2 %copy-start.8 = (bf16[256,1152]{1,0:T(8,128)(2,1)S(1)}, bf16[256,1152]{1,0:T(8,128)(2,1)}, u32[]{:S(2)}) copy-start(bf16[256,1152]{1,0:T(8,128)(2,1)} %param.16) | copy-start | bytes 1769476
  8.0 157.5 %all-gather.8.cloned.1.call-start = ((), (), s32[]{:S(2)}) async-start(), calls=%async_computation.2 | async-start | bytes 2506752 | tf_op jit(solution)/shard_map/all_gather | solution.py:109
  8.8 211.9 %all-gather.10.cloned.1.call-start = ((), (), s32[]{:S(2)}) async-start(), calls=%async_computation.3 | async-start | bytes 16920576 | tf_op jit(solution)/shard_map/all_gather | solution.py:183
  9.5 76.5 %copy-start.36 = (bf16[72,256]{1,0:T(8,128)(2,1)S(1)}, bf16[72,256]{1,0:T(8,128)(2,1)}, u32[]{:S(2)}) copy-start(bf16[72,256]{1,0:T(8,128)(2,1)} %param.20) | copy-start | bytes 110596
  9.5 316.5 %all-gather.12.cloned.1.call-start = ((), (), s32[]{:S(2)}) async-start(), calls=%async_computation.4 | async-start | bytes 16920576 | tf_op jit(solution)/shard_map/all_gather | solution.py:184
  10.1 421.3 %all-gather.14.cloned.1.call-start = ((), (), s32[]{:S(2)}) async-start(), calls=%async_computation.5 | async-start | bytes 16920576 | tf_op jit(solution)/shard_map/all_gather | solution.py:194
  10.7 1123.1 %reduce-scatter.5.cloned.1.call-start = ((), (), s32[]{:S(2)}) async-start(), calls=%async_computation.7 | async-start | bytes 57341952
  110.4 27.4 %copy-start.22 = (bf16[1152,256]{1,0:T(8,128)(2,1)}, bf16[1152,256]{1,0:T(8,128)(2,1)S(1)}, u32[]{:S(2)}) copy-start(bf16[1152,256]{1,0:T(8,128)(2,1)S(1)} %all_gather.47) | copy-start | bytes 1769476
  111.0 27.4 %copy-start.19 = (f32[256,256]{0,1:T(8,128)}, f32[256,256]{0,1:T(8,128)S(1)}, u32[]{:S(2)}) copy-start(f32[256,256]{0,1:T(8,128)S(1)} %get-tuple-element.79) | copy-start | bytes 786436
  138.8 10.2 collective-permute-start.1
  142.2 11.7 collective-permute-start
  157.4 4.3 copy-start.4
  165.5 3.9 copy-start.9
  443.8 3.3 copy-start.17
  443.8 3.3 copy-start.30
  491.1 3.0 copy-start.2
  508.1 12.4 copy-start.13
  525.7 36.7 %collective-permute-start.3 = (bf16[256,512]{0,1:T(8,128)(2,1)}, bf16[256,512]{0,1:T(8,128)(2,1)}, u32[]{:S(2)}, u32[]{:S(2)}) collective-permute-start(bf16[256,512]{0,1:T(8,128)(2,1)} %get-tuple-element.59), channel_id=1, source_target_pairs={{2,0},{3,1},{4,2},{5,3},{6,4},{7,5},{10,8},{11,9},{12,10},{13,11},... | collective-permute-start | bytes 786440 | tf_op jit(solution)/shard_map/ppermute | solution.py:18
  527.0 13.6 %copy-start.18 = (bf16[256,1152]{1,0:T(8,128)(2,1)S(1)}, bf16[256,1152]{1,0:T(8,128)(2,1)}, u32[]{:S(2)}) copy-start(bf16[256,1152]{1,0:T(8,128)(2,1)} %param.17) | copy-start | bytes 1769476
  527.0 35.4 %collective-permute-start.2 = (bf16[256,512]{0,1:T(8,128)(2,1)}, bf16[256,512]{0,1:T(8,128)(2,1)}, u32[]{:S(2)}, u32[]{:S(2)}) collective-permute-start(bf16[256,512]{0,1:T(8,128)(2,1)} %get-tuple-element.58), channel_id=1, source_target_pairs={{1,0},{2,1},{3,2},{4,3},{5,4},{6,5},{7,6},{9,8},{10,9},{11,10},{12... | collective-permute-start | bytes 786440 | tf_op jit(solution)/shard_map/ppermute | solution.py:18
  557.2 2.8 copy-start.10
  557.3 2.8 copy-start.29
  572.6 653.8 %all-reduce.13.cloned.1.call-start = ((), (), s32[]{:S(2)}) async-start(), calls=%async_computation.6 | async-start | bytes 6746112 | tf_op jit(solution)/shard_map/psum | solution.py:347
  1226.4 4.0 copy-start
  (25 other events, 36.9 us)
Sparse Core Ops, SparseCore 0:
  10.5 51.0 all-gather.5
  64.0 47.4 all-gather.7
  113.9 106.7 all-gather.9
  222.9 103.0 all-gather.11
  328.3 103.0 all-gather.13
  572.7 560.9 reduce-scatter.4
  1136.5 89.9 all-reduce.12
where the time goes:
time: 1250 us; the launch traced here: 1240 us
  waiting for transfers between devices  892 us (71%)
  matrix products  149 us (12%)
  blocking collectives  122 us (10%)
  local copies, waits for them, and re-layouts  27.5 us (2%)
  other arithmetic  23 us (2%)
  between operations  17.3 us (1%)
    unnamed x8, waiting for transfers between devices  564 us
    all_gather x1, waiting for transfers between devices, local(): lax.all_gather(down_weight, 'dp', axis=0, tiled=True)  92.2 us
    all_gather x1, waiting for transfers between devices, local(): lax.all_gather(up_weight, 'dp', axis=0, tiled=True)  92 us
    psum x1, waiting for transfers between devices, local(): lax.psum(grad_part.astype(jnp.bfloat16), 'seq').astype(jnp.float32)  90.2 us
    unnamed x1, blocking collectives  71.1 us
    all_gather x1, waiting for transfers between devices, local(): lax.all_gather(gate_weight, 'dp', axis=0, tiled=True)  48.8 us
    all_gather x1, blocking collectives, local(): lax.all_gather(value_weight, 'dp', axis=0, tiled=True)  26.2 us
  transfers between devices with their start and end apart: 11, of which 6 were waited for; matrix products, arithmetic and copies ran while one was open for 7% of the time, Pallas kernels for 0%

commit v1 on v0

v1 whole, which is shorter than its diff:
```python
import math

import jax
import jax.numpy as jnp
from jax import lax
from jax.sharding import Mesh
from jax.sharding import PartitionSpec as P

WINDOW = 512


EPSILON = 1e-06
GELU_COEFF = 0.044715


AXES = ("z", "xh", "core", "xl", "y")
SIZES = (4, 2, 2, 2, 4)
DP = ("z", "xh", "core")
SEQ = ("xl", "y")
FEED_SLICE = 1792


def from_behind(array, by):
    pairs = [(i, i + by) for i in range(8) if 0 <= i + by < 8]
    return lax.ppermute(array, SEQ, pairs)


def take(array, axis, by):
    count = lax.axis_size(axis)
    return lax.ppermute(array, axis, [((i + by) % count, i) for i in range(count)])


def give(array, axis, by):
    count = lax.axis_size(axis)
    return lax.ppermute(array, axis, [(i, (i + by) % count) for i in range(count)])


def swap_x(array):
    return lax.ppermute(array, ("xh", "xl"), [(0, 3), (3, 0), (1, 2), (2, 1)])


def gather_rows(block):
    rows, width = block.shape
    z = lax.axis_index("z")
    xh = lax.axis_index("xh")
    core = lax.axis_index("core")
    beside = swap_x(block)
    pair = jnp.where(xh == 0, jnp.stack([block, beside]), jnp.stack([beside, block]))
    own = jnp.zeros((4, 2, rows, width), block.dtype)
    own = lax.dynamic_update_slice_in_dim(own, pair[None], z, 0)
    for by in (1, 3, 2):
        own = lax.dynamic_update_slice_in_dim(own, take(pair, "z", by)[None], (z + by) % 4, 0)
    other = give(own, "core", 1)
    both = jnp.where(
        core == 0, jnp.stack([own, other], axis=2), jnp.stack([other, own], axis=2)
    )
    return both.reshape(16 * rows, width)


def gather_ring(block):
    return [block, take(block, "y", 1), take(block, "y", 2), take(block, "y", 3)]


def sum_ring(blocks):
    total = blocks[0].astype(jnp.float32)
    for by in (1, 3, 2):
        total = total + give(blocks[by].astype(jnp.bfloat16), "y", by).astype(jnp.float32)
    return total


def pick(array, index, axis):
    return lax.dynamic_index_in_dim(array, index, axis, keepdims=False)


def reduce_rows(part):
    z = lax.axis_index("z")
    xh = lax.axis_index("xh")
    core = lax.axis_index("core")
    width = part.shape[1]
    rows = part.shape[0] // 16
    by_core = part.reshape(8, 2, rows, width)
    got = give(pick(by_core, 1 - core, 1), "core", 1)
    chip = (pick(by_core, core, 1).astype(jnp.float32) + got.astype(jnp.float32)).astype(
        jnp.bfloat16
    )
    by_z = chip.reshape(4, 2, rows, width)
    total = pick(by_z, z, 0).astype(jnp.float32)
    for by in (1, 3, 2):
        total = total + give(pick(by_z, (z + by) % 4, 0), "z", by).astype(jnp.float32)
    column = total.astype(jnp.bfloat16)
    got = swap_x(pick(column, 1 - xh, 0))
    half = (pick(column, xh, 0).astype(jnp.float32) + got.astype(jnp.float32)).astype(jnp.bfloat16)
    got = give(half, "xl", 1)
    return (half.astype(jnp.float32) + got.astype(jnp.float32)).astype(jnp.bfloat16)


def in_order(blocks):
    y = lax.axis_index("y")
    ordered = []
    for place in range(4):
        value = blocks[(place - 3) % 4]
        for at in range(3):
            value = jnp.where(y == at, blocks[(place - at) % 4], value)
        ordered.append(value.astype(jnp.float32))
    return ordered


def inverse_rms(values):
    return lax.rsqrt(jnp.mean(values * values, axis=-1, keepdims=True) + EPSILON)


def rms_backward(values, scaling, upstream):
    inner = jnp.mean(upstream * values, axis=-1, keepdims=True)
    return scaling * (upstream - values * (scaling * scaling) * inner)


def rotary_tables(positions, head_size):
    half_size = head_size // 2
    exponents = lax.iota(jnp.float32, half_size) * (2.0 / head_size)
    frequency = jnp.power(10000.0, -exponents)
    angles = positions.astype(jnp.float32)[:, None] * frequency[None, :]
    return (jnp.cos(angles), jnp.sin(angles))


def rotate(values, cosine_table, sine_table):
    half_size = values.shape[-1] // 2
    first_half = values[..., :half_size]
    second_half = values[..., half_size:]
    return jnp.concatenate(
        [
            first_half * cosine_table - second_half * sine_table,
            second_half * cosine_table + first_half * sine_table,
        ],
        axis=-1,
    )


def rotate_back(upstream, cosine_table, sine_table):
    half_size = upstream.shape[-1] // 2
    first_half = upstream[..., :half_size]
    second_half = upstream[..., half_size:]
    return jnp.concatenate(
        [
            first_half * cosine_table + second_half * sine_table,
            second_half * cosine_table - first_half * sine_table,
        ],
        axis=-1,
    )


def gelu_parts(values):
    root_coeff = math.sqrt(2.0 / math.pi)
    bend = jnp.tanh(root_coeff * (values + GELU_COEFF * values * values * values))
    gelu_value = 0.5 * values * (1.0 + bend)
    gelu_slope = 0.5 * (1.0 + bend) + 0.5 * values * (1.0 - bend * bend) * root_coeff * (
        1.0 + 3.0 * GELU_COEFF * values * values
    )
    return (gelu_value, gelu_slope)


def feed_slice(weight):
    y = lax.axis_index("y")
    padded = jnp.pad(weight, ((0, 0), (0, 4 * FEED_SLICE - weight.shape[1])))
    return lax.dynamic_slice_in_dim(padded, y * FEED_SLICE, FEED_SLICE, 1)


def local(
    tokens,
    cotangent,
    lengths,
    query_weight,
    key_weight,
    value_weight,
    out_weight,
    gate_weight,
    up_weight,
    down_weight,
    input_gain,
    query_gain,
    key_gain,
    attention_gain,
    feedforward_gain,
    output_gain,
):
    low = jnp.bfloat16
    row_count, model_width = tokens.shape
    head_size = key_weight.shape[1]
    head_count = query_weight.shape[1] // head_size
    query_width = head_count * head_size
    feed_width = gate_weight.shape[1]
    gain_shard = input_gain.shape[0]
    head_shard = query_gain.shape[0]
    scaling_factor = head_size ** (-0.5)
    y = lax.axis_index("y")
    seq_index = lax.axis_index("xl") * 4 + y
    positions = seq_index * row_count + lax.iota(jnp.int32, row_count)
    valid_rows = (positions < lengths[0]).astype(jnp.float32)[:, None]
    cosine_table, sine_table = rotary_tables(positions, head_size)
    hop_total = 2

    def spread(vector):
        return jnp.pad(vector, (0, gain_shard - head_shard))

    gain_columns = jnp.stack(
        [
            input_gain,
            attention_gain,
            feedforward_gain,
            output_gain,
            spread(query_gain),
            spread(key_gain),
        ],
        axis=1,
    )
    gain_columns = jnp.pad(gain_columns, ((0, 0), (0, 122)))
    first = gather_rows(
        jnp.concatenate([query_weight, key_weight, value_weight, gain_columns], axis=1)
    )
    full_qkv = first[:, : query_width + 2 * head_size]
    gains = 1.0 + first[:, query_width + 2 * head_size :].astype(jnp.float32)
    full_out = gather_rows(out_weight)
    gate_up = lax.all_gather(
        jnp.concatenate([feed_slice(gate_weight), feed_slice(up_weight)], axis=1),
        DP,
        axis=0,
        tiled=True,
    )
    down = lax.all_gather(feed_slice(down_weight), DP, axis=0, tiled=True)
    gain_rows = gains.T
    one_input = gain_rows[0]
    one_attention = gain_rows[1]
    one_feed = gain_rows[2]
    one_output = gain_rows[3]
    one_query = gain_rows[4].reshape(16, gain_shard)[:, :head_shard].reshape(head_size)
    one_key = gain_rows[5].reshape(16, gain_shard)[:, :head_shard].reshape(head_size)

    residual = tokens.astype(jnp.float32)
    input_scale = inverse_rms(residual)
    normed_input = residual * input_scale
    attention_input = (normed_input * one_input).astype(low)
    input_ring = jnp.concatenate(gather_ring(attention_input), axis=0)
    qkv_raw = jnp.dot(attention_input, full_qkv, preferred_element_type=jnp.float32)
    query_raw = qkv_raw[:, :query_width]
    key_raw = qkv_raw[:, query_width : query_width + head_size]
    value_raw = qkv_raw[:, query_width + head_size :]
    query_heads = query_raw.reshape(row_count, head_count, head_size)
    query_scale = inverse_rms(query_heads)
    query_hat = query_heads * query_scale
    query_low = rotate(
        query_hat * one_query, cosine_table[:, None, :], sine_table[:, None, :]
    ).astype(low)
    key_scale = inverse_rms(key_raw)
    key_hat = key_raw * key_scale
    key_low = rotate(key_hat * one_key, cosine_table, sine_table).astype(low)
    value_low = value_raw.astype(low)
    local_pair = jnp.concatenate([key_low, value_low], axis=1)
    rim_blocks = [from_behind(local_pair, distance) for distance in (1, 2)]
    key_rows = jnp.concatenate(rim_blocks[::-1] + [local_pair], axis=0)
    key_count = key_rows.shape[0]
    key_positions = (seq_index - hop_total) * row_count + lax.iota(jnp.int32, key_count)
    offsets = positions[:, None] - key_positions[None, :]
    allowed = (offsets >= 0) & (offsets < WINDOW) & (key_positions[None, :] >= 0)
    keys_only = key_rows[:, :head_size]
    values_only = key_rows[:, head_size:]

    def masked_scores():
        raw_scores = (
            jnp.einsum("thd,kd->htk", query_low, keys_only, preferred_element_type=jnp.float32)
            * scaling_factor
        )
        return jnp.where(allowed[None], raw_scores, -1e30)

    masked = masked_scores()
    row_top = jnp.max(masked, axis=-1, keepdims=True)
    exponent_terms = jnp.exp(masked - row_top)
    row_total = jnp.sum(exponent_terms, axis=-1, keepdims=True)
    log_total = row_top + jnp.log(row_total)
    probs_low = (exponent_terms / row_total).astype(low)
    context = jnp.einsum("htk,kd->thd", probs_low, values_only, preferred_element_type=jnp.float32)
    context_low = context.reshape(row_count, query_width).astype(low)
    attention_raw = jnp.einsum(
        "tq,dq->td", context_low, full_out, preferred_element_type=jnp.float32
    )
    attention_scale = inverse_rms(attention_raw)
    attention_hat = attention_raw * attention_scale
    hidden_state = residual + attention_hat * one_attention
    state_scale = inverse_rms(hidden_state)
    state_hat = hidden_state * state_scale
    feed_input = (state_hat * one_feed).astype(low)

    feed_ring = jnp.concatenate(gather_ring(feed_input), axis=0)
    gate_up_raw = jnp.dot(feed_ring, gate_up, preferred_element_type=jnp.float32)
    gate_raw = gate_up_raw[:, :FEED_SLICE]
    up_raw = gate_up_raw[:, FEED_SLICE:]
    gelu_value, gelu_slope = gelu_parts(gate_raw)
    hidden_low = (gelu_value * up_raw).astype(low)
    down_part = jnp.einsum("tf,df->td", hidden_low, down, preferred_element_type=jnp.float32)
    down_raw = sum_ring(jnp.split(down_part, 4, axis=0))
    down_scale = inverse_rms(down_raw)
    down_hat = down_raw * down_scale
    layer_value = hidden_state + down_hat * one_output
    layer_output = (valid_rows * layer_value).astype(low)
    upstream = cotangent.astype(jnp.float32) * valid_rows
    output_gain_vec = jnp.sum(upstream * down_hat, axis=0)
    down_grad_low = rms_backward(down_raw, down_scale, upstream * one_output).astype(low)

    down_ring = jnp.concatenate(gather_ring(down_grad_low), axis=0)
    hidden_grad = jnp.dot(down_ring, down, preferred_element_type=jnp.float32)
    down_weight_part = jnp.einsum(
        "tc,tf->cf", down_ring, hidden_low, preferred_element_type=jnp.float32
    ).astype(low)
    gate_grad_low = (hidden_grad * up_raw * gelu_slope).astype(low)
    up_grad_low = (hidden_grad * gelu_value).astype(low)
    gate_up_grad = jnp.concatenate([gate_grad_low, up_grad_low], axis=1)
    feed_part = jnp.einsum("tf,df->td", gate_up_grad, gate_up, preferred_element_type=jnp.float32)
    gate_up_part = jnp.einsum(
        "tc,tf->cf", feed_ring, gate_up_grad, preferred_element_type=jnp.float32
    ).astype(low)
    block_part = sum_ring(jnp.split(feed_part, 4, axis=0))
    down_weight_sum = reduce_rows(down_weight_part)
    gate_up_sum = reduce_rows(gate_up_part)

    feed_gain_vec = jnp.sum(block_part * state_hat, axis=0)
    state_grad = upstream + rms_backward(hidden_state, state_scale, block_part * one_feed)
    attention_gain_vec = jnp.sum(state_grad * attention_hat, axis=0)
    attention_grad_low = rms_backward(
        attention_raw, attention_scale, state_grad * one_attention
    ).astype(low)
    attention_ring = jnp.concatenate(gather_ring(attention_grad_low), axis=0)
    context_cut = context_low.reshape(row_count, 4, query_width // 4)
    context_ring = jnp.concatenate(
        [pick(context_cut, y, 1)]
        + [give(pick(context_cut, (y + by) % 4, 1), "y", by) for by in (3, 2, 1)],
        axis=0,
    )
    context_grad = jnp.einsum(
        "td,dq->tq", attention_grad_low, full_out, preferred_element_type=jnp.float32
    )
    context_grad_low = context_grad.reshape(row_count, head_count, head_size).astype(low)
    probs_again = jnp.exp(masked_scores() - log_total)
    probs_again_low = probs_again.astype(low)
    prob_grad = jnp.einsum(
        "thd,kd->htk", context_grad_low, values_only, preferred_element_type=jnp.float32
    )
    score_grad = probs_again * (
        prob_grad - jnp.sum(probs_again * prob_grad, axis=-1, keepdims=True)
    )
    score_grad_low = score_grad.astype(low)
    key_rot_rows = (
        jnp.einsum("htk,thd->kd", score_grad_low, query_low, preferred_element_type=jnp.float32)
        * scaling_factor
    )
    value_rows = jnp.einsum(
        "htk,thd->kd", probs_again_low, context_grad_low, preferred_element_type=jnp.float32
    )
    pair_grad = jnp.concatenate([key_rot_rows, value_rows], axis=1)
    local_grad = pair_grad[hop_total * row_count :]
    for distance in range(1, hop_total + 1):
        begin_row = (hop_total - distance) * row_count
        local_grad = local_grad + from_behind(
            pair_grad[begin_row : begin_row + row_count].astype(low), -distance
        ).astype(jnp.float32)
    query_rot_grad = (
        jnp.einsum("htk,kd->thd", score_grad_low, keys_only, preferred_element_type=jnp.float32)
        * scaling_factor
    )
    key_norm_grad = rotate_back(local_grad[:, :head_size], cosine_table, sine_table)
    key_gain_vec = jnp.sum(key_norm_grad * key_hat, axis=0)
    key_raw_low = rms_backward(key_raw, key_scale, key_norm_grad * one_key).astype(low)
    value_raw_low = local_grad[:, head_size:].astype(low)
    query_norm_grad = rotate_back(query_rot_grad, cosine_table[:, None, :], sine_table[:, None, :])
    query_gain_vec = jnp.sum(query_norm_grad * query_hat, axis=(0, 1))
    query_raw_low = (
        rms_backward(query_heads, query_scale, query_norm_grad * one_query)
        .reshape(row_count, query_width)
        .astype(low)
    )
    qkv_grad = jnp.concatenate([query_raw_low, key_raw_low, value_raw_low], axis=1)
    qkv_cut = qkv_grad.reshape(row_count, 4, qkv_grad.shape[1] // 4)
    qkv_ring = jnp.concatenate(
        [pick(qkv_cut, y, 1)]
        + [give(pick(qkv_cut, (y + by) % 4, 1), "y", by) for by in (3, 2, 1)],
        axis=0,
    )
    input_grad = jnp.einsum("tq,dq->td", qkv_grad, full_qkv, preferred_element_type=jnp.float32)
    input_gain_vec = jnp.sum(input_grad * normed_input, axis=0)
    tokens_grad = (state_grad + rms_backward(residual, input_scale, input_grad * one_input)).astype(
        low
    )

    def spread_head(vector):
        return jnp.pad(
            vector.reshape(16, head_shard), ((0, 0), (0, gain_shard - head_shard))
        ).reshape(model_width)

    gain_block = jnp.stack(
        [
            input_gain_vec,
            attention_gain_vec,
            feed_gain_vec,
            output_gain_vec,
            spread_head(query_gain_vec),
            spread_head(key_gain_vec),
        ],
        axis=1,
    )
    gain_block = jnp.pad(gain_block, ((0, 0), (0, 122)))
    qkv_part = jnp.einsum("tc,tq->cq", input_ring, qkv_ring, preferred_element_type=jnp.float32)
    out_part = jnp.einsum(
        "tc,tq->cq", attention_ring, context_ring, preferred_element_type=jnp.float32
    )
    attention_sum = reduce_rows(
        jnp.concatenate([qkv_part, out_part, gain_block], axis=1).astype(low)
    )
    down_blocks = in_order(gather_ring(down_weight_sum))
    gate_up_blocks = in_order(gather_ring(gate_up_sum))
    attention_blocks = in_order(gather_ring(attention_sum))
    down_weight_grad = jnp.concatenate(down_blocks, axis=1)[:, :feed_width]
    gate_weight_grad = jnp.concatenate([b[:, :FEED_SLICE] for b in gate_up_blocks], axis=1)
    up_weight_grad = jnp.concatenate([b[:, FEED_SLICE:] for b in gate_up_blocks], axis=1)
    qkv_cols = qkv_grad.shape[1] // 4
    out_cols = query_width // 4
    qkv_weight_grad = jnp.concatenate([b[:, :qkv_cols] for b in attention_blocks], axis=1)
    out_weight_grad = jnp.concatenate(
        [b[:, qkv_cols : qkv_cols + out_cols] for b in attention_blocks], axis=1
    )
    gain_sum = sum(b[:, qkv_cols + out_cols :] for b in attention_blocks)
    return (
        layer_output,
        tokens_grad,
        qkv_weight_grad[:, :query_width],
        qkv_weight_grad[:, query_width : query_width + head_size],
        qkv_weight_grad[:, query_width + head_size :],
        out_weight_grad,
        gate_weight_grad[:, :feed_width],
        up_weight_grad[:, :feed_width],
        down_weight_grad,
        gain_sum[:, 0],
        gain_sum[:head_shard, 4],
        gain_sum[:head_shard, 5],
        gain_sum[:, 1],
        gain_sum[:, 2],
        gain_sum[:, 3],
    )


def solution(mesh):
    fine = Mesh(mesh.devices.reshape(SIZES), AXES)
    rows = P(AXES, None)
    matrix = P(DP, None)
    vector = P(DP)
    return jax.shard_map(
        local,
        mesh=fine,
        in_specs=(rows, rows, vector) + (matrix,) * 7 + (vector,) * 6,
        out_specs=(rows, rows) + (matrix,) * 7 + (vector,) * 6,
        check_vma=False,
    )
```

time: 1250 us -> 592 us (0.47)
  waiting for transfers between devices: 892 us -> 264 us
  blocking collectives: 122 us -> 0 us
  starting transfers between devices: 11.3 us -> 108 us
  matrix products: 149 us -> 92.1 us
  other arithmetic: 23 us -> 52.2 us
  local copies, waits for them, and re-layouts: 27.5 us -> 53.7 us
    unnamed x8 -> x2, waiting for transfers between devices: 564 us -> 0.03 us
    ppermute x4 -> x65, waiting for transfers between devices: 4.93 us -> 264 us  [the longest x29 138 us: give(): lax.ppermute(array, axis, [(i, (i + by) % count) for i in range(count)])]
    all_gather x5 -> x2, waiting for transfers between devices: 233 us -> 0.01 us  [the longest x1 0.01 us: local(): lax.all_gather(jnp.concatenate([feed_slice(gate_weight), feed_slice(up_we...]
    ppermute x4 -> x65, starting transfers between devices: 11 us -> 108 us  [the longest x27 43.8 us: take(): lax.ppermute(array, axis, [((i + by) % count, i) for i in range(count)])]
    psum x1 -> x0, waiting for transfers between devices: 90.2 us -> none  [local(): lax.psum(grad_part.astype(jnp.bfloat16), 'seq').astype(jnp.float32)]
    unnamed x1 -> x0, blocking collectives: 71.1 us -> none
    all_gather x2 -> x0, blocking collectives: 50.7 us -> none  [the longest x1 26.2 us: local(): lax.all_gather(value_weight, 'dp', axis=0, tiled=True)]
    dot_general x20 -> x11, matrix products: 137 us -> 87.2 us  [the longest x1 16.4 us: local(): hidden_grad = jnp.dot(down_ring, down, preferred_element_type=jnp.float32)]
  transfers between devices with their start and end apart: 11 -> 67, of which waited for: 6 -> 36; matrix products, arithmetic and copies ran while one was open for 7% -> 28% of each run, Pallas kernels for 0% -> 0%
where the time goes in v1:
time: 592 us; the launch traced here: 587 us
  waiting for transfers between devices  264 us (45%)
  starting transfers between devices  108 us (18%)
  matrix products  92.1 us (16%)
  local copies, waits for them, and re-layouts  53.7 us (9%)
  other arithmetic  52.2 us (9%)
  between operations  16.6 us (3%)
    ppermute x29, waiting for transfers between devices, give(): lax.ppermute(array, axis, [(i, (i + by) % count) for i in range(count)])  138 us
    ppermute x27, waiting for transfers between devices, take(): lax.ppermute(array, axis, [((i + by) % count, i) for i in range(count)])  104 us
    ppermute x27, starting transfers between devices, take(): lax.ppermute(array, axis, [((i + by) % count, i) for i in range(count)])  43.8 us
    ppermute x29, starting transfers between devices, give(): lax.ppermute(array, axis, [(i, (i + by) % count) for i in range(count)])  32.2 us
    ppermute x4, starting transfers between devices, from_behind(): return lax.ppermute(array, SEQ, pairs)  23.6 us
    unnamed x192, local copies, waits for them, and re-layouts  21.3 us
    dot_general x1, matrix products, local(): hidden_grad = jnp.dot(down_ring, down, preferred_element_type=jnp.float32)  16.4 us
    ppermute x5, waiting for transfers between devices, swap_x(): return lax.ppermute(array, ('xh', 'xl'), [(0, 3), (3, 0), (1, 2), (2, 1)])  16.2 us
  transfers between devices with their start and end apart: 67, of which 36 were waited for; matrix products, arithmetic and copies ran while one was open for 28% of the time, Pallas kernels for 0%

profile of v1, /device:TPU:0, one launch (start us, length us, event | category | flops | bytes accessed | tf_op | source)
XLA Modules:
  0.0 586.9 jit_solution(2126036900187103818)
XLA Ops:
  13.1 8.5 %collective-permute-done.7 = bf16[72,1024]{1,0:T(8,128)(2,1)S(1)} collective-permute-done((bf16[72,1024]{1,0:T(8,128)(2,1)S(1)}, bf16[72,1024]{1,0:T(8,128)(2,1)S(1)}, u32[]{:S(2)}, u32[]{:S(2)}) %collective-permute-start.7) | collective-permute-done | bytes 147488 | tf_op jit(solution)/shard_map/ppermute | solution.py:39
  21.7 4.3 collective-permute-start.8
  32.5 11.7 %collective-permute-done.8 = bf16[2,72,1024]{2,1,0:T(8,128)(2,1)S(1)} collective-permute-done((bf16[2,72,1024]{2,1,0:T(8,128)(2,1)S(1)}, bf16[2,72,1024]{2,1,0:T(8,128)(2,1)S(1)}, u32[]{:S(2)}, u32[]{:S(2)}) %collective-permute-start.8) | collective-permute-done | bytes 294944 | tf_op jit(solution)/shard_map/ppermute | solution.py:30
  44.9 21.7 %collective-permute-done.1 = bf16[2,72,1664]{2,1,0:T(8,128)(2,1)S(1)} collective-permute-done((bf16[2,72,1664]{2,1,0:T(8,128)(2,1)S(1)}, bf16[2,72,1664]{2,1,0:T(8,128)(2,1)S(1)}, u32[]{:S(2)}, u32[]{:S(2)}) %collective-permute-start.1) | collective-permute-done | bytes 479264 | tf_op jit(solution)/shard_map/ppermute | solution.py:30
  66.9 10.1 %collective-permute-done.3 = bf16[2,72,1664]{2,1,0:T(8,128)(2,1)S(1)} collective-permute-done((bf16[2,72,1664]{2,1,0:T(8,128)(2,1)S(1)}, bf16[2,72,1664]{2,1,0:T(8,128)(2,1)S(1)}, u32[]{:S(2)}, u32[]{:S(2)}) %collective-permute-start.3) | collective-permute-done | bytes 479264 | tf_op jit(solution)/shard_map/ppermute | solution.py:30
  83.3 4.5 maximum_select_fusion.1
  99.1 4.2 collective-permute-start.6
  103.3 16.8 %collective-permute-start.5 = (bf16[256,512]{1,0:T(8,128)(2,1)S(1)}, bf16[256,512]{1,0:T(8,128)(2,1)}, u32[]{:S(2)}, u32[]{:S(2)}) collective-permute-start(bf16[256,512]{1,0:T(8,128)(2,1)S(1)} %pad_maximum_fusion.29), channel_id=1, source_target_pairs={{0,2},{1,3},{2,4},{3,5},{4,6},{5,7},{8,10},{9,11},{10,12},{11,13},... | collective-permute-start | bytes 786440 | tf_op jit(solution)/shard_map/ppermute | solution.py:25
  135.2 25.4 %collective-permute-done.14 = bf16[256,1152]{1,0:T(8,128)(2,1)S(1)} collective-permute-done((bf16[256,1152]{1,0:T(8,128)(2,1)S(1)}, bf16[256,1152]{1,0:T(8,128)(2,1)S(1)}, u32[]{:S(2)}, u32[]{:S(2)}) %collective-permute-start.14) | collective-permute-done | bytes 589856 | tf_op jit(solution)/shard_map/ppermute | solution.py:30
  162.2 12.7 %fusion.99 = f32[1024,3584]{1,0:T(8,128)S(1)} fusion(bf16[1152,3584]{1,0:T(8,128)(2,1)} %all-gather.3.cloned.1.call-done, bf16[256,1152]{1,0:T(8,128)(2,1)} %copy-done.85, bf16[256,1152]{1,0:T(8,128)(2,1)} %copy-done.86, bf16[256,1152]{1,0:T(8,128)(2,1)} %collective-permute-done.12, bf16[256,1152]{1,0:T(8,128)(2,1)} %copy-done.37), kind=kOutput, calls=%fused_computation.210 | convolution fusion | flops 8465154048 | bytes 25296896 | tf_op jit(solution)/shard_map/dot_general | solution.py:292
  175.0 5.1 copy-done.8
  183.8 8.2 %fusion.145 = (bf16[1024,1152]{1,0:T(8,128)(2,1)S(1)}, f32[1024,1152]{1,0:T(8,128)S(1)}) fusion(bf16[1024,1792]{1,0:T(8,128)(2,1)} %multiply_convert_fusion.1, bf16[1152,1792]{1,0:T(8,128)(2,1)} %all-gather.5.cloned.1.call-done), kind=kOutput, calls=%fused_computation.333 | convolution fusion | flops 4229038080 | bytes 14876672 | tf_op jit(solution)/shard_map/tf,df->td/dot_general | solution.py:297
  195.2 14.9 %collective-permute-done.17 = bf16[256,1152]{1,0:T(8,128)(2,1)S(1)} collective-permute-done((bf16[256,1152]{1,0:T(8,128)(2,1)S(1)}, bf16[256,1152]{1,0:T(8,128)(2,1)S(1)}, u32[]{:S(2)}, u32[]{:S(2)}) %collective-permute-start.17) | collective-permute-done | bytes 589856 | tf_op jit(solution)/shard_map/ppermute | solution.py:35
  210.1 10.0 %collective-permute-done.16 = bf16[256,1152]{1,0:T(8,128)(2,1)S(1)} collective-permute-done((bf16[256,1152]{1,0:T(8,128)(2,1)S(1)}, bf16[256,1152]{1,0:T(8,128)(2,1)S(1)}, u32[]{:S(2)}, u32[]{:S(2)}) %collective-permute-start.16) | collective-permute-done | bytes 589856 | tf_op jit(solution)/shard_map/ppermute | solution.py:35
  227.1 4.4 copy.208
  239.6 12.9 %collective-permute-done.20 = bf16[256,1152]{1,0:T(8,128)(2,1)} collective-permute-done((bf16[256,1152]{1,0:T(8,128)(2,1)}, bf16[256,1152]{1,0:T(8,128)(2,1)}, u32[]{:S(2)}, u32[]{:S(2)}) %collective-permute-start.20) | collective-permute-done | bytes 589856 | tf_op jit(solution)/shard_map/ppermute | solution.py:30
  254.3 16.4 %fusion.7 = (bf16[1024,1792]{1,0:T(8,128)(2,1)}, bf16[1024,1792]{1,0:T(8,128)(2,1)}) fusion(f32[1024,3584]{1,0:T(8,128)} %copy-done.8, bf16[1152,1792]{1,0:T(8,128)(2,1)} %all-gather.5.cloned.1.call-done, bf16[256,1152]{1,0:T(8,128)(2,1)} %collective-permute-done.20, bf16[256,1152]{1,0:T(8,128)(2,1)} %collective-permute-done.19, ...), kind=kOutput, calls=%fused_computation.12 | convolution fusion | flops 4279500800 | bytes 28508160 | tf_op jit(solution)/shard_map/dot_general | solution.py:308
  270.7 15.9 %fusion.146 = (bf16[1024,1152]{1,0:T(8,128)(2,1)S(1)}, f32[1024,1152]{1,0:T(8,128)}) fusion(bf16[1152,3584]{1,0:T(8,128)(2,1)} %all-gather.3.cloned.1.call-done, bf16[1024,1792]{1,0:T(8,128)(2,1)} %get-tuple-element.44, bf16[1024,1792]{1,0:T(8,128)(2,1)} %get-tuple-element.43), kind=kOutput, calls=%fused_computation.334 | convolution fusion | flops 8471576576 | bytes 22675456 | tf_op jit(solution)/shard_map/tf,df->td/dot_general | solution.py:315
  290.4 8.4 %convolution_convert_fusion.1 = bf16[1152,1792]{1,0:T(8,128)(2,1)} fusion(bf16[1024,1792]{1,0:T(8,128)(2,1)S(1)} %copy-done.25, bf16[256,1152]{1,0:T(8,128)(2,1)} %collective-permute-done.20, bf16[256,1152]{1,0:T(8,128)(2,1)} %collective-permute-done.19, bf16[256,1152]{1,0:T(8,128)(2,1)} %collective-permute-done.18, bf16[256,1152]{1,0:T(8,128)(2,1)} %get-tuple-element.67), kind=kOutput, calls=%fused_computation.5 | convolution fusion | flops 4239360000 | bytes 10158080 | tf_op jit(solution)/shard_map/tc,tf->cf/dot_general | solution.py:309
  298.8 5.8 collective-permute-done.23
  307.3 9.8 %collective-permute-done.22 = bf16[256,1152]{1,0:T(8,128)(2,1)S(1)} collective-permute-done((bf16[256,1152]{1,0:T(8,128)(2,1)S(1)}, bf16[256,1152]{1,0:T(8,128)(2,1)S(1)}, u32[]{:S(2)}, u32[]{:S(2)}) %collective-permute-start.22) | collective-permute-done | bytes 589856 | tf_op jit(solution)/shard_map/ppermute | solution.py:35
  368.5 4.1 fusion.51
  373.2 18.7 %collective-permute-done.30 = bf16[256,384]{1,0:T(8,128)(2,1)} collective-permute-done((bf16[256,384]{1,0:T(8,128)(2,1)}, bf16[256,384]{1,0:T(8,128)(2,1)}, u32[]{:S(2)}, u32[]{:S(2)}) %collective-permute-start.30) | collective-permute-done | bytes 196640 | tf_op jit(solution)/shard_map/ppermute | solution.py:35
  392.4 5.9 %collective-permute-done.29 = bf16[256,384]{1,0:T(8,128)(2,1)} collective-permute-done((bf16[256,384]{1,0:T(8,128)(2,1)S(1)}, bf16[256,384]{1,0:T(8,128)(2,1)}, u32[]{:S(2)}, u32[]{:S(2)}) %collective-permute-start.29) | collective-permute-done | bytes 196640 | tf_op jit(solution)/shard_map/ppermute | solution.py:35
  408.4 11.7 %convolution_convert_fusion = bf16[1152,3584]{1,0:T(8,128)(2,1)S(1)} fusion(bf16[1024,1792]{1,0:T(8,128)(2,1)} %get-tuple-element.44, bf16[1024,1792]{1,0:T(8,128)(2,1)} %get-tuple-element.43, bf16[256,1152]{1,0:T(8,128)(2,1)} %copy-done.85, bf16[256,1152]{1,0:T(8,128)(2,1)} %copy-done.86, bf16[256,1152]{1,0:T(8,128)(2,1)} %collective-permute-done.12, ...), kind=kOutput, calls=%fused_computation | convolution fusion | flops 8483962880 | bytes 17956864 | tf_op jit(solution)/shard_map/tc,tf->cf/dot_general | solution.py:316
  459.7 6.4 %collective-permute-done.58 = bf16[2,72,1792]{2,1,0:T(8,128)(2,1)S(1)} collective-permute-done((bf16[2,72,1792]{2,1,0:T(8,128)(2,1)S(1)}, bf16[2,72,1792]{2,1,0:T(8,128)(2,1)S(1)}, u32[]{:S(2)}, u32[]{:S(2)}) %collective-permute-start.58) | collective-permute-done | bytes 516128 | tf_op jit(solution)/shard_map/ppermute | solution.py:35
  485.0 18.7 %collective-permute-done.50 = bf16[2,72,3584]{2,1,0:T(8,128)(2,1)S(1)} collective-permute-done((bf16[2,72,3584]{2,1,0:T(8,128)(2,1)S(1)}, bf16[2,72,3584]{2,1,0:T(8,128)(2,1)S(1)}, u32[]{:S(2)}, u32[]{:S(2)}) %collective-permute-start.50) | collective-permute-done | bytes 1032224 | tf_op jit(solution)/shard_map/ppermute | solution.py:35
  503.7 20.4 %collective-permute-done.49 = bf16[2,72,3584]{2,1,0:T(8,128)(2,1)S(1)} collective-permute-done((bf16[2,72,3584]{2,1,0:T(8,128)(2,1)S(1)}, bf16[2,72,3584]{2,1,0:T(8,128)(2,1)S(1)}, u32[]{:S(2)}, u32[]{:S(2)}) %collective-permute-start.49) | collective-permute-done | bytes 1032224 | tf_op jit(solution)/shard_map/ppermute | solution.py:35
  531.5 7.2 %collective-permute-done.51 = bf16[72,3584]{1,0:T(8,128)(2,1)S(1)} collective-permute-done((bf16[72,3584]{1,0:T(8,128)(2,1)S(1)}, bf16[72,3584]{1,0:T(8,128)(2,1)S(1)}, u32[]{:S(2)}, u32[]{:S(2)}) %collective-permute-start.51) | collective-permute-done | bytes 516128 | tf_op jit(solution)/shard_map/ppermute | solution.py:39
  541.3 9.3 %collective-permute-done.52 = bf16[72,3584]{1,0:T(8,128)(2,1)S(1)} collective-permute-done((bf16[72,3584]{1,0:T(8,128)(2,1)S(1)}, bf16[72,3584]{1,0:T(8,128)(2,1)S(1)}, u32[]{:S(2)}, u32[]{:S(2)}) %collective-permute-start.52) | collective-permute-done | bytes 516128 | tf_op jit(solution)/shard_map/ppermute | solution.py:35
  559.0 8.1 %collective-permute-done.53 = bf16[72,3584]{1,0:T(8,128)(2,1)S(1)} collective-permute-done((bf16[72,3584]{1,0:T(8,128)(2,1)S(1)}, bf16[72,3584]{1,0:T(8,128)(2,1)S(1)}, u32[]{:S(2)}, u32[]{:S(2)}) %collective-permute-start.53) | collective-permute-done | bytes 516128 | tf_op jit(solution)/shard_map/ppermute | solution.py:30
  567.1 8.5 %collective-permute-done.54 = bf16[72,3584]{1,0:T(8,128)(2,1)S(1)} collective-permute-done((bf16[72,3584]{1,0:T(8,128)(2,1)S(1)}, bf16[72,3584]{1,0:T(8,128)(2,1)S(1)}, u32[]{:S(2)}, u32[]{:S(2)}) %collective-permute-start.54) | collective-permute-done | bytes 516128 | tf_op jit(solution)/shard_map/ppermute | solution.py:30
  (472 shorter events, 219.5 us)
Async XLA Ops:
  7.3 155.0 %all-gather.3.cloned.1.call-start = ((), (), s32[]{:S(2)}) async-start(), calls=%async_computation | async-start | bytes 8773632 | tf_op jit(solution)/shard_map/all_gather | solution.py:222
  9.4 174.4 %all-gather.5.cloned.1.call-start = ((), (), s32[]{:S(2)}) async-start(), calls=%async_computation.1 | async-start | bytes 4386816 | tf_op jit(solution)/shard_map/all_gather | solution.py:228
  26.0 51.2 %collective-permute-start.9 = (bf16[2,72,1024]{2,1,0:T(8,128)(2,1)S(1)}, bf16[2,72,1024]{2,1,0:T(8,128)(2,1)S(1)}, u32[]{:S(2)}, u32[]{:S(2)}) collective-permute-start(bf16[2,72,1024]{2,1,0:T(8,128)(2,1)S(1)} %maximum_select_fusion.5), channel_id=1, source_target_pairs={{96,0},{0,32},{32,64},{64,96},{97,1},{1,33},{33,65},{65,97},{98,2}... | collective-permute-start | bytes 884744 | tf_op jit(solution)/shard_map/ppermute | solution.py:30
  26.0 51.9 %collective-permute-start.10 = (bf16[2,72,1024]{2,1,0:T(8,128)(2,1)S(1)}, bf16[2,72,1024]{2,1,0:T(8,128)(2,1)S(1)}, u32[]{:S(2)}, u32[]{:S(2)}) collective-permute-start(bf16[2,72,1024]{2,1,0:T(8,128)(2,1)S(1)} %maximum_select_fusion.5), channel_id=1, source_target_pairs={{64,0},{96,32},{0,64},{32,96},{65,1},{97,33},{1,65},{33,97},{66,2}... | collective-permute-start | bytes 884744 | tf_op jit(solution)/shard_map/ppermute | solution.py:30
  28.0 38.7 %collective-permute-start.1 = (bf16[2,72,1664]{2,1,0:T(8,128)(2,1)S(1)}, bf16[2,72,1664]{2,1,0:T(8,128)(2,1)S(1)}, u32[]{:S(2)}, u32[]{:S(2)}) collective-permute-start(bf16[2,72,1664]{2,1,0:T(8,128)(2,1)S(1)} %maximum_select_fusion.3), channel_id=1, source_target_pairs={{32,0},{64,32},{96,64},{0,96},{33,1},{65,33},{97,65},{1,97},{34,2}... | collective-permute-start | bytes 1437704 | tf_op jit(solution)/shard_map/ppermute | solution.py:30
  31.4 35.4 %collective-permute-start.2 = (bf16[2,72,1664]{2,1,0:T(8,128)(2,1)S(1)}, bf16[2,72,1664]{2,1,0:T(8,128)(2,1)S(1)}, u32[]{:S(2)}, u32[]{:S(2)}) collective-permute-start(bf16[2,72,1664]{2,1,0:T(8,128)(2,1)S(1)} %maximum_select_fusion.3), channel_id=1, source_target_pairs={{96,0},{0,32},{32,64},{64,96},{97,1},{1,33},{33,65},{65,97},{98,2}... | collective-permute-start | bytes 1437704 | tf_op jit(solution)/shard_map/ppermute | solution.py:30
  44.2 32.8 %collective-permute-start.3 = (bf16[2,72,1664]{2,1,0:T(8,128)(2,1)S(1)}, bf16[2,72,1664]{2,1,0:T(8,128)(2,1)S(1)}, u32[]{:S(2)}, u32[]{:S(2)}) collective-permute-start(bf16[2,72,1664]{2,1,0:T(8,128)(2,1)S(1)} %maximum_select_fusion.3), channel_id=1, source_target_pairs={{64,0},{96,32},{0,64},{32,96},{65,1},{97,33},{1,65},{33,97},{66,2}... | collective-permute-start | bytes 1437704 | tf_op jit(solution)/shard_map/ppermute | solution.py:30
  99.1 26.1 %collective-permute-start.6 = (bf16[256,512]{1,0:T(8,128)(2,1)S(1)}, bf16[256,512]{1,0:T(8,128)(2,1)}, u32[]{:S(2)}, u32[]{:S(2)}) collective-permute-start(bf16[256,512]{1,0:T(8,128)(2,1)S(1)} %pad_maximum_fusion.29), channel_id=1, source_target_pairs={{0,1},{1,2},{2,3},{3,4},{4,5},{5,6},{6,7},{8,9},{9,10},{10,11},{11... | collective-permute-start | bytes 786440 | tf_op jit(solution)/shard_map/ppermute | solution.py:25
  131.9 28.7 %collective-permute-start.14 = (bf16[256,1152]{1,0:T(8,128)(2,1)S(1)}, bf16[256,1152]{1,0:T(8,128)(2,1)S(1)}, u32[]{:S(2)}, u32[]{:S(2)}) collective-permute-start(bf16[256,1152]{1,0:T(8,128)(2,1)S(1)} %multiply_convert_fusion.5), channel_id=1, source_target_pairs={{3,0},{0,1},{1,2},{2,3},{7,4},{4,5},{5,6},{6,7},{11,8},{8,9},{9,10... | collective-permute-start | bytes 1769480 | tf_op jit(solution)/shard_map/ppermute | solution.py:30
  132.0 28.7 %collective-permute-start.13 = (bf16[256,1152]{1,0:T(8,128)(2,1)S(1)}, bf16[256,1152]{1,0:T(8,128)(2,1)S(1)}, u32[]{:S(2)}, u32[]{:S(2)}) collective-permute-start(bf16[256,1152]{1,0:T(8,128)(2,1)S(1)} %multiply_convert_fusion.5), channel_id=1, source_target_pairs={{2,0},{3,1},{0,2},{1,3},{6,4},{7,5},{4,6},{5,7},{10,8},{11,9},{8,1... | collective-permute-start | bytes 1769480 | tf_op jit(solution)/shard_map/ppermute | solution.py:30
  134.0 28.3 %collective-permute-start.12 = (bf16[256,1152]{1,0:T(8,128)(2,1)S(1)}, bf16[256,1152]{1,0:T(8,128)(2,1)}, u32[]{:S(2)}, u32[]{:S(2)}) collective-permute-start(bf16[256,1152]{1,0:T(8,128)(2,1)S(1)} %multiply_convert_fusion.5), channel_id=1, source_target_pairs={{1,0},{2,1},{3,2},{0,3},{5,4},{6,5},{7,6},{4,7},{9,8},{10,9},{11,1... | collective-permute-start | bytes 1769480 | tf_op jit(solution)/shard_map/ppermute | solution.py:30
  192.3 27.8 %collective-permute-start.16 = (bf16[256,1152]{1,0:T(8,128)(2,1)S(1)}, bf16[256,1152]{1,0:T(8,128)(2,1)S(1)}, u32[]{:S(2)}, u32[]{:S(2)}) collective-permute-start(bf16[256,1152]{1,0:T(8,128)(2,1)S(1)} %get-tuple-element.55), channel_id=1, source_target_pairs={{0,3},{1,0},{2,1},{3,2},{4,7},{5,4},{6,5},{7,6},{8,11},{9,8},{10,9... | collective-permute-start | bytes 1769480 | tf_op jit(solution)/shard_map/ppermute | solution.py:35
  194.3 25.8 %collective-permute-start.15 = (bf16[256,1152]{1,0:T(8,128)(2,1)S(1)}, bf16[256,1152]{1,0:T(8,128)(2,1)S(1)}, u32[]{:S(2)}, u32[]{:S(2)}) collective-permute-start(bf16[256,1152]{1,0:T(8,128)(2,1)S(1)} %get-tuple-element.53), channel_id=1, source_target_pairs={{0,1},{1,2},{2,3},{3,0},{4,5},{5,6},{6,7},{7,4},{8,9},{9,10},{10,1... | collective-permute-start | bytes 1769480 | tf_op jit(solution)/shard_map/ppermute | solution.py:35
  223.0 29.5 %collective-permute-start.20 = (bf16[256,1152]{1,0:T(8,128)(2,1)}, bf16[256,1152]{1,0:T(8,128)(2,1)}, u32[]{:S(2)}, u32[]{:S(2)}) collective-permute-start(bf16[256,1152]{1,0:T(8,128)(2,1)} %get-tuple-element.67), channel_id=1, source_target_pairs={{3,0},{0,1},{1,2},{2,3},{7,4},{4,5},{5,6},{6,7},{11,8},{8,9},{9,10... | collective-permute-start | bytes 1769480 | tf_op jit(solution)/shard_map/ppermute | solution.py:30
  223.8 30.4 %collective-permute-start.19 = (bf16[256,1152]{1,0:T(8,128)(2,1)}, bf16[256,1152]{1,0:T(8,128)(2,1)}, u32[]{:S(2)}, u32[]{:S(2)}) collective-permute-start(bf16[256,1152]{1,0:T(8,128)(2,1)} %get-tuple-element.67), channel_id=1, source_target_pairs={{2,0},{3,1},{0,2},{1,3},{6,4},{7,5},{4,6},{5,7},{10,8},{11,9},{8,1... | collective-permute-start | bytes 1769480 | tf_op jit(solution)/shard_map/ppermute | solution.py:30
  227.1 27.2 %collective-permute-start.18 = (bf16[256,1152]{1,0:T(8,128)(2,1)}, bf16[256,1152]{1,0:T(8,128)(2,1)}, u32[]{:S(2)}, u32[]{:S(2)}) collective-permute-start(bf16[256,1152]{1,0:T(8,128)(2,1)} %get-tuple-element.67), channel_id=1, source_target_pairs={{1,0},{2,1},{3,2},{0,3},{5,4},{6,5},{7,6},{4,7},{9,8},{10,9},{11,1... | collective-permute-start | bytes 1769480 | tf_op jit(solution)/shard_map/ppermute | solution.py:30
  231.6 127.6 %collective-permute-start.28 = (bf16[256,1152]{1,0:T(8,128)(2,1)}, bf16[256,1152]{1,0:T(8,128)(2,1)}, u32[]{:S(2)}, u32[]{:S(2)}) collective-permute-start(bf16[256,1152]{1,0:T(8,128)(2,1)} %fusion.50), channel_id=1, source_target_pairs={{3,0},{0,1},{1,2},{2,3},{7,4},{4,5},{5,6},{6,7},{11,8},{8,9},{9,10... | collective-permute-start | bytes 1769480 | tf_op jit(solution)/shard_map/ppermute | solution.py:30
  233.6 129.4 %collective-permute-start.27 = (bf16[256,1152]{1,0:T(8,128)(2,1)}, bf16[256,1152]{1,0:T(8,128)(2,1)}, u32[]{:S(2)}, u32[]{:S(2)}) collective-permute-start(bf16[256,1152]{1,0:T(8,128)(2,1)} %fusion.50), channel_id=1, source_target_pairs={{2,0},{3,1},{0,2},{1,3},{6,4},{7,5},{4,6},{5,7},{10,8},{11,9},{8,1... | collective-permute-start | bytes 1769480 | tf_op jit(solution)/shard_map/ppermute | solution.py:30
  288.3 28.8 %collective-permute-start.22 = (bf16[256,1152]{1,0:T(8,128)(2,1)S(1)}, bf16[256,1152]{1,0:T(8,128)(2,1)S(1)}, u32[]{:S(2)}, u32[]{:S(2)}) collective-permute-start(bf16[256,1152]{1,0:T(8,128)(2,1)S(1)} %get-tuple-element.52), channel_id=1, source_target_pairs={{0,3},{1,0},{2,1},{3,2},{4,7},{5,4},{6,5},{7,6},{8,11},{9,8},{10,9... | collective-permute-start | bytes 1769480 | tf_op jit(solution)/shard_map/ppermute | solution.py:35
  290.3 26.8 %collective-permute-start.21 = (bf16[256,1152]{1,0:T(8,128)(2,1)S(1)}, bf16[256,1152]{1,0:T(8,128)(2,1)S(1)}, u32[]{:S(2)}, u32[]{:S(2)}) collective-permute-start(bf16[256,1152]{1,0:T(8,128)(2,1)S(1)} %get-tuple-element.50), channel_id=1, source_target_pairs={{0,1},{1,2},{2,3},{3,0},{4,5},{5,6},{6,7},{7,4},{8,9},{9,10},{10,1... | collective-permute-start | bytes 1769480 | tf_op jit(solution)/shard_map/ppermute | solution.py:35
  304.6 60.9 %collective-permute-start.26 = (bf16[256,1152]{1,0:T(8,128)(2,1)}, bf16[256,1152]{1,0:T(8,128)(2,1)}, u32[]{:S(2)}, u32[]{:S(2)}) collective-permute-start(bf16[256,1152]{1,0:T(8,128)(2,1)} %fusion.50), channel_id=1, source_target_pairs={{1,0},{2,1},{3,2},{0,3},{5,4},{6,5},{7,6},{4,7},{9,8},{10,9},{11,1... | collective-permute-start | bytes 1769480 | tf_op jit(solution)/shard_map/ppermute | solution.py:30
  358.2 46.0 %collective-permute-start.34 = (bf16[256,1152]{1,0:T(8,128)(2,1)}, bf16[256,1152]{1,0:T(8,128)(2,1)}, u32[]{:S(2)}, u32[]{:S(2)}) collective-permute-start(bf16[256,1152]{1,0:T(8,128)(2,1)} %multiply_convert_fusion.2), channel_id=1, source_target_pairs={{3,0},{0,1},{1,2},{2,3},{7,4},{4,5},{5,6},{6,7},{11,8},{8,9},{9,10... | collective-permute-start | bytes 1769480 | tf_op jit(solution)/shard_map/ppermute | solution.py:30
  359.2 45.0 %collective-permute-start.33 = (bf16[256,1152]{1,0:T(8,128)(2,1)}, bf16[256,1152]{1,0:T(8,128)(2,1)}, u32[]{:S(2)}, u32[]{:S(2)}) collective-permute-start(bf16[256,1152]{1,0:T(8,128)(2,1)} %multiply_convert_fusion.2), channel_id=1, source_target_pairs={{2,0},{3,1},{0,2},{1,3},{6,4},{7,5},{4,6},{5,7},{10,8},{11,9},{8,1... | collective-permute-start | bytes 1769480 | tf_op jit(solution)/shard_map/ppermute | solution.py:30
  363.0 41.2 %collective-permute-start.32 = (bf16[256,1152]{1,0:T(8,128)(2,1)}, bf16[256,1152]{1,0:T(8,128)(2,1)}, u32[]{:S(2)}, u32[]{:S(2)}) collective-permute-start(bf16[256,1152]{1,0:T(8,128)(2,1)} %multiply_convert_fusion.2), channel_id=1, source_target_pairs={{1,0},{2,1},{3,2},{0,3},{5,4},{6,5},{7,6},{4,7},{9,8},{10,9},{11,1... | collective-permute-start | bytes 1769480 | tf_op jit(solution)/shard_map/ppermute | solution.py:30
  365.5 26.4 %collective-permute-start.30 = (bf16[256,384]{1,0:T(8,128)(2,1)}, bf16[256,384]{1,0:T(8,128)(2,1)}, u32[]{:S(2)}, u32[]{:S(2)}) collective-permute-start(bf16[256,384]{1,0:T(8,128)(2,1)} %bitcast.205), channel_id=1, source_target_pairs={{0,2},{1,3},{2,0},{3,1},{4,6},{5,7},{6,4},{7,5},{8,10},{9,11},{10,... | collective-permute-start | bytes 589832 | tf_op jit(solution)/shard_map/ppermute | solution.py:35
  366.2 32.0 %collective-permute-start.29 = (bf16[256,384]{1,0:T(8,128)(2,1)S(1)}, bf16[256,384]{1,0:T(8,128)(2,1)}, u32[]{:S(2)}, u32[]{:S(2)}) collective-permute-start(bf16[256,384]{1,0:T(8,128)(2,1)S(1)} %bitcast.249), channel_id=1, source_target_pairs={{0,3},{1,0},{2,1},{3,2},{4,7},{5,4},{6,5},{7,6},{8,11},{9,8},{10,9... | collective-permute-start | bytes 589832 | tf_op jit(solution)/shard_map/ppermute | solution.py:35
  404.1 26.1 %collective-permute-start.56 = (bf16[8,72,1792]{2,1,0:T(8,128)(2,1)}, bf16[8,72,1792]{2,1,0:T(8,128)(2,1)}, u32[]{:S(2)}, u32[]{:S(2)}) collective-permute-start(bf16[8,72,1792]{2,1,0:T(8,128)(2,1)} %dynamic-slice_bitcast_fusion.1), channel_id=1, source_target_pairs={{0,8},{8,0},{1,9},{9,1},{2,10},{10,2},{3,11},{11,3},{4,12},{12,4},... | collective-permute-start | bytes 6193160 | tf_op jit(solution)/shard_map/ppermute | solution.py:35
  424.8 48.0 %collective-permute-start.47 = (bf16[8,72,3584]{2,1,0:T(8,128)(2,1)}, bf16[8,72,3584]{2,1,0:T(8,128)(2,1)}, u32[]{:S(2)}, u32[]{:S(2)}) collective-permute-start(bf16[8,72,3584]{2,1,0:T(8,128)(2,1)} %dynamic-slice_bitcast_fusion), channel_id=1, source_target_pairs={{0,8},{8,0},{1,9},{9,1},{2,10},{10,2},{3,11},{11,3},{4,12},{12,4},... | collective-permute-start | bytes 12386312 | tf_op jit(solution)/shard_map/ppermute | solution.py:35
  476.4 27.4 %collective-permute-start.50 = (bf16[2,72,3584]{2,1,0:T(8,128)(2,1)S(1)}, bf16[2,72,3584]{2,1,0:T(8,128)(2,1)S(1)}, u32[]{:S(2)}, u32[]{:S(2)}) collective-permute-start(bf16[2,72,3584]{2,1,0:T(8,128)(2,1)S(1)} %get-tuple-element.46), channel_id=1, source_target_pairs={{0,64},{32,96},{64,0},{96,32},{1,65},{33,97},{65,1},{97,33},{2,66}... | collective-permute-start | bytes 3096584 | tf_op jit(solution)/shard_map/ppermute | solution.py:35
  479.6 44.6 %collective-permute-start.49 = (bf16[2,72,3584]{2,1,0:T(8,128)(2,1)S(1)}, bf16[2,72,3584]{2,1,0:T(8,128)(2,1)S(1)}, u32[]{:S(2)}, u32[]{:S(2)}) collective-permute-start(bf16[2,72,3584]{2,1,0:T(8,128)(2,1)S(1)} %get-tuple-element.47), channel_id=1, source_target_pairs={{0,96},{32,0},{64,32},{96,64},{1,97},{33,1},{65,33},{97,65},{2,98}... | collective-permute-start | bytes 3096584 | tf_op jit(solution)/shard_map/ppermute | solution.py:35
  481.4 42.8 %collective-permute-start.48 = (bf16[2,72,3584]{2,1,0:T(8,128)(2,1)S(1)}, bf16[2,72,3584]{2,1,0:T(8,128)(2,1)S(1)}, u32[]{:S(2)}, u32[]{:S(2)}) collective-permute-start(bf16[2,72,3584]{2,1,0:T(8,128)(2,1)S(1)} %get-tuple-element.45), channel_id=1, source_target_pairs={{0,32},{32,64},{64,96},{96,0},{1,33},{33,65},{65,97},{97,1},{2,34}... | collective-permute-start | bytes 3096584 | tf_op jit(solution)/shard_map/ppermute | solution.py:35
  484.0 43.1 %collective-permute-start.61 = (bf16[72,1792]{1,0:T(8,128)(2,1)S(1)}, bf16[72,1792]{1,0:T(8,128)(2,1)S(1)}, u32[]{:S(2)}, u32[]{:S(2)}) collective-permute-start(bf16[72,1792]{1,0:T(8,128)(2,1)S(1)} %fusion.92), channel_id=1, source_target_pairs={{0,4},{4,0},{1,5},{5,1},{2,6},{6,2},{3,7},{7,3},{8,12},{12,8},{9,1... | collective-permute-start | bytes 774152 | tf_op jit(solution)/shard_map/ppermute | solution.py:35
  (125 other events, 1237.8 us)
Sparse Core Ops, SparseCore 0:
  11.2 83.9 all-gather.2
  97.5 54.6 all-gather.4

commit v2 on v1

--- a/solution.py
+++ b/solution.py
@@ -39,70 +39,84 @@
     return lax.ppermute(array, ("xh", "xl"), [(0, 3), (3, 0), (1, 2), (2, 1)])
 
 
-def gather_rows(block):
+def ordered(value, *after):
+    return lax.optimization_barrier((value,) + after)[0]
+
+
+def gather_rows(block, wait=()):
     rows, width = block.shape
     z = lax.axis_index("z")
     xh = lax.axis_index("xh")
     core = lax.axis_index("core")
     beside = swap_x(block)
     pair = jnp.where(xh == 0, jnp.stack([block, beside]), jnp.stack([beside, block]))
+    ring = [(take(pair, "z", by), by) for by in (1, 3, 2)]
+    arrived = [piece for piece, _ in ring]
     own = jnp.zeros((4, 2, rows, width), block.dtype)
     own = lax.dynamic_update_slice_in_dim(own, pair[None], z, 0)
-    for by in (1, 3, 2):
-        own = lax.dynamic_update_slice_in_dim(own, take(pair, "z", by)[None], (z + by) % 4, 0)
+    if wait:
+        own = ordered(own, *wait)
+    for piece, by in ring:
+        own = lax.dynamic_update_slice_in_dim(own, piece[None], (z + by) % 4, 0)
     other = give(own, "core", 1)
     both = jnp.where(
         core == 0, jnp.stack([own, other], axis=2), jnp.stack([other, own], axis=2)
     )
-    return both.reshape(16 * rows, width)
-
-
-def gather_ring(block):
-    return [block, take(block, "y", 1), take(block, "y", 2), take(block, "y", 3)]
-
-
-def sum_ring(blocks):
-    total = blocks[0].astype(jnp.float32)
-    for by in (1, 3, 2):
-        total = total + give(blocks[by].astype(jnp.bfloat16), "y", by).astype(jnp.float32)
-    return total
-
-
-def pick(array, index, axis):
-    return lax.dynamic_index_in_dim(array, index, axis, keepdims=False)
-
-
-def reduce_rows(part):
-    z = lax.axis_index("z")
-    xh = lax.axis_index("xh")
+    return both.reshape(16 * rows, width), arrived
+
+
+def core_sum(part):
     core = lax.axis_index("core")
-    width = part.shape[1]
-    rows = part.shape[0] // 16
+    rows, width = part.shape[0] // 16, part.shape[1]
     by_core = part.reshape(8, 2, rows, width)
     got = give(pick(by_core, 1 - core, 1), "core", 1)
-    chip = (pick(by_core, core, 1).astype(jnp.float32) + got.astype(jnp.float32)).astype(
-        jnp.bfloat16
-    )
-    by_z = chip.reshape(4, 2, rows, width)
-    total = pick(by_z, z, 0).astype(jnp.float32)
+    total = pick(by_core, core, 1).astype(jnp.float32) + got.astype(jnp.float32)
+    return total.astype(jnp.bfloat16).reshape(4, 2, rows, width)
+
+
+def z_sum(chip):
+    z = lax.axis_index("z")
+    total = pick(chip, z, 0).astype(jnp.float32)
     for by in (1, 3, 2):
-        total = total + give(pick(by_z, (z + by) % 4, 0), "z", by).astype(jnp.float32)
-    column = total.astype(jnp.bfloat16)
+        total = total + give(pick(chip, (z + by) % 4, 0), "z", by).astype(jnp.float32)
+    return total.astype(jnp.bfloat16)
+
+
+def x_sum(column):
+    xh = lax.axis_index("xh")
     got = swap_x(pick(column, 1 - xh, 0))
     half = (pick(column, xh, 0).astype(jnp.float32) + got.astype(jnp.float32)).astype(jnp.bfloat16)
     got = give(half, "xl", 1)
     return (half.astype(jnp.float32) + got.astype(jnp.float32)).astype(jnp.bfloat16)
 
 
+def gather_ring(block):
+    return [block, take(block, "y", 1), take(block, "y", 2), take(block, "y", 3)]
+
+
+def sum_ring(parts):
+    rows = parts[0].shape[0]
+    low = jnp.bfloat16
+    others = ((parts[1][:rows], 1), (parts[1][rows:], 3), (parts[2], 2))
+    total = parts[0].astype(jnp.float32)
+    for part, by in others:
+        total = total + give(part.astype(low), "y", by).astype(jnp.float32)
+    return total
+
+
 def in_order(blocks):
     y = lax.axis_index("y")
-    ordered = []
+    placed = []
     for place in range(4):
         value = blocks[(place - 3) % 4]
         for at in range(3):
             value = jnp.where(y == at, blocks[(place - at) % 4], value)
-        ordered.append(value.astype(jnp.float32))
-    return ordered
+        placed.append(value)
+    return placed
+
+
+def pick(array, index, axis):
+    return lax.dynamic_index_in_dim(array, index, axis, keepdims=False)
 
 
 def inverse_rms(values):
@@ -213,19 +227,20 @@
         axis=1,
     )
     gain_columns = jnp.pad(gain_columns, ((0, 0), (0, 122)))
-    first = gather_rows(
-        jnp.concatenate([query_weight, key_weight, value_weight, gain_columns], axis=1)
-    )
-    full_qkv = first[:, : query_width + 2 * head_size]
-    gains = 1.0 + first[:, query_width + 2 * head_size :].astype(jnp.float32)
-    full_out = gather_rows(out_weight)
-    gate_up = lax.all_gather(
-        jnp.concatenate([feed_slice(gate_weight), feed_slice(up_weight)], axis=1),
+    feed_blocks = lax.all_gather(
+        jnp.concatenate(
+            [feed_slice(gate_weight), feed_slice(up_weight), feed_slice(down_weight)], axis=1
+        ),
         DP,
         axis=0,
         tiled=True,
     )
-    down = lax.all_gather(feed_slice(down_weight), DP, axis=0, tiled=True)
+    first, arrived = gather_rows(
+        jnp.concatenate([query_weight, key_weight, value_weight, gain_columns], axis=1)
+    )
+    qkv_width = query_width + 2 * head_size
+    full_qkv = first[:, :qkv_width]
+    gains = 1.0 + first[:, qkv_width:].astype(jnp.float32)
     gain_rows = gains.T
     one_input = gain_rows[0]
     one_attention = gain_rows[1]
@@ -238,7 +253,6 @@
     input_scale = inverse_rms(residual)
     normed_input = residual * input_scale
     attention_input = (normed_input * one_input).astype(low)
-    input_ring = jnp.concatenate(gather_ring(attention_input), axis=0)
     qkv_raw = jnp.dot(attention_input, full_qkv, preferred_element_type=jnp.float32)
     query_raw = qkv_raw[:, :query_width]
     key_raw = qkv_raw[:, query_width : query_width + head_size]
@@ -255,6 +269,8 @@
     value_low = value_raw.astype(low)
     local_pair = jnp.concatenate([key_low, value_low], axis=1)
     rim_blocks = [from_behind(local_pair, distance) for distance in (1, 2)]
+    input_ring = lax.all_gather(ordered(attention_input, *rim_blocks), "y", axis=0, tiled=True)
+    full_out, _ = gather_rows(ordered(out_weight, *arrived), (local_pair,))
     key_rows = jnp.concatenate(rim_blocks[::-1] + [local_pair], axis=0)
     key_count = key_rows.shape[0]
     key_positions = (seq_index - hop_total) * row_count + lax.iota(jnp.int32, key_count)
@@ -288,14 +304,22 @@
     state_hat = hidden_state * state_scale
     feed_input = (state_hat * one_feed).astype(low)
 
-    feed_ring = jnp.concatenate(gather_ring(feed_input), axis=0)
-    gate_up_raw = jnp.dot(feed_ring, gate_up, preferred_element_type=jnp.float32)
-    gate_raw = gate_up_raw[:, :FEED_SLICE]
-    up_raw = gate_up_raw[:, FEED_SLICE:]
-    gelu_value, gelu_slope = gelu_parts(gate_raw)
-    hidden_low = (gelu_value * up_raw).astype(low)
-    down_part = jnp.einsum("tf,df->td", hidden_low, down, preferred_element_type=jnp.float32)
-    down_raw = sum_ring(jnp.split(down_part, 4, axis=0))
+    feed_blocks, feed_input = lax.optimization_barrier((feed_blocks, feed_input))
+    gate_up = feed_blocks[:, : 2 * FEED_SLICE]
+    down = feed_blocks[:, 2 * FEED_SLICE :]
+    _, feed_1, feed_2, feed_3 = gather_ring(feed_input)
+    feed_chunks = [feed_input, jnp.concatenate([feed_1, feed_3], axis=0), feed_2]
+    kept = []
+    parts = []
+    for chunk in feed_chunks:
+        raw = jnp.dot(chunk, gate_up, preferred_element_type=jnp.float32)
+        gate_raw = raw[:, :FEED_SLICE]
+        up_raw = raw[:, FEED_SLICE:]
+        gelu_value, gelu_slope = gelu_parts(gate_raw)
+        hidden = (gelu_value * up_raw).astype(low)
+        kept.append((hidden, gelu_value.astype(low), (gelu_slope * up_raw).astype(low)))
+        parts.append(jnp.einsum("tf,df->td", hidden, down, preferred_element_type=jnp.float32))
+    down_raw = sum_ring(parts)
     down_scale = inverse_rms(down_raw)
     down_hat = down_raw * down_scale
     layer_value = hidden_state + down_hat * one_output
@@ -304,21 +328,39 @@
     output_gain_vec = jnp.sum(upstream * down_hat, axis=0)
     down_grad_low = rms_backward(down_raw, down_scale, upstream * one_output).astype(low)
 
-    down_ring = jnp.concatenate(gather_ring(down_grad_low), axis=0)
-    hidden_grad = jnp.dot(down_ring, down, preferred_element_type=jnp.float32)
+    _, down_1, down_2, down_3 = gather_ring(down_grad_low)
+    down_chunks = [down_grad_low, jnp.concatenate([down_1, down_3], axis=0), down_2]
+    grads = []
+    parts = []
+    for chunk, (_, value, slope) in zip(down_chunks, kept):
+        hidden_grad = jnp.dot(chunk, down, preferred_element_type=jnp.float32)
+        both = jnp.concatenate(
+            [
+                (hidden_grad * slope.astype(jnp.float32)).astype(low),
+                (hidden_grad * value.astype(jnp.float32)).astype(low),
+            ],
+            axis=1,
+        )
+        grads.append(both)
+        parts.append(jnp.einsum("tf,df->td", both, gate_up, preferred_element_type=jnp.float32))
+    block_part = sum_ring(parts)
     down_weight_part = jnp.einsum(
-        "tc,tf->cf", down_ring, hidden_low, preferred_element_type=jnp.float32
+        "tc,tf->cf",
+        jnp.concatenate(down_chunks, axis=0),
+        jnp.concatenate([hidden for hidden, _, _ in kept], axis=0),
+        preferred_element_type=jnp.float32,
     ).astype(low)
-    gate_grad_low = (hidden_grad * up_raw * gelu_slope).astype(low)
-    up_grad_low = (hidden_grad * gelu_value).astype(low)
-    gate_up_grad = jnp.concatenate([gate_grad_low, up_grad_low], axis=1)
-    feed_part = jnp.einsum("tf,df->td", gate_up_grad, gate_up, preferred_element_type=jnp.float32)
     gate_up_part = jnp.einsum(
-        "tc,tf->cf", feed_ring, gate_up_grad, preferred_element_type=jnp.float32
+        "tc,tf->cf",
+        jnp.concatenate(feed_chunks, axis=0),
+        jnp.concatenate(grads, axis=0),
+        preferred_element_type=jnp.float32,
     ).astype(low)
-    block_part = sum_ring(jnp.split(feed_part, 4, axis=0))
-    down_weight_sum = reduce_rows(down_weight_part)
-    gate_up_sum = reduce_rows(gate_up_part)
+    block_part, down_weight_part, gate_up_part = lax.optimization_barrier(
+        (block_part, down_weight_part, gate_up_part)
+    )
+    down_chip = core_sum(down_weight_part)
+    gate_up_chip = core_sum(gate_up_part)
 
     feed_gain_vec = jnp.sum(block_part * state_hat, axis=0)
     state_grad = upstream + rms_backward(hidden_state, state_scale, block_part * one_feed)
@@ -326,12 +368,17 @@
     attention_grad_low = rms_backward(
         attention_raw, attention_scale, state_grad * one_attention
     ).astype(low)
-    attention_ring = jnp.concatenate(gather_ring(attention_grad_low), axis=0)
-    context_cut = context_low.reshape(row_count, 4, query_width // 4)
-    context_ring = jnp.concatenate(
-        [pick(context_cut, y, 1)]
-        + [give(pick(context_cut, (y + by) % 4, 1), "y", by) for by in (3, 2, 1)],
-        axis=0,
+    attention_grad_low, down_chip, gate_up_chip = lax.optimization_barrier(
+        (attention_grad_low, down_chip, gate_up_chip)
+    )
+    down_column = z_sum(down_chip)
+    gate_up_column = z_sum(gate_up_chip)
+    out_ring = lax.all_gather(
+        jnp.concatenate([attention_grad_low, context_low], axis=1), "y", axis=0, tiled=True
+    )
+    attention_ring = out_ring[:, :model_width]
+    context_ring = lax.dynamic_slice_in_dim(
+        out_ring, model_width + y * (query_width // 4), query_width // 4, 1
     )
     context_grad = jnp.einsum(
         "td,dq->tq", attention_grad_low, full_out, preferred_element_type=jnp.float32
@@ -345,7 +392,8 @@
     score_grad = probs_again * (
         prob_grad - jnp.sum(probs_again * prob_grad, axis=-1, keepdims=True)
     )
-    score_grad_low = score_grad.astype(low)
+    score_grad_low, down_column = lax.optimization_barrier((score_grad.astype(low), down_column))
+    down_weight_sum = x_sum(down_column)
     key_rot_rows = (
         jnp.einsum("htk,thd->kd", score_grad_low, query_low, preferred_element_type=jnp.float32)
         * scaling_factor
@@ -376,12 +424,14 @@
         .astype(low)
     )
     qkv_grad = jnp.concatenate([query_raw_low, key_raw_low, value_raw_low], axis=1)
+    qkv_grad, gate_up_column = lax.optimization_barrier((qkv_grad, gate_up_column))
+    gate_up_sum = x_sum(gate_up_column)
     qkv_cut = qkv_grad.reshape(row_count, 4, qkv_grad.shape[1] // 4)
-    qkv_ring = jnp.concatenate(
+    qkv_ring = in_order(
         [pick(qkv_cut, y, 1)]
-        + [give(pick(qkv_cut, (y + by) % 4, 1), "y", by) for by in (3, 2, 1)],
-        axis=0,
-    )
+        + [give(pick(qkv_cut, (y + by) % 4, 1), "y", by) for by in (3, 2, 1)]
+    )
+    qkv_ring = jnp.concatenate(qkv_ring, axis=0)
     input_grad = jnp.einsum("tq,dq->td", qkv_grad, full_qkv, preferred_element_type=jnp.float32)
     input_gain_vec = jnp.sum(input_grad * normed_input, axis=0)
     tokens_grad = (state_grad + rms_backward(residual, input_scale, input_grad * one_input)).astype(
@@ -404,14 +454,13 @@
         ],
         axis=1,
     )
-    gain_block = jnp.pad(gain_block, ((0, 0), (0, 122)))
+    gain_block = jnp.pad(gain_block, ((0, 0), (0, 122))).astype(low)
     qkv_part = jnp.einsum("tc,tq->cq", input_ring, qkv_ring, preferred_element_type=jnp.float32)
     out_part = jnp.einsum(
         "tc,tq->cq", attention_ring, context_ring, preferred_element_type=jnp.float32
     )
-    attention_sum = reduce_rows(
-        jnp.concatenate([qkv_part, out_part, gain_block], axis=1).astype(low)
-    )
+    attention_part = jnp.concatenate([qkv_part.astype(low), out_part.astype(low), gain_block], axis=1)
+    attention_sum = x_sum(z_sum(core_sum(attention_part)))
     down_blocks = in_order(gather_ring(down_weight_sum))
     gate_up_blocks = in_order(gather_ring(gate_up_sum))
     attention_blocks = in_order(gather_ring(attention_sum))
@@ -424,17 +473,18 @@
     out_weight_grad = jnp.concatenate(
         [b[:, qkv_cols : qkv_cols + out_cols] for b in attention_blocks], axis=1
     )
-    gain_sum = sum(b[:, qkv_cols + out_cols :] for b in attention_blocks)
+    gain_sum = sum(b[:, qkv_cols + out_cols :].astype(jnp.float32) for b in attention_blocks)
+    wide = jnp.float32
     return (
         layer_output,
         tokens_grad,
-        qkv_weight_grad[:, :query_width],
-        qkv_weight_grad[:, query_width : query_width + head_size],
-        qkv_weight_grad[:, query_width + head_size :],
-        out_weight_grad,
-        gate_weight_grad[:, :feed_width],
-        up_weight_grad[:, :feed_width],
-        down_weight_grad,
+        qkv_weight_grad[:, :query_width].astype(wide),
+        qkv_weight_grad[:, query_width : query_width + head_size].astype(wide),
+        qkv_weight_grad[:, query_width + head_size :].astype(wide),
+        out_weight_grad.astype(wide),
+        gate_weight_grad[:, :feed_width].astype(wide),
+        up_weight_grad[:, :feed_width].astype(wide),
+        down_weight_grad.astype(wide),
         gain_sum[:, 0],
         gain_sum[:head_shard, 4],
         gain_sum[:head_shard, 5],

time: 592 us -> 503 us (0.85)
  waiting for transfers between devices: 264 us -> 172 us
  starting transfers between devices: 108 us -> 91.9 us
  other arithmetic: 52.2 us -> 61 us
    ppermute x29 -> x26, waiting for transfers between devices: 138 us -> 45.6 us  [give(): lax.ppermute(array, axis, [(i, (i + by) % count) for i in range(count)])]
    ppermute x27 -> x21, waiting for transfers between devices: 104 us -> 82.2 us  [take(): lax.ppermute(array, axis, [((i + by) % count, i) for i in range(count)])]
    ppermute x4, starting transfers between devices: 23.6 us -> 11.7 us  [from_behind(): return lax.ppermute(array, SEQ, pairs)]
    convert_element_type x16 -> x21, other arithmetic: 13.7 us -> 24.1 us  [the longest x3 6.43 us: core_sum(): return total.astype(jnp.bfloat16).reshape(4, 2, rows, width)]
    ppermute x5, waiting for transfers between devices: 16.2 us -> 26 us  [swap_x(): return lax.ppermute(array, ('xh', 'xl'), [(0, 3), (3, 0), (1, 2), (2, 1)])]
    all_gather x1, waiting for transfers between devices: 0.01 us -> 7.89 us  [local(): lax.all_gather(jnp.concatenate([feed_slice(gate_weight), feed_slice(up_we...]
    unnamed x192 -> x230, local copies, waits for them, and re-layouts: 21.3 us -> 13.9 us
    dot_general x6 -> x14, matrix products: 73.3 us -> 76.7 us  [the longest x3 19.4 us: local(): jnp.einsum('tf,df->td', both, gate_up, preferred_element_type=jnp.float32)]
  transfers between devices with their start and end apart: 67 -> 59, of which waited for: 36 -> 32; matrix products, arithmetic and copies ran while one was open for 28% -> 36% of each run, Pallas kernels for 0% -> 0%
where the time goes in v2:
time: 503 us; the launch traced here: 495 us
  waiting for transfers between devices  172 us (34%)
  matrix products  96.4 us (19%)
  starting transfers between devices  91.9 us (18%)
  other arithmetic  61 us (12%)
  local copies, waits for them, and re-layouts  55.3 us (11%)
  between operations  18.6 us (4%)
    ppermute x21, waiting for transfers between devices, take(): lax.ppermute(array, axis, [((i + by) % count, i) for i in range(count)])  82.2 us
    ppermute x26, waiting for transfers between devices, give(): lax.ppermute(array, axis, [(i, (i + by) % count) for i in range(count)])  45.6 us
    ppermute x21, starting transfers between devices, take(): lax.ppermute(array, axis, [((i + by) % count, i) for i in range(count)])  42.4 us
    ppermute x26, starting transfers between devices, give(): lax.ppermute(array, axis, [(i, (i + by) % count) for i in range(count)])  28.8 us
    ppermute x5, waiting for transfers between devices, swap_x(): return lax.ppermute(array, ('xh', 'xl'), [(0, 3), (3, 0), (1, 2), (2, 1)])  26 us
    dot_general x3, matrix products, local(): jnp.einsum('tf,df->td', both, gate_up, preferred_element_type=jnp.float32)  19.4 us
    dot_general x1, matrix products, local(): jnp.einsum('tc,tf->cf', jnp.concatenate(feed_chunks, axis=0), jnp.concate...  15 us
    unnamed x230, local copies, waits for them, and re-layouts  13.9 us
  transfers between devices with their start and end apart: 59, of which 32 were waited for; matrix products, arithmetic and copies ran while one was open for 36% of the time, Pallas kernels for 0%

profile of v2, /device:TPU:0, one launch (start us, length us, event | category | flops | bytes accessed | tf_op | source)
XLA Modules:
  0.0 494.8 jit_solution(7769918814026190800)
XLA Ops:
  14.8 5.8 %collective-permute-done = bf16[72,1664]{1,0:T(8,128)(2,1)S(1)} collective-permute-done((bf16[72,1664]{1,0:T(8,128)(2,1)S(1)}, bf16[72,1664]{1,0:T(8,128)(2,1)S(1)}, u32[]{:S(2)}, u32[]{:S(2)}) %collective-permute-start) | collective-permute-done | bytes 239648 | tf_op jit(solution)/shard_map/ppermute | solution.py:39
  20.7 4.3 collective-permute-start.1
  27.3 24.2 %collective-permute-done.1 = bf16[2,72,1664]{2,1,0:T(8,128)(2,1)} collective-permute-done((bf16[2,72,1664]{2,1,0:T(8,128)(2,1)S(1)}, bf16[2,72,1664]{2,1,0:T(8,128)(2,1)}, u32[]{:S(2)}, u32[]{:S(2)}) %collective-permute-start.1) | collective-permute-done | bytes 479264 | tf_op jit(solution)/shard_map/ppermute | solution.py:30
  52.9 6.4 %collective-permute-done.3 = bf16[2,72,1664]{2,1,0:T(8,128)(2,1)S(1)} collective-permute-done((bf16[2,72,1664]{2,1,0:T(8,128)(2,1)S(1)}, bf16[2,72,1664]{2,1,0:T(8,128)(2,1)S(1)}, u32[]{:S(2)}, u32[]{:S(2)}) %collective-permute-start.3) | collective-permute-done | bytes 479264 | tf_op jit(solution)/shard_map/ppermute | solution.py:30
  64.6 4.1 collective-permute-done.7
  84.8 4.2 collective-permute-start.6
  89.0 4.8 collective-permute-start.5
  111.1 7.9 %all-gather.4.cloned.1.call-done = bf16[1152,5376]{1,0:T(8,128)(2,1)} async-done(((bf16[72,5376]{1,0:T(8,128)(2,1)}), bf16[1152,5376]{1,0:T(8,128)(2,1)}) %all-gather.4.cloned.1.call-update) | async-done | bytes 12386320 | tf_op jit(solution)/shard_map/all_gather | solution.py:230
  119.0 8.6 %collective-permute-start.16 = (bf16[256,1152]{1,0:T(8,128)(2,1)}, bf16[256,1152]{1,0:T(8,128)(2,1)}, u32[]{:S(2)}, u32[]{:S(2)}) collective-permute-start(bf16[256,1152]{1,0:T(8,128)(2,1)} %multiply_convert_fusion.12), channel_id=1, source_target_pairs={{2,0},{3,1},{0,2},{1,3},{6,4},{7,5},{4,6},{5,7},{10,8},{11,9},{8,1... | collective-permute-start | bytes 1769480 | tf_op jit(solution)/shard_map/ppermute | solution.py:30
  128.3 6.3 %collective-permute-start.13 = (bf16[256,1152]{1,0:T(8,128)(2,1)}, bf16[256,1152]{1,0:T(8,128)(2,1)S(1)}, u32[]{:S(2)}, u32[]{:S(2)}) collective-permute-start(bf16[256,1152]{1,0:T(8,128)(2,1)} %multiply_convert_fusion.12), channel_id=1, source_target_pairs={{3,0},{0,1},{1,2},{2,3},{7,4},{4,5},{5,6},{6,7},{11,8},{8,9},{9,10... | collective-permute-start | bytes 1769480 | tf_op jit(solution)/shard_map/ppermute | solution.py:30
  134.6 7.5 %collective-permute-done.16 = bf16[256,1152]{1,0:T(8,128)(2,1)} collective-permute-done((bf16[256,1152]{1,0:T(8,128)(2,1)}, bf16[256,1152]{1,0:T(8,128)(2,1)}, u32[]{:S(2)}, u32[]{:S(2)}) %collective-permute-start.16) | collective-permute-done | bytes 589856 | tf_op jit(solution)/shard_map/ppermute | solution.py:30
  142.1 6.2 %fusion.36 = f32[256,3584]{1,0:T(8,128)S(1)} fusion(bf16[256,1152]{1,0:T(8,128)(2,1)} %collective-permute-done.16, bf16[1152,5376]{1,0:T(8,128)(2,1)} %all-gather.4.cloned.1.call-done), kind=kOutput, calls=%fused_computation.49 | convolution fusion | flops 2113929216 | bytes 12517376 | tf_op jit(solution)/shard_map/dot_general | solution.py:315
  154.4 6.1 %collective-permute-done.12 = bf16[256,1152]{1,0:T(8,128)(2,1)S(1)} collective-permute-done((bf16[256,1152]{1,0:T(8,128)(2,1)}, bf16[256,1152]{1,0:T(8,128)(2,1)S(1)}, u32[]{:S(2)}, u32[]{:S(2)}) %collective-permute-start.12) | collective-permute-done | bytes 589856 | tf_op jit(solution)/shard_map/ppermute | solution.py:30
  160.4 4.9 fusion.38
  175.2 10.3 %collective-permute-done.15 = bf16[256,1152]{1,0:T(8,128)(2,1)S(1)} collective-permute-done((bf16[256,1152]{1,0:T(8,128)(2,1)S(1)}, bf16[256,1152]{1,0:T(8,128)(2,1)S(1)}, u32[]{:S(2)}, u32[]{:S(2)}) %collective-permute-start.15) | collective-permute-done | bytes 589856 | tf_op jit(solution)/shard_map/ppermute | solution.py:35
  200.1 11.0 %collective-permute-done.22 = bf16[256,1152]{1,0:T(8,128)(2,1)S(1)} collective-permute-done((bf16[256,1152]{1,0:T(8,128)(2,1)S(1)}, bf16[256,1152]{1,0:T(8,128)(2,1)S(1)}, u32[]{:S(2)}, u32[]{:S(2)}) %collective-permute-start.22) | collective-permute-done | bytes 589856 | tf_op jit(solution)/shard_map/ppermute | solution.py:30
  214.4 4.8 fusion.54
  219.2 4.1 collective-permute-done.19
  223.4 6.0 %multiply_convert_fusion.1 = (bf16[512,1792]{1,0:T(8,128)(2,1)}, bf16[512,1792]{1,0:T(8,128)(2,1)}) fusion(f32[512,3584]{1,0:T(8,128)S(1)} %fusion.38, bf16[1152,5376]{1,0:T(8,128)(2,1)S(1)} %copy-done.100, bf16[256,1152]{1,0:T(8,128)(2,1)S(1)} %collective-permute-done.19, bf16[256,1152]{1,0:T(8,128)(2,1)S(1)} %collective-permute-done.18), kind=kOutput, calls=%fused_computation.39 | convolution fusion | flops 2141061120 | bytes 16318464 | tf_op jit(solution)/shard_map/dot_general | solution.py:336
  229.4 7.0 %fusion.48 = bf16[512,1152]{1,0:T(8,128)(2,1)S(1)} fusion(bf16[1152,5376]{1,0:T(8,128)(2,1)S(1)} %copy-done.100, bf16[512,1792]{1,0:T(8,128)(2,1)} %get-tuple-element.75, bf16[512,1792]{1,0:T(8,128)(2,1)} %get-tuple-element.74), kind=kOutput, calls=%fused_computation.67 | convolution fusion | flops 4235788288 | bytes 13107200 | tf_op jit(solution)/shard_map/tf,df->td/dot_general | solution.py:345
  239.9 15.0 %convolution_convert_fusion = bf16[1152,3584]{1,0:T(8,128)(2,1)} fusion(bf16[256,1792]{1,0:T(8,128)(2,1)} %get-tuple-element.79, bf16[256,1792]{1,0:T(8,128)(2,1)} %get-tuple-element.78, bf16[512,1792]{1,0:T(8,128)(2,1)} %get-tuple-element.75, bf16[512,1792]{1,0:T(8,128)(2,1)} %get-tuple-element.74, bf16[256,1792]{1,0:T(8,128)(2,1)} %get-tuple-element.77, ...), kind=kOutput, calls=%fused_computation.1 | convolution fusion | flops 8513323008 | bytes 17956864 | tf_op jit(solution)/shard_map/tc,tf->cf/dot_general | solution.py:353
  255.0 9.3 %convolution_convert_fusion.1 = bf16[1152,1792]{1,0:T(8,128)(2,1)} fusion(bf16[256,1792]{1,0:T(8,128)(2,1)} %copy-done.46, bf16[512,1792]{1,0:T(8,128)(2,1)} %copy-done.39, bf16[256,1792]{1,0:T(8,128)(2,1)} %copy-done.47, bf16[256,1152]{1,0:T(8,128)(2,1)} %copy-done.103, bf16[256,1152]{1,0:T(8,128)(2,1)} %copy-done.104, bf16[256,1152]{1,0:T(8,128)(2,1)} %copy-done.105, ...), kind=kOutput, calls=%fused_computation.4 | convolution fusion | flops 4250370048 | bytes 10158080 | tf_op jit(solution)/shard_map/tc,tf->cf/dot_general | solution.py:347
  264.3 7.6 %convert_add_fusion.5 = f32[256,1152]{1,0:T(8,128)} fusion(bf16[256,1152]{1,0:T(8,128)(2,1)} %collective-permute-done.23, bf16[256,1152]{1,0:T(8,128)(2,1)} %collective-permute-done.21, bf16[256,1152]{1,0:T(8,128)(2,1)} %collective-permute-done.20, bf16[1152,5376]{1,0:T(8,128)(2,1)} %all-gather.4.cloned.1.call-done, bf16[256,1792]{1,0:T(8,128)(2,1)S(1)} %copy-done.107, ...), kind=kOutput, calls=%fused_computation.185 | convolution fusion | flops 2119368704 | bytes 13041664 | tf_op jit(solution)/shard_map/tf,df->td/dot_general | solution.py:345
  326.8 5.1 %collective-permute-done.27 = bf16[2,72,1792]{2,1,0:T(8,128)(2,1)} collective-permute-done((bf16[2,72,1792]{2,1,0:T(8,128)(2,1)}, bf16[2,72,1792]{2,1,0:T(8,128)(2,1)}, u32[]{:S(2)}, u32[]{:S(2)}) %collective-permute-start.27) | collective-permute-done | bytes 516128 | tf_op jit(solution)/shard_map/ppermute | solution.py:35
  348.2 5.7 %collective-permute-done.51 = bf16[72,1792]{1,0:T(8,128)(2,1)} collective-permute-done((bf16[72,1792]{1,0:T(8,128)(2,1)}, bf16[72,1792]{1,0:T(8,128)(2,1)}, u32[]{:S(2)}, u32[]{:S(2)}) %collective-permute-start.51) | collective-permute-done | bytes 258080 | tf_op jit(solution)/shard_map/ppermute | solution.py:39
  361.8 8.4 %collective-permute-done.29 = bf16[256,512]{1,0:T(8,128)(2,1)S(1)} collective-permute-done((bf16[256,512]{1,0:T(8,128)(2,1)}, bf16[256,512]{1,0:T(8,128)(2,1)S(1)}, u32[]{:S(2)}, u32[]{:S(2)}) %collective-permute-start.29) | collective-permute-done | bytes 262176 | tf_op jit(solution)/shard_map/ppermute | solution.py:25
  398.2 4.3 collective-permute-done.46
  407.8 8.1 %collective-permute-done.47 = bf16[72,3584]{1,0:T(8,128)(2,1)S(1)} collective-permute-done((bf16[72,3584]{1,0:T(8,128)(2,1)S(1)}, bf16[72,3584]{1,0:T(8,128)(2,1)S(1)}, u32[]{:S(2)}, u32[]{:S(2)}) %collective-permute-start.47) | collective-permute-done | bytes 516128 | tf_op jit(solution)/shard_map/ppermute | solution.py:35
  422.1 10.3 %collective-permute-done.48 = bf16[72,3584]{1,0:T(8,128)(2,1)S(1)} collective-permute-done((bf16[72,3584]{1,0:T(8,128)(2,1)S(1)}, bf16[72,3584]{1,0:T(8,128)(2,1)S(1)}, u32[]{:S(2)}, u32[]{:S(2)}) %collective-permute-start.48) | collective-permute-done | bytes 516128 | tf_op jit(solution)/shard_map/ppermute | solution.py:30
  432.3 7.6 %collective-permute-done.49 = bf16[72,3584]{1,0:T(8,128)(2,1)S(1)} collective-permute-done((bf16[72,3584]{1,0:T(8,128)(2,1)S(1)}, bf16[72,3584]{1,0:T(8,128)(2,1)S(1)}, u32[]{:S(2)}, u32[]{:S(2)}) %collective-permute-start.49) | collective-permute-done | bytes 516128 | tf_op jit(solution)/shard_map/ppermute | solution.py:30
  451.6 6.6 %collective-permute-done.40 = bf16[2,72,768]{2,1,0:T(8,128)(2,1)S(1)} collective-permute-done((bf16[2,72,768]{2,1,0:T(8,128)(2,1)S(1)}, bf16[2,72,768]{2,1,0:T(8,128)(2,1)S(1)}, u32[]{:S(2)}, u32[]{:S(2)}) %collective-permute-start.40) | collective-permute-done | bytes 221216 | tf_op jit(solution)/shard_map/ppermute | solution.py:35
  462.3 6.1 %collective-permute-done.41 = bf16[72,768]{1,0:T(8,128)(2,1)S(1)} collective-permute-done((bf16[72,768]{1,0:T(8,128)(2,1)S(1)}, bf16[72,768]{1,0:T(8,128)(2,1)S(1)}, u32[]{:S(2)}, u32[]{:S(2)}) %collective-permute-start.41) | collective-permute-done | bytes 110624 | tf_op jit(solution)/shard_map/ppermute | solution.py:39
  (507 shorter events, 237.6 us)
Async XLA Ops:
  8.0 111.0 %all-gather.4.cloned.1.call-start = ((), (), s32[]{:S(2)}) async-start(), calls=%async_computation | async-start | bytes 13160448 | tf_op jit(solution)/shard_map/all_gather | solution.py:230
  11.5 392.3 %all-gather.6.cloned.1.call-start = ((), (), s32[]{:S(2)}) async-start(), calls=%async_computation.1 | async-start | bytes 2949120 | tf_op jit(solution)/shard_map/all_gather | solution.py:272
  20.7 30.8 %collective-permute-start.1 = (bf16[2,72,1664]{2,1,0:T(8,128)(2,1)S(1)}, bf16[2,72,1664]{2,1,0:T(8,128)(2,1)}, u32[]{:S(2)}, u32[]{:S(2)}) collective-permute-start(bf16[2,72,1664]{2,1,0:T(8,128)(2,1)S(1)} %maximum_select_fusion.3), channel_id=1, source_target_pairs={{32,0},{64,32},{96,64},{0,96},{33,1},{65,33},{97,65},{1,97},{34,2}... | collective-permute-start | bytes 1437704 | tf_op jit(solution)/shard_map/ppermute | solution.py:30
  25.1 27.8 %collective-permute-start.2 = (bf16[2,72,1664]{2,1,0:T(8,128)(2,1)S(1)}, bf16[2,72,1664]{2,1,0:T(8,128)(2,1)S(1)}, u32[]{:S(2)}, u32[]{:S(2)}) collective-permute-start(bf16[2,72,1664]{2,1,0:T(8,128)(2,1)S(1)} %maximum_select_fusion.3), channel_id=1, source_target_pairs={{96,0},{0,32},{32,64},{64,96},{97,1},{1,33},{33,65},{65,97},{98,2}... | collective-permute-start | bytes 1437704 | tf_op jit(solution)/shard_map/ppermute | solution.py:30
  25.1 34.2 %collective-permute-start.3 = (bf16[2,72,1664]{2,1,0:T(8,128)(2,1)S(1)}, bf16[2,72,1664]{2,1,0:T(8,128)(2,1)S(1)}, u32[]{:S(2)}, u32[]{:S(2)}) collective-permute-start(bf16[2,72,1664]{2,1,0:T(8,128)(2,1)S(1)} %maximum_select_fusion.3), channel_id=1, source_target_pairs={{64,0},{96,32},{0,64},{32,96},{65,1},{97,33},{1,65},{33,97},{66,2}... | collective-permute-start | bytes 1437704 | tf_op jit(solution)/shard_map/ppermute | solution.py:30
  68.7 25.6 %collective-permute-start.8 = (bf16[2,72,1024]{2,1,0:T(8,128)(2,1)S(1)}, bf16[2,72,1024]{2,1,0:T(8,128)(2,1)}, u32[]{:S(2)}, u32[]{:S(2)}) collective-permute-start(bf16[2,72,1024]{2,1,0:T(8,128)(2,1)S(1)} %maximum_select_fusion.5), channel_id=1, source_target_pairs={{32,0},{64,32},{96,64},{0,96},{33,1},{65,33},{97,65},{1,97},{34,2}... | collective-permute-start | bytes 884744 | tf_op jit(solution)/shard_map/ppermute | solution.py:30
  69.4 27.3 %collective-permute-start.9 = (bf16[2,72,1024]{2,1,0:T(8,128)(2,1)S(1)}, bf16[2,72,1024]{2,1,0:T(8,128)(2,1)}, u32[]{:S(2)}, u32[]{:S(2)}) collective-permute-start(bf16[2,72,1024]{2,1,0:T(8,128)(2,1)S(1)} %maximum_select_fusion.5), channel_id=1, source_target_pairs={{96,0},{0,32},{32,64},{64,96},{97,1},{1,33},{33,65},{65,97},{98,2}... | collective-permute-start | bytes 884744 | tf_op jit(solution)/shard_map/ppermute | solution.py:30
  70.8 27.7 %collective-permute-start.10 = (bf16[2,72,1024]{2,1,0:T(8,128)(2,1)S(1)}, bf16[2,72,1024]{2,1,0:T(8,128)(2,1)}, u32[]{:S(2)}, u32[]{:S(2)}) collective-permute-start(bf16[2,72,1024]{2,1,0:T(8,128)(2,1)S(1)} %maximum_select_fusion.5), channel_id=1, source_target_pairs={{64,0},{96,32},{0,64},{32,96},{65,1},{97,33},{1,65},{33,97},{66,2}... | collective-permute-start | bytes 884744 | tf_op jit(solution)/shard_map/ppermute | solution.py:30
  84.8 17.1 %collective-permute-start.6 = (bf16[256,512]{1,0:T(8,128)(2,1)S(1)}, bf16[256,512]{1,0:T(8,128)(2,1)}, u32[]{:S(2)}, u32[]{:S(2)}) collective-permute-start(bf16[256,512]{1,0:T(8,128)(2,1)S(1)} %pad_maximum_fusion.17), channel_id=1, source_target_pairs={{0,1},{1,2},{2,3},{3,4},{4,5},{5,6},{6,7},{8,9},{9,10},{10,11},{11... | collective-permute-start | bytes 786440 | tf_op jit(solution)/shard_map/ppermute | solution.py:25
  119.0 23.1 %collective-permute-start.16 = (bf16[256,1152]{1,0:T(8,128)(2,1)}, bf16[256,1152]{1,0:T(8,128)(2,1)}, u32[]{:S(2)}, u32[]{:S(2)}) collective-permute-start(bf16[256,1152]{1,0:T(8,128)(2,1)} %multiply_convert_fusion.12), channel_id=1, source_target_pairs={{2,0},{3,1},{0,2},{1,3},{6,4},{7,5},{4,6},{5,7},{10,8},{11,9},{8,1... | collective-permute-start | bytes 1769480 | tf_op jit(solution)/shard_map/ppermute | solution.py:30
  128.3 26.1 %collective-permute-start.13 = (bf16[256,1152]{1,0:T(8,128)(2,1)}, bf16[256,1152]{1,0:T(8,128)(2,1)S(1)}, u32[]{:S(2)}, u32[]{:S(2)}) collective-permute-start(bf16[256,1152]{1,0:T(8,128)(2,1)} %multiply_convert_fusion.12), channel_id=1, source_target_pairs={{3,0},{0,1},{1,2},{2,3},{7,4},{4,5},{5,6},{6,7},{11,8},{8,9},{9,10... | collective-permute-start | bytes 1769480 | tf_op jit(solution)/shard_map/ppermute | solution.py:30
  134.6 25.8 %collective-permute-start.12 = (bf16[256,1152]{1,0:T(8,128)(2,1)}, bf16[256,1152]{1,0:T(8,128)(2,1)S(1)}, u32[]{:S(2)}, u32[]{:S(2)}) collective-permute-start(bf16[256,1152]{1,0:T(8,128)(2,1)} %multiply_convert_fusion.12), channel_id=1, source_target_pairs={{1,0},{2,1},{3,2},{0,3},{5,4},{6,5},{7,6},{4,7},{9,8},{10,9},{11,1... | collective-permute-start | bytes 1769480 | tf_op jit(solution)/shard_map/ppermute | solution.py:30
  150.5 24.7 %collective-permute-start.17 = (bf16[256,1152]{1,0:T(8,128)(2,1)S(1)}, bf16[256,1152]{1,0:T(8,128)(2,1)S(1)}, u32[]{:S(2)}, u32[]{:S(2)}) collective-permute-start(bf16[256,1152]{1,0:T(8,128)(2,1)S(1)} %convolution_convert_fusion.5), channel_id=1, source_target_pairs={{0,2},{1,3},{2,0},{3,1},{4,6},{5,7},{6,4},{7,5},{8,10},{9,11},{10,... | collective-permute-start | bytes 1769480 | tf_op jit(solution)/shard_map/ppermute | solution.py:35
  193.2 17.8 %collective-permute-start.22 = (bf16[256,1152]{1,0:T(8,128)(2,1)S(1)}, bf16[256,1152]{1,0:T(8,128)(2,1)S(1)}, u32[]{:S(2)}, u32[]{:S(2)}) collective-permute-start(bf16[256,1152]{1,0:T(8,128)(2,1)S(1)} %get-tuple-element.96), channel_id=1, source_target_pairs={{2,0},{3,1},{0,2},{1,3},{6,4},{7,5},{4,6},{5,7},{10,8},{11,9},{8,1... | collective-permute-start | bytes 1769480 | tf_op jit(solution)/shard_map/ppermute | solution.py:30
  193.2 30.1 %collective-permute-start.19 = (bf16[256,1152]{1,0:T(8,128)(2,1)S(1)}, bf16[256,1152]{1,0:T(8,128)(2,1)S(1)}, u32[]{:S(2)}, u32[]{:S(2)}) collective-permute-start(bf16[256,1152]{1,0:T(8,128)(2,1)S(1)} %get-tuple-element.96), channel_id=1, source_target_pairs={{3,0},{0,1},{1,2},{2,3},{7,4},{4,5},{5,6},{6,7},{11,8},{8,9},{9,10... | collective-permute-start | bytes 1769480 | tf_op jit(solution)/shard_map/ppermute | solution.py:30
  195.2 28.2 %collective-permute-start.18 = (bf16[256,1152]{1,0:T(8,128)(2,1)S(1)}, bf16[256,1152]{1,0:T(8,128)(2,1)S(1)}, u32[]{:S(2)}, u32[]{:S(2)}) collective-permute-start(bf16[256,1152]{1,0:T(8,128)(2,1)S(1)} %get-tuple-element.96), channel_id=1, source_target_pairs={{1,0},{2,1},{3,2},{0,3},{5,4},{6,5},{7,6},{4,7},{9,8},{10,9},{11,1... | collective-permute-start | bytes 1769480 | tf_op jit(solution)/shard_map/ppermute | solution.py:30
  219.2 45.1 %collective-permute-start.23 = (bf16[256,1152]{1,0:T(8,128)(2,1)}, bf16[256,1152]{1,0:T(8,128)(2,1)}, u32[]{:S(2)}, u32[]{:S(2)}) collective-permute-start(bf16[256,1152]{1,0:T(8,128)(2,1)} %fusion.54), channel_id=1, source_target_pairs={{0,2},{1,3},{2,0},{3,1},{4,6},{5,7},{6,4},{7,5},{8,10},{9,11},{10,... | collective-permute-start | bytes 1769480 | tf_op jit(solution)/shard_map/ppermute | solution.py:35
  237.5 26.7 %collective-permute-start.21 = (bf16[256,1152]{1,0:T(8,128)(2,1)}, bf16[256,1152]{1,0:T(8,128)(2,1)}, u32[]{:S(2)}, u32[]{:S(2)}) collective-permute-start(bf16[256,1152]{1,0:T(8,128)(2,1)} %get-tuple-element.99), channel_id=1, source_target_pairs={{0,3},{1,0},{2,1},{3,2},{4,7},{5,4},{6,5},{7,6},{8,11},{9,8},{10,9... | collective-permute-start | bytes 1769480 | tf_op jit(solution)/shard_map/ppermute | solution.py:35
  238.6 25.6 %collective-permute-start.20 = (bf16[256,1152]{1,0:T(8,128)(2,1)}, bf16[256,1152]{1,0:T(8,128)(2,1)}, u32[]{:S(2)}, u32[]{:S(2)}) collective-permute-start(bf16[256,1152]{1,0:T(8,128)(2,1)} %get-tuple-element.98), channel_id=1, source_target_pairs={{0,1},{1,2},{2,3},{3,0},{4,5},{5,6},{6,7},{7,4},{8,9},{9,10},{10,1... | collective-permute-start | bytes 1769480 | tf_op jit(solution)/shard_map/ppermute | solution.py:35
  274.1 26.9 %collective-permute-start.25 = (bf16[8,72,3584]{2,1,0:T(8,128)(2,1)}, bf16[8,72,3584]{2,1,0:T(8,128)(2,1)}, u32[]{:S(2)}, u32[]{:S(2)}) collective-permute-start(bf16[8,72,3584]{2,1,0:T(8,128)(2,1)} %dynamic-slice_bitcast_fusion), channel_id=1, source_target_pairs={{0,8},{8,0},{1,9},{9,1},{2,10},{10,2},{3,11},{11,3},{4,12},{12,4},... | collective-permute-start | bytes 12386312 | tf_op jit(solution)/shard_map/ppermute | solution.py:35
  288.2 153.3 %all-gather.8.cloned.1.call-start = ((), (), s32[]{:S(2)}) async-start(), calls=%async_computation.2 | async-start | bytes 5570560 | tf_op jit(solution)/shard_map/all_gather | solution.py:376
  306.3 18.8 %collective-permute-start.28 = (bf16[2,72,1792]{2,1,0:T(8,128)(2,1)}, bf16[2,72,1792]{2,1,0:T(8,128)(2,1)}, u32[]{:S(2)}, u32[]{:S(2)}) collective-permute-start(bf16[2,72,1792]{2,1,0:T(8,128)(2,1)} %get-tuple-element.90), channel_id=1, source_target_pairs={{0,64},{32,96},{64,0},{96,32},{1,65},{33,97},{65,1},{97,33},{2,66}... | collective-permute-start | bytes 1548296 | tf_op jit(solution)/shard_map/ppermute | solution.py:35
  307.6 24.2 %collective-permute-start.27 = (bf16[2,72,1792]{2,1,0:T(8,128)(2,1)}, bf16[2,72,1792]{2,1,0:T(8,128)(2,1)}, u32[]{:S(2)}, u32[]{:S(2)}) collective-permute-start(bf16[2,72,1792]{2,1,0:T(8,128)(2,1)} %get-tuple-element.91), channel_id=1, source_target_pairs={{0,96},{32,0},{64,32},{96,64},{1,97},{33,1},{65,33},{97,65},{2,98}... | collective-permute-start | bytes 1548296 | tf_op jit(solution)/shard_map/ppermute | solution.py:35
  309.0 24.9 %collective-permute-start.26 = (bf16[2,72,1792]{2,1,0:T(8,128)(2,1)}, bf16[2,72,1792]{2,1,0:T(8,128)(2,1)}, u32[]{:S(2)}, u32[]{:S(2)}) collective-permute-start(bf16[2,72,1792]{2,1,0:T(8,128)(2,1)} %get-tuple-element.89), channel_id=1, source_target_pairs={{0,32},{32,64},{64,96},{96,0},{1,33},{33,65},{65,97},{97,1},{2,34}... | collective-permute-start | bytes 1548296 | tf_op jit(solution)/shard_map/ppermute | solution.py:35
  311.5 66.1 %collective-permute-start.33 = (bf16[2,72,3584]{2,1,0:T(8,128)(2,1)}, bf16[2,72,3584]{2,1,0:T(8,128)(2,1)}, u32[]{:S(2)}, u32[]{:S(2)}) collective-permute-start(bf16[2,72,3584]{2,1,0:T(8,128)(2,1)} %get-tuple-element.81), channel_id=1, source_target_pairs={{0,64},{32,96},{64,0},{96,32},{1,65},{33,97},{65,1},{97,33},{2,66}... | collective-permute-start | bytes 3096584 | tf_op jit(solution)/shard_map/ppermute | solution.py:35
  313.7 63.8 %collective-permute-start.32 = (bf16[2,72,3584]{2,1,0:T(8,128)(2,1)}, bf16[2,72,3584]{2,1,0:T(8,128)(2,1)}, u32[]{:S(2)}, u32[]{:S(2)}) collective-permute-start(bf16[2,72,3584]{2,1,0:T(8,128)(2,1)} %get-tuple-element.82), channel_id=1, source_target_pairs={{0,96},{32,0},{64,32},{96,64},{1,97},{33,1},{65,33},{97,65},{2,98}... | collective-permute-start | bytes 3096584 | tf_op jit(solution)/shard_map/ppermute | solution.py:35
  325.2 52.3 %collective-permute-start.31 = (bf16[2,72,3584]{2,1,0:T(8,128)(2,1)}, bf16[2,72,3584]{2,1,0:T(8,128)(2,1)}, u32[]{:S(2)}, u32[]{:S(2)}) collective-permute-start(bf16[2,72,3584]{2,1,0:T(8,128)(2,1)} %get-tuple-element.80), channel_id=1, source_target_pairs={{0,32},{32,64},{64,96},{96,0},{1,33},{33,65},{65,97},{97,1},{2,34}... | collective-permute-start | bytes 3096584 | tf_op jit(solution)/shard_map/ppermute | solution.py:35
  340.0 18.1 %collective-permute-start.30 = (bf16[256,512]{1,0:T(8,128)(2,1)}, bf16[256,512]{1,0:T(8,128)(2,1)}, u32[]{:S(2)}, u32[]{:S(2)}) collective-permute-start(bf16[256,512]{1,0:T(8,128)(2,1)} %get-tuple-element.119), channel_id=1, source_target_pairs={{2,0},{3,1},{4,2},{5,3},{6,4},{7,5},{10,8},{11,9},{12,10},{13,11},... | collective-permute-start | bytes 786440 | tf_op jit(solution)/shard_map/ppermute | solution.py:25
  353.9 16.3 %collective-permute-start.29 = (bf16[256,512]{1,0:T(8,128)(2,1)}, bf16[256,512]{1,0:T(8,128)(2,1)S(1)}, u32[]{:S(2)}, u32[]{:S(2)}) collective-permute-start(bf16[256,512]{1,0:T(8,128)(2,1)} %get-tuple-element.118), channel_id=1, source_target_pairs={{1,0},{2,1},{3,2},{4,3},{5,4},{6,5},{7,6},{9,8},{10,9},{11,10},{12... | collective-permute-start | bytes 786440 | tf_op jit(solution)/shard_map/ppermute | solution.py:25
  373.6 34.0 %collective-permute-start.53 = (bf16[72,1792]{1,0:T(8,128)(2,1)S(1)}, bf16[72,1792]{1,0:T(8,128)(2,1)S(1)}, u32[]{:S(2)}, u32[]{:S(2)}) collective-permute-start(bf16[72,1792]{1,0:T(8,128)(2,1)S(1)} %add_convert_fusion.2), channel_id=1, source_target_pairs={{2,0},{3,1},{0,2},{1,3},{6,4},{7,5},{4,6},{5,7},{10,8},{11,9},{8,1... | collective-permute-start | bytes 774152 | tf_op jit(solution)/shard_map/ppermute | solution.py:30
  417.4 22.6 %collective-permute-start.49 = (bf16[72,3584]{1,0:T(8,128)(2,1)S(1)}, bf16[72,3584]{1,0:T(8,128)(2,1)S(1)}, u32[]{:S(2)}, u32[]{:S(2)}) collective-permute-start(bf16[72,3584]{1,0:T(8,128)(2,1)S(1)} %add_convert_fusion), channel_id=1, source_target_pairs={{3,0},{0,1},{1,2},{2,3},{7,4},{4,5},{5,6},{6,7},{11,8},{8,9},{9,10... | collective-permute-start | bytes 1548296 | tf_op jit(solution)/shard_map/ppermute | solution.py:30
  417.7 22.3 %collective-permute-start.50 = (bf16[72,3584]{1,0:T(8,128)(2,1)S(1)}, bf16[72,3584]{1,0:T(8,128)(2,1)S(1)}, u32[]{:S(2)}, u32[]{:S(2)}) collective-permute-start(bf16[72,3584]{1,0:T(8,128)(2,1)S(1)} %add_convert_fusion), channel_id=1, source_target_pairs={{1,0},{2,1},{3,2},{0,3},{5,4},{6,5},{7,6},{4,7},{9,8},{10,9},{11,1... | collective-permute-start | bytes 1548296 | tf_op jit(solution)/shard_map/ppermute | solution.py:30
  (137 other events, 1014.6 us)
Sparse Core Ops, SparseCore 0:
  11.8 107.1 all-gather.3
Sparse Core Ops, SparseCore 1:
  288.3 29.2 all-gather.5
  321.2 63.9 all-gather.7

commit v3 on v2

--- a/solution.py
+++ b/solution.py
@@ -1,8 +1,11 @@
+import functools
 import math
 
 import jax
 import jax.numpy as jnp
 from jax import lax
+from jax.experimental import pallas as pl
+from jax.experimental.pallas import tpu as pltpu
 from jax.sharding import Mesh
 from jax.sharding import PartitionSpec as P
 
@@ -170,6 +173,186 @@
         1.0 + 3.0 * GELU_COEFF * values * values
     )
     return (gelu_value, gelu_slope)
+
+
+HEADS = 4
+HEAD = 256
+SCALE = HEAD**-0.5
+ROWS = 256
+
+
+def dot(left, right, left_axis=1, right_axis=0):
+    return lax.dot_general(
+        left,
+        right,
+        (((left_axis,), (right_axis,)), ((), ())),
+        preferred_element_type=jnp.float32,
+    )
+
+
+def turn(first, second, cosine, sine):
+    return first * cosine - second * sine, second * cosine + first * sine
+
+
+def turn_back(first, second, cosine, sine):
+    return first * cosine + second * sine, second * cosine - first * sine
+
+
+def rows_call(body, outs, flops, name):
+    def call(*operands):
+        specs = [
+            pl.BlockSpec(memory_space=pltpu.SMEM)
+            if operand.dtype == jnp.int32
+            else pl.BlockSpec(memory_space=pltpu.VMEM)
+            for operand in operands
+        ]
+        moved = sum(operand.size * operand.dtype.itemsize for operand in operands)
+        return pl.pallas_call(
+            body,
+            out_shape=[jax.ShapeDtypeStruct(shape, dtype) for shape, dtype in outs],
+            in_specs=specs,
+            out_specs=[pl.BlockSpec(memory_space=pltpu.VMEM) for _ in outs],
+            compiler_params=pltpu.CompilerParams(vmem_limit_bytes=48 * 1024 * 1024),
+            cost_estimate=pl.CostEstimate(flops=flops, bytes_accessed=moved, transcendentals=0),
+            name=name,
+        )(*operands)
+
+    return call
+
+
+def prepare_body(raw, gain, cosine, sine, query, pair):
+    cos, sin = cosine[...], sine[...]
+    half = HEAD // 2
+
+    def finish(block, gains):
+        hat = block * inverse_rms(block) * gains
+        first, second = turn(hat[:, :half], hat[:, half:], cos, sin)
+        return jnp.concatenate([first, second], axis=1).astype(jnp.bfloat16)
+
+    for head in range(HEADS):
+        at = slice(head * HEAD, (head + 1) * HEAD)
+        query[:, at] = finish(raw[:, at], gain[0:1, :])
+    keys = HEADS * HEAD
+    pair[:, :HEAD] = finish(raw[:, keys : keys + HEAD], gain[1:2, :])
+    pair[:, HEAD:] = raw[:, keys + HEAD : keys + 2 * HEAD].astype(jnp.bfloat16)
+
+
+def attend_body(place, query, far, near, own, context, log_total):
+    row = lax.broadcasted_iota(jnp.int32, (ROWS, ROWS), 0)
+    column = lax.broadcasted_iota(jnp.int32, (ROWS, ROWS), 1)
+    seq = place[0]
+    allowed = (
+        (row < column) & (seq >= 2),
+        jnp.full((ROWS, ROWS), seq >= 1),
+        column <= row,
+    )
+    blocks = (far, near, own)
+    lane = lax.broadcasted_iota(jnp.int32, (ROWS, 128), 1)
+    logs = jnp.zeros((ROWS, 128), jnp.float32)
+    for head in range(HEADS):
+        at = slice(head * HEAD, (head + 1) * HEAD)
+        scores = [
+            jnp.where(ok, dot(query[:, at], block[:, :HEAD], 1, 1) * SCALE, -1e30)
+            for ok, block in zip(allowed, blocks)
+        ]
+        top = jnp.max(jnp.maximum(jnp.maximum(scores[0], scores[1]), scores[2]), 1, keepdims=True)
+        terms = [jnp.exp(score - top) for score in scores]
+        total = jnp.sum(terms[0] + terms[1] + terms[2], 1, keepdims=True)
+        share = 1.0 / total
+        out = sum(
+            dot((term * share).astype(jnp.bfloat16), block[:, HEAD:])
+            for term, block in zip(terms, blocks)
+        )
+        context[:, at] = out.astype(jnp.bfloat16)
+        logs = jnp.where(lane == head, top + jnp.log(total), logs)
+    log_total[...] = logs.T[:8]
+
+
+def attend_back_body(
+    place,
+    upstream,
+    out_weight,
+    query,
+    far,
+    near,
+    own,
+    log_total,
+    raw,
+    gain,
+    cosine,
+    sine,
+    far_grad,
+    near_grad,
+    own_grad,
+    query_grad,
+    gain_grad,
+):
+    low = jnp.bfloat16
+    half = HEAD // 2
+    key_at = lax.broadcasted_iota(jnp.int32, (ROWS, ROWS), 0)
+    query_at = lax.broadcasted_iota(jnp.int32, (ROWS, ROWS), 1)
+    seq = place[0]
+    allowed = (
+        (query_at < key_at) & (seq >= 2),
+        jnp.full((ROWS, ROWS), seq >= 1),
+        key_at <= query_at,
+    )
+    blocks = (far, near, own)
+    cos, sin = cosine[...], sine[...]
+    key_grads = [0.0, 0.0, 0.0]
+    value_grads = [0.0, 0.0, 0.0]
+    gain_sum = jnp.zeros((1, HEAD), jnp.float32)
+    for head in range(HEADS):
+        at = slice(head * HEAD, (head + 1) * HEAD)
+        context_grad = dot(upstream[...], out_weight[:, at]).astype(low)
+        queries = query[:, at]
+        logs = log_total[head : head + 1, :]
+        probs = [
+            jnp.where(ok, jnp.exp(dot(block[:, :HEAD], queries, 1, 1) * SCALE - logs), 0.0)
+            for ok, block in zip(allowed, blocks)
+        ]
+        prob_grads = [dot(block[:, HEAD:], context_grad, 1, 1) for block in blocks]
+        inner = jnp.sum(
+            probs[0] * prob_grads[0] + probs[1] * prob_grads[1] + probs[2] * prob_grads[2],
+            0,
+            keepdims=True,
+        )
+        query_rot = 0.0
+        for at_block, block in enumerate(blocks):
+            score_grad = (probs[at_block] * (prob_grads[at_block] - inner)).astype(low)
+            query_rot = query_rot + dot(score_grad, block[:, :HEAD], 0, 0)
+            key_grads[at_block] = key_grads[at_block] + dot(score_grad, queries)
+            value_grads[at_block] = value_grads[at_block] + dot(
+                probs[at_block].astype(low), context_grad
+            )
+        query_rot = query_rot * SCALE
+        first, second = turn_back(query_rot[:, :half], query_rot[:, half:], cos, sin)
+        upper = jnp.concatenate([first, second], axis=1)
+        block = raw[:, at]
+        scaling = inverse_rms(block)
+        gain_sum = gain_sum + jnp.sum(upper * (block * scaling), 0, keepdims=True)
+        query_grad[:, at] = rms_backward(block, scaling, upper * gain[0:1, :]).astype(low)
+    gain_grad[...] = jnp.broadcast_to(gain_sum, (8, HEAD))
+    far_grad[:, :HEAD] = (key_grads[0] * SCALE).astype(low)
+    far_grad[:, HEAD:] = value_grads[0].astype(low)
+    near_grad[:, :HEAD] = (key_grads[1] * SCALE).astype(low)
+    near_grad[:, HEAD:] = value_grads[1].astype(low)
+    own_grad[:, :HEAD] = key_grads[2] * SCALE
+    own_grad[:, HEAD:] = value_grads[2]
+
+
+def pair_back_body(own, near, far, raw, gain, cosine, sine, pair_grad, gain_grad):
+    half = HEAD // 2
+    low = jnp.bfloat16
+    total = own[...] + near[...].astype(jnp.float32) + far[...].astype(jnp.float32)
+    first, second = turn_back(total[:, :half], total[:, half:HEAD], cosine[...], sine[...])
+    upper = jnp.concatenate([first, second], axis=1)
+    block = raw[:, HEADS * HEAD : (HEADS + 1) * HEAD]
+    scaling = inverse_rms(block)
+    gain_sum = jnp.sum(upper * (block * scaling), 0, keepdims=True)
+    gain_grad[...] = jnp.broadcast_to(gain_sum, (8, HEAD))
+    pair_grad[:, :HEAD] = rms_backward(block, scaling, upper * gain[1:2, :]).astype(low)
+    pair_grad[:, HEAD:] = total[:, HEAD:].astype(low)
 
 
 def feed_slice(weight):
@@ -204,13 +387,11 @@
     feed_width = gate_weight.shape[1]
     gain_shard = input_gain.shape[0]
     head_shard = query_gain.shape[0]
-    scaling_factor = head_size ** (-0.5)
     y = lax.axis_index("y")
     seq_index = lax.axis_index("xl") * 4 + y
     positions = seq_index * row_count + lax.iota(jnp.int32, row_count)
     valid_rows = (positions < lengths[0]).astype(jnp.float32)[:, None]
     cosine_table, sine_table = rotary_tables(positions, head_size)
-    hop_total = 2
 
     def spread(vector):
         return jnp.pad(vector, (0, gain_shard - head_shard))
@@ -254,46 +435,26 @@
     normed_input = residual * input_scale
     attention_input = (normed_input * one_input).astype(low)
     qkv_raw = jnp.dot(attention_input, full_qkv, preferred_element_type=jnp.float32)
-    query_raw = qkv_raw[:, :query_width]
-    key_raw = qkv_raw[:, query_width : query_width + head_size]
-    value_raw = qkv_raw[:, query_width + head_size :]
-    query_heads = query_raw.reshape(row_count, head_count, head_size)
-    query_scale = inverse_rms(query_heads)
-    query_hat = query_heads * query_scale
-    query_low = rotate(
-        query_hat * one_query, cosine_table[:, None, :], sine_table[:, None, :]
-    ).astype(low)
-    key_scale = inverse_rms(key_raw)
-    key_hat = key_raw * key_scale
-    key_low = rotate(key_hat * one_key, cosine_table, sine_table).astype(low)
-    value_low = value_raw.astype(low)
-    local_pair = jnp.concatenate([key_low, value_low], axis=1)
-    rim_blocks = [from_behind(local_pair, distance) for distance in (1, 2)]
+    head_gain = jnp.pad(jnp.stack([one_query, one_key]), ((0, 6), (0, 0)))
+    prepare = rows_call(
+        prepare_body,
+        [((row_count, query_width), low), ((row_count, 2 * head_size), low)],
+        1000000,
+        "prepare",
+    )
+    query_low, local_pair = prepare(qkv_raw, head_gain, cosine_table, sine_table)
+    near_pair, far_pair = (from_behind(local_pair, distance) for distance in (1, 2))
+    rim_blocks = [near_pair, far_pair]
     input_ring = lax.all_gather(ordered(attention_input, *rim_blocks), "y", axis=0, tiled=True)
     full_out, _ = gather_rows(ordered(out_weight, *arrived), (local_pair,))
-    key_rows = jnp.concatenate(rim_blocks[::-1] + [local_pair], axis=0)
-    key_count = key_rows.shape[0]
-    key_positions = (seq_index - hop_total) * row_count + lax.iota(jnp.int32, key_count)
-    offsets = positions[:, None] - key_positions[None, :]
-    allowed = (offsets >= 0) & (offsets < WINDOW) & (key_positions[None, :] >= 0)
-    keys_only = key_rows[:, :head_size]
-    values_only = key_rows[:, head_size:]
-
-    def masked_scores():
-        raw_scores = (
-            jnp.einsum("thd,kd->htk", query_low, keys_only, preferred_element_type=jnp.float32)
-            * scaling_factor
-        )
-        return jnp.where(allowed[None], raw_scores, -1e30)
-
-    masked = masked_scores()
-    row_top = jnp.max(masked, axis=-1, keepdims=True)
-    exponent_terms = jnp.exp(masked - row_top)
-    row_total = jnp.sum(exponent_terms, axis=-1, keepdims=True)
-    log_total = row_top + jnp.log(row_total)
-    probs_low = (exponent_terms / row_total).astype(low)
-    context = jnp.einsum("htk,kd->thd", probs_low, values_only, preferred_element_type=jnp.float32)
-    context_low = context.reshape(row_count, query_width).astype(low)
+    place = seq_index.reshape(1).astype(jnp.int32)
+    attend = rows_call(
+        attend_body,
+        [((row_count, query_width), low), ((8, row_count), jnp.float32)],
+        4 * head_count * row_count * 3 * row_count * head_size,
+        "attend",
+    )
+    context_low, log_total = attend(place, query_low, far_pair, near_pair, local_pair)
     attention_raw = jnp.einsum(
         "tq,dq->td", context_low, full_out, preferred_element_type=jnp.float32
     )
@@ -380,50 +541,52 @@
     context_ring = lax.dynamic_slice_in_dim(
         out_ring, model_width + y * (query_width // 4), query_width // 4, 1
     )
-    context_grad = jnp.einsum(
-        "td,dq->tq", attention_grad_low, full_out, preferred_element_type=jnp.float32
-    )
-    context_grad_low = context_grad.reshape(row_count, head_count, head_size).astype(low)
-    probs_again = jnp.exp(masked_scores() - log_total)
-    probs_again_low = probs_again.astype(low)
-    prob_grad = jnp.einsum(
-        "thd,kd->htk", context_grad_low, values_only, preferred_element_type=jnp.float32
-    )
-    score_grad = probs_again * (
-        prob_grad - jnp.sum(probs_again * prob_grad, axis=-1, keepdims=True)
-    )
-    score_grad_low, down_column = lax.optimization_barrier((score_grad.astype(low), down_column))
+    attend_back = rows_call(
+        attend_back_body,
+        [
+            ((row_count, 2 * head_size), low),
+            ((row_count, 2 * head_size), low),
+            ((row_count, 2 * head_size), jnp.float32),
+            ((row_count, query_width), low),
+            ((8, head_size), jnp.float32),
+        ],
+        2 * row_count * query_width * (model_width + 15 * row_count),
+        "attend_back",
+    )
+    far_grad, near_grad, own_grad, query_raw_low, query_gain_rows = attend_back(
+        place,
+        attention_grad_low,
+        full_out,
+        query_low,
+        far_pair,
+        near_pair,
+        local_pair,
+        log_total,
+        qkv_raw,
+        head_gain,
+        cosine_table,
+        sine_table,
+    )
+    far_grad, near_grad, down_column = lax.optimization_barrier((far_grad, near_grad, down_column))
     down_weight_sum = x_sum(down_column)
-    key_rot_rows = (
-        jnp.einsum("htk,thd->kd", score_grad_low, query_low, preferred_element_type=jnp.float32)
-        * scaling_factor
-    )
-    value_rows = jnp.einsum(
-        "htk,thd->kd", probs_again_low, context_grad_low, preferred_element_type=jnp.float32
-    )
-    pair_grad = jnp.concatenate([key_rot_rows, value_rows], axis=1)
-    local_grad = pair_grad[hop_total * row_count :]
-    for distance in range(1, hop_total + 1):
-        begin_row = (hop_total - distance) * row_count
-        local_grad = local_grad + from_behind(
-            pair_grad[begin_row : begin_row + row_count].astype(low), -distance
-        ).astype(jnp.float32)
-    query_rot_grad = (
-        jnp.einsum("htk,kd->thd", score_grad_low, keys_only, preferred_element_type=jnp.float32)
-        * scaling_factor
-    )
-    key_norm_grad = rotate_back(local_grad[:, :head_size], cosine_table, sine_table)
-    key_gain_vec = jnp.sum(key_norm_grad * key_hat, axis=0)
-    key_raw_low = rms_backward(key_raw, key_scale, key_norm_grad * one_key).astype(low)
-    value_raw_low = local_grad[:, head_size:].astype(low)
-    query_norm_grad = rotate_back(query_rot_grad, cosine_table[:, None, :], sine_table[:, None, :])
-    query_gain_vec = jnp.sum(query_norm_grad * query_hat, axis=(0, 1))
-    query_raw_low = (
-        rms_backward(query_heads, query_scale, query_norm_grad * one_query)
-        .reshape(row_count, query_width)
-        .astype(low)
-    )
-    qkv_grad = jnp.concatenate([query_raw_low, key_raw_low, value_raw_low], axis=1)
+    pair_back = rows_call(
+        pair_back_body,
+        [((row_count, 2 * head_size), low), ((8, head_size), jnp.float32)],
+        1000000,
+        "pair_back",
+    )
+    pair_raw_low, key_gain_rows = pair_back(
+        own_grad,
+        from_behind(near_grad, -1),
+        from_behind(far_grad, -2),
+        qkv_raw,
+        head_gain,
+        cosine_table,
+        sine_table,
+    )
+    query_gain_vec = query_gain_rows[0]
+    key_gain_vec = key_gain_rows[0]
+    qkv_grad = jnp.concatenate([query_raw_low, pair_raw_low], axis=1)
     qkv_grad, gate_up_column = lax.optimization_barrier((qkv_grad, gate_up_column))
     gate_up_sum = x_sum(gate_up_column)
     qkv_cut = qkv_grad.reshape(row_count, 4, qkv_grad.shape[1] // 4)
@@ -460,9 +623,11 @@
         "tc,tq->cq", attention_ring, context_ring, preferred_element_type=jnp.float32
     )
     attention_part = jnp.concatenate([qkv_part.astype(low), out_part.astype(low), gain_block], axis=1)
-    attention_sum = x_sum(z_sum(core_sum(attention_part)))
+    attention_column = z_sum(core_sum(attention_part))
+    attention_sum = x_sum(attention_column)
     down_blocks = in_order(gather_ring(down_weight_sum))
-    gate_up_blocks = in_order(gather_ring(gate_up_sum))
+    gate_up_pieces = gather_ring(gate_up_sum)
+    gate_up_blocks = in_order([ordered(piece, attention_column) for piece in gate_up_pieces])
     attention_blocks = in_order(gather_ring(attention_sum))
     down_weight_grad = jnp.concatenate(down_blocks, axis=1)[:, :feed_width]
     gate_weight_grad = jnp.concatenate([b[:, :FEED_SLICE] for b in gate_up_blocks], axis=1)

time: 503 us -> 474 us (0.942)
  local copies, waits for them, and re-layouts: 55.3 us -> 37.6 us
  waiting for transfers between devices: 172 us -> 187 us
  other arithmetic: 61 us -> 48.3 us
  starting transfers between devices: 91.9 us -> 79.2 us
  matrix products: 96.4 us -> 87.4 us
  Pallas kernels: 0 us -> 8.74 us
    ppermute x26, waiting for transfers between devices: 45.6 us -> 70.5 us  [give(): lax.ppermute(array, axis, [(i, (i + by) % count) for i in range(count)])]
    ppermute x4, waiting for transfers between devices: 9.94 us -> 25.9 us  [from_behind(): return lax.ppermute(array, SEQ, pairs)]
    ppermute x5, waiting for transfers between devices: 26 us -> 13.3 us  [swap_x(): return lax.ppermute(array, ('xh', 'xl'), [(0, 3), (3, 0), (1, 2), (2, 1)])]
    ppermute x21, starting transfers between devices: 42.4 us -> 32.2 us  [take(): lax.ppermute(array, axis, [((i + by) % count, i) for i in range(count)])]
    pallas_call x0 -> x4, Pallas kernels: none -> 8.74 us  [call(): pl.pallas_call(body, out_shape=[jax.ShapeDtypeStruct(shape, dtype) for sh...]
    all_gather x1, waiting for transfers between devices: 7.89 us -> 0.01 us  [local(): lax.all_gather(jnp.concatenate([feed_slice(gate_weight), feed_slice(up_we...]
    dot_general x7 -> x0, matrix products: 7.26 us -> none  [the longest x1 2.23 us: local(): jnp.einsum('thd,kd->htk', context_grad_low, values_only, preferred_elemen...]
    unnamed x230 -> x154, local copies, waits for them, and re-layouts: 13.9 us -> 9.34 us
  transfers between devices with their start and end apart: 59 -> 59, of which waited for: 32 -> 36; matrix products, arithmetic and copies ran while one was open for 36% -> 30% of each run, Pallas kernels for 0% -> 2%
where the time goes in v3:
time: 474 us; the launch traced here: 466 us
  waiting for transfers between devices  187 us (39%)
  matrix products  87.4 us (18%)
  starting transfers between devices  79.2 us (17%)
  other arithmetic  48.3 us (10%)
  local copies, waits for them, and re-layouts  37.6 us (8%)
  between operations  18 us (4%)
  Pallas kernels  8.74 us (2%)
    ppermute x21, waiting for transfers between devices, take(): lax.ppermute(array, axis, [((i + by) % count, i) for i in range(count)])  77.2 us
    ppermute x26, waiting for transfers between devices, give(): lax.ppermute(array, axis, [(i, (i + by) % count) for i in range(count)])  70.5 us
    ppermute x21, starting transfers between devices, take(): lax.ppermute(array, axis, [((i + by) % count, i) for i in range(count)])  32.2 us
    ppermute x4, waiting for transfers between devices, from_behind(): return lax.ppermute(array, SEQ, pairs)  25.9 us
    ppermute x26, starting transfers between devices, give(): lax.ppermute(array, axis, [(i, (i + by) % count) for i in range(count)])  24.8 us
    dot_general x3, matrix products, local(): jnp.einsum('tf,df->td', both, gate_up, preferred_element_type=jnp.float32)  20.8 us
    dot_general x1, matrix products, local(): jnp.einsum('tc,tf->cf', jnp.concatenate(feed_chunks, axis=0), jnp.concate...  15 us
    dot_general x3, matrix products, local(): raw = jnp.dot(chunk, gate_up, preferred_element_type=jnp.float32)  13.7 us
  transfers between devices with their start and end apart: 59, of which 36 were waited for; matrix products, arithmetic and copies ran while one was open for 30% of the time, Pallas kernels for 2%

profile of v3, /device:TPU:0, one launch (start us, length us, event | category | flops | bytes accessed | tf_op | source)
XLA Modules:
  0.0 466.3 jit_solution(6226069610747221142)
XLA Ops:
  14.8 5.8 %collective-permute-done = bf16[72,1664]{1,0:T(8,128)(2,1)S(1)} collective-permute-done((bf16[72,1664]{1,0:T(8,128)(2,1)S(1)}, bf16[72,1664]{1,0:T(8,128)(2,1)S(1)}, u32[]{:S(2)}, u32[]{:S(2)}) %collective-permute-start) | collective-permute-done | bytes 239648 | tf_op jit(solution)/shard_map/ppermute | solution.py:42
  20.7 4.3 collective-permute-start.1
  27.3 24.2 %collective-permute-done.1 = bf16[2,72,1664]{2,1,0:T(8,128)(2,1)} collective-permute-done((bf16[2,72,1664]{2,1,0:T(8,128)(2,1)S(1)}, bf16[2,72,1664]{2,1,0:T(8,128)(2,1)}, u32[]{:S(2)}, u32[]{:S(2)}) %collective-permute-start.1) | collective-permute-done | bytes 479264 | tf_op jit(solution)/shard_map/ppermute | solution.py:33
  52.9 6.4 %collective-permute-done.3 = bf16[2,72,1664]{2,1,0:T(8,128)(2,1)S(1)} collective-permute-done((bf16[2,72,1664]{2,1,0:T(8,128)(2,1)S(1)}, bf16[2,72,1664]{2,1,0:T(8,128)(2,1)S(1)}, u32[]{:S(2)}, u32[]{:S(2)}) %collective-permute-start.3) | collective-permute-done | bytes 479264 | tf_op jit(solution)/shard_map/ppermute | solution.py:33
  63.7 4.1 collective-permute-done.7
  87.8 10.7 %collective-permute-done.10 = bf16[2,72,1024]{2,1,0:T(8,128)(2,1)} collective-permute-done((bf16[2,72,1024]{2,1,0:T(8,128)(2,1)}, bf16[2,72,1024]{2,1,0:T(8,128)(2,1)}, u32[]{:S(2)}, u32[]{:S(2)}) %collective-permute-start.10) | collective-permute-done | bytes 294944 | tf_op jit(solution)/shard_map/ppermute | solution.py:33
  99.6 4.9 %collective-permute-start.5 = (bf16[256,512]{1,0:T(8,128)(2,1)S(1)}, bf16[256,512]{1,0:T(8,128)(2,1)S(1)}, u32[]{:S(2)}, u32[]{:S(2)}) collective-permute-start(bf16[256,512]{1,0:T(8,128)(2,1)S(1)} %get-tuple-element.47.own), channel_id=1, source_target_pairs={{0,2},{1,3},{2,4},{3,5},{4,6},{5,7},{8,10},{9,11},{10,12},{11,13},... | collective-permute-start | bytes 786440 | tf_op jit(solution)/shard_map/ppermute | solution.py:28
  107.3 3.9 collective-permute-done.5.far
  111.2 5.2 %collective-permute-done.6.near = bf16[256,512]{1,0:T(8,128)(2,1)S(1)} collective-permute-done((bf16[256,512]{1,0:T(8,128)(2,1)S(1)}, bf16[256,512]{1,0:T(8,128)(2,1)S(1)}, u32[]{:S(2)}, u32[]{:S(2)}) %collective-permute-start.6) | collective-permute-done | bytes 262176 | tf_op jit(solution)/shard_map/ppermute | solution.py:28
  123.3 3.9 collective-permute-start.16
  131.3 10.5 %collective-permute-done.16 = bf16[256,1152]{1,0:T(8,128)(2,1)} collective-permute-done((bf16[256,1152]{1,0:T(8,128)(2,1)}, bf16[256,1152]{1,0:T(8,128)(2,1)}, u32[]{:S(2)}, u32[]{:S(2)}) %collective-permute-start.16) | collective-permute-done | bytes 589856 | tf_op jit(solution)/shard_map/ppermute | solution.py:33
  141.8 6.2 %fusion.35 = f32[256,3584]{1,0:T(8,128)S(1)} fusion(bf16[256,1152]{1,0:T(8,128)(2,1)} %collective-permute-done.16, bf16[1152,5376]{1,0:T(8,128)(2,1)} %all-gather.4.cloned.1.call-done), kind=kOutput, calls=%fused_computation.48 | convolution fusion | flops 2113929216 | bytes 12517376 | tf_op jit(solution)/shard_map/dot_general | solution.py:476
  150.2 4.1 collective-permute-start.17
  154.3 4.9 %fusion.37 = f32[512,3584]{1,0:T(8,128)S(1)} fusion(bf16[1152,5376]{1,0:T(8,128)(2,1)S(1)} %copy-done.65, bf16[256,1152]{1,0:T(8,128)(2,1)S(1)} %collective-permute-done.13, bf16[256,1152]{1,0:T(8,128)(2,1)S(1)} %collective-permute-done.12), kind=kOutput, calls=%fused_computation.50 | convolution fusion | flops 4230217728 | bytes 16777216 | tf_op jit(solution)/shard_map/dot_general | solution.py:476
  168.5 9.5 %collective-permute-done.15 = bf16[256,1152]{1,0:T(8,128)(2,1)S(1)} collective-permute-done((bf16[256,1152]{1,0:T(8,128)(2,1)S(1)}, bf16[256,1152]{1,0:T(8,128)(2,1)S(1)}, u32[]{:S(2)}, u32[]{:S(2)}) %collective-permute-start.15) | collective-permute-done | bytes 589856 | tf_op jit(solution)/shard_map/ppermute | solution.py:38
  190.9 3.4 multiply_convert_fusion.6
  194.3 8.6 %collective-permute-done.22 = bf16[256,1152]{1,0:T(8,128)(2,1)S(1)} collective-permute-done((bf16[256,1152]{1,0:T(8,128)(2,1)S(1)}, bf16[256,1152]{1,0:T(8,128)(2,1)S(1)}, u32[]{:S(2)}, u32[]{:S(2)}) %collective-permute-start.22) | collective-permute-done | bytes 589856 | tf_op jit(solution)/shard_map/ppermute | solution.py:33
  206.2 4.9 %fusion.50 = bf16[256,1152]{1,0:T(8,128)(2,1)} fusion(bf16[1152,5376]{1,0:T(8,128)(2,1)S(1)} %copy-done.65, bf16[256,1792]{1,0:T(8,128)(2,1)} %get-tuple-element.109, bf16[256,1792]{1,0:T(8,128)(2,1)} %get-tuple-element.108), kind=kOutput, calls=%fused_computation.67 | convolution fusion | flops 2117894144 | bytes 10682368 | tf_op jit(solution)/shard_map/tf,df->td/dot_general | solution.py:506
  214.5 6.0 %multiply_convert_fusion.1 = (bf16[512,1792]{1,0:T(8,128)(2,1)}, bf16[512,1792]{1,0:T(8,128)(2,1)}) fusion(f32[512,3584]{1,0:T(8,128)S(1)} %fusion.37, bf16[1152,5376]{1,0:T(8,128)(2,1)S(1)} %copy-done.65, bf16[256,1152]{1,0:T(8,128)(2,1)S(1)} %collective-permute-done.19, bf16[256,1152]{1,0:T(8,128)(2,1)S(1)} %collective-permute-done.18), kind=kOutput, calls=%fused_computation.38 | convolution fusion | flops 2141061120 | bytes 16318464 | tf_op jit(solution)/shard_map/dot_general | solution.py:497
  220.5 7.0 %fusion.45 = bf16[512,1152]{1,0:T(8,128)(2,1)S(1)} fusion(bf16[1152,5376]{1,0:T(8,128)(2,1)S(1)} %copy-done.65, bf16[512,1792]{1,0:T(8,128)(2,1)} %get-tuple-element.105, bf16[512,1792]{1,0:T(8,128)(2,1)} %get-tuple-element.104), kind=kOutput, calls=%fused_computation.58 | convolution fusion | flops 4235788288 | bytes 13107200 | tf_op jit(solution)/shard_map/tf,df->td/dot_general | solution.py:506
  230.8 15.0 %convolution_convert_fusion = bf16[1152,3584]{1,0:T(8,128)(2,1)} fusion(bf16[256,1792]{1,0:T(8,128)(2,1)} %get-tuple-element.109, bf16[256,1792]{1,0:T(8,128)(2,1)} %get-tuple-element.108, bf16[512,1792]{1,0:T(8,128)(2,1)} %get-tuple-element.105, bf16[512,1792]{1,0:T(8,128)(2,1)} %get-tuple-element.104, bf16[256,1792]{1,0:T(8,128)(2,1)} %get-tuple-element.107, ...), kind=kOutput, calls=%fused_computation | convolution fusion | flops 8513323008 | bytes 17956864 | tf_op jit(solution)/shard_map/tc,tf->cf/dot_general | solution.py:514
  245.9 7.3 %convolution_convert_fusion.1 = bf16[1152,1792]{1,0:T(8,128)(2,1)S(1)} fusion(bf16[256,1792]{1,0:T(8,128)(2,1)} %copy-done.33, bf16[512,1792]{1,0:T(8,128)(2,1)} %copy-done.30, bf16[256,1792]{1,0:T(8,128)(2,1)} %copy-done.34, bf16[256,1152]{1,0:T(8,128)(2,1)} %copy-done.68, bf16[256,1152]{1,0:T(8,128)(2,1)} %copy-done.69, bf16[256,1152]{1,0:T(8,128)(2,1)} %copy-done.70, ...), kind=kOutput, calls=%fused_computation.3 | convolution fusion | flops 4250370048 | bytes 10158080 | tf_op jit(solution)/shard_map/tc,tf->cf/dot_general | solution.py:508
  253.3 8.9 %convert_add_fusion.5 = f32[256,1152]{1,0:T(8,128)} fusion(bf16[256,1152]{1,0:T(8,128)(2,1)} %collective-permute-done.23, bf16[256,1152]{1,0:T(8,128)(2,1)} %collective-permute-done.21, bf16[256,1152]{1,0:T(8,128)(2,1)} %collective-permute-done.20, bf16[1152,5376]{1,0:T(8,128)(2,1)} %all-gather.4.cloned.1.call-done, bf16[256,1792]{1,0:T(8,128)(2,1)S(1)} %copy-done.72, ...), kind=kOutput, calls=%fused_computation.159 | convolution fusion | flops 2119368704 | bytes 13041664 | tf_op jit(solution)/shard_map/tf,df->td/dot_general | solution.py:506
  277.5 5.9 %fusion = bf16[8,72,3584]{2,1,0:T(8,128)(2,1)} fusion(bf16[8,72,3584]{2,1,0:T(8,128)(2,1)} %collective-permute-done.25, bf16[8,2,72,3584]{3,2,1,0:T(8,128)(2,1)S(1)} %bitcast.137, s32[]{:T(128)S(6)} %select_n.437), kind=kLoop, calls=%fused_computation.2 | loop fusion | flops 8257536 | bytes 12386308 | tf_op jit(solution)/shard_map/convert_element_type | solution.py:77
  292.3 6.4 %attend_back.1 = (bf16[256,512]{1,0:T(8,128)(2,1)S(1)}, bf16[256,512]{1,0:T(8,128)(2,1)S(1)}, f32[256,512]{1,0:T(8,128)S(1)}, bf16[256,1024]{1,0:T(8,128)(2,1)S(1)}, f32[8,256]{1,0:T(8,128)S(1)}) custom-call(s32[1]{0:T(128)} %bitcast.1.place, bf16[256,1152]{1,0:T(8,128)(2,1)S(1)} %multiply_convert_fusion.9.upstream, bf16[1152,1024]{1,0:T(8,128)(2,1)} %bitcast.133, ...), custom_call_target="tpu_custom_call" | custom-call | flops 2617245696 | bytes 6111236 | tf_op jit(solution)/shard_map/attend_back/pallas_call | solution.py:210
  301.0 8.8 %collective-permute-done.27 = bf16[2,72,1792]{2,1,0:T(8,128)(2,1)} collective-permute-done((bf16[2,72,1792]{2,1,0:T(8,128)(2,1)}, bf16[2,72,1792]{2,1,0:T(8,128)(2,1)}, u32[]{:S(2)}, u32[]{:S(2)}) %collective-permute-start.27) | collective-permute-done | bytes 516128 | tf_op jit(solution)/shard_map/ppermute | solution.py:38
  314.0 4.7 %collective-permute-start.51 = (bf16[72,1792]{1,0:T(8,128)(2,1)}, bf16[72,1792]{1,0:T(8,128)(2,1)}, u32[]{:S(2)}, u32[]{:S(2)}) collective-permute-start(bf16[72,1792]{1,0:T(8,128)(2,1)} %dynamic-slice_bitcast_fusion.10), channel_id=1, source_target_pairs={{0,20},{20,0},{4,16},{16,4},{1,21},{21,1},{5,17},{17,5},{2,22},{22... | collective-permute-start | bytes 774152 | tf_op jit(solution)/shard_map/ppermute | solution.py:42
  328.4 16.7 %collective-permute-done.29.near = bf16[256,512]{1,0:T(8,128)(2,1)S(1)} collective-permute-done((bf16[256,512]{1,0:T(8,128)(2,1)}, bf16[256,512]{1,0:T(8,128)(2,1)S(1)}, u32[]{:S(2)}, u32[]{:S(2)}) %collective-permute-start.29) | collective-permute-done | bytes 262176 | tf_op jit(solution)/shard_map/ppermute | solution.py:28
  345.8 6.2 %collective-permute-done.52 = bf16[72,1792]{1,0:T(8,128)(2,1)S(1)} collective-permute-done((bf16[72,1792]{1,0:T(8,128)(2,1)}, bf16[72,1792]{1,0:T(8,128)(2,1)S(1)}, u32[]{:S(2)}, u32[]{:S(2)}) %collective-permute-start.52) | collective-permute-done | bytes 258080 | tf_op jit(solution)/shard_map/ppermute | solution.py:38
  353.3 14.2 %collective-permute-done.32 = bf16[2,72,3584]{2,1,0:T(8,128)(2,1)} collective-permute-done((bf16[2,72,3584]{2,1,0:T(8,128)(2,1)}, bf16[2,72,3584]{2,1,0:T(8,128)(2,1)}, u32[]{:S(2)}, u32[]{:S(2)}) %collective-permute-start.32) | collective-permute-done | bytes 1032224 | tf_op jit(solution)/shard_map/ppermute | solution.py:38
  404.5 9.4 %collective-permute-done.47 = bf16[72,3584]{1,0:T(8,128)(2,1)S(1)} collective-permute-done((bf16[72,3584]{1,0:T(8,128)(2,1)S(1)}, bf16[72,3584]{1,0:T(8,128)(2,1)S(1)}, u32[]{:S(2)}, u32[]{:S(2)}) %collective-permute-start.47) | collective-permute-done | bytes 516128 | tf_op jit(solution)/shard_map/ppermute | solution.py:38
  430.3 7.3 %collective-permute-done.49 = bf16[72,3584]{1,0:T(8,128)(2,1)S(1)} collective-permute-done((bf16[72,3584]{1,0:T(8,128)(2,1)S(1)}, bf16[72,3584]{1,0:T(8,128)(2,1)S(1)}, u32[]{:S(2)}, u32[]{:S(2)}) %collective-permute-start.49) | collective-permute-done | bytes 516128 | tf_op jit(solution)/shard_map/ppermute | solution.py:33
  (389 shorter events, 198.8 us)
Async XLA Ops:
  8.0 115.3 %all-gather.4.cloned.1.call-start = ((), (), s32[]{:S(2)}) async-start(), calls=%async_computation | async-start | bytes 13160448 | tf_op jit(solution)/shard_map/all_gather | solution.py:411
  11.5 377.0 %all-gather.6.cloned.1.call-start = ((), (), s32[]{:S(2)}) async-start(), calls=%async_computation.1 | async-start | bytes 2949120 | tf_op jit(solution)/shard_map/all_gather | solution.py:448
  20.7 30.8 %collective-permute-start.1 = (bf16[2,72,1664]{2,1,0:T(8,128)(2,1)S(1)}, bf16[2,72,1664]{2,1,0:T(8,128)(2,1)}, u32[]{:S(2)}, u32[]{:S(2)}) collective-permute-start(bf16[2,72,1664]{2,1,0:T(8,128)(2,1)S(1)} %maximum_select_fusion.3), channel_id=1, source_target_pairs={{32,0},{64,32},{96,64},{0,96},{33,1},{65,33},{97,65},{1,97},{34,2}... | collective-permute-start | bytes 1437704 | tf_op jit(solution)/shard_map/ppermute | solution.py:33
  25.1 27.8 %collective-permute-start.2 = (bf16[2,72,1664]{2,1,0:T(8,128)(2,1)S(1)}, bf16[2,72,1664]{2,1,0:T(8,128)(2,1)S(1)}, u32[]{:S(2)}, u32[]{:S(2)}) collective-permute-start(bf16[2,72,1664]{2,1,0:T(8,128)(2,1)S(1)} %maximum_select_fusion.3), channel_id=1, source_target_pairs={{96,0},{0,32},{32,64},{64,96},{97,1},{1,33},{33,65},{65,97},{98,2}... | collective-permute-start | bytes 1437704 | tf_op jit(solution)/shard_map/ppermute | solution.py:33
  25.1 34.2 %collective-permute-start.3 = (bf16[2,72,1664]{2,1,0:T(8,128)(2,1)S(1)}, bf16[2,72,1664]{2,1,0:T(8,128)(2,1)S(1)}, u32[]{:S(2)}, u32[]{:S(2)}) collective-permute-start(bf16[2,72,1664]{2,1,0:T(8,128)(2,1)S(1)} %maximum_select_fusion.3), channel_id=1, source_target_pairs={{64,0},{96,32},{0,64},{32,96},{65,1},{97,33},{1,65},{33,97},{66,2}... | collective-permute-start | bytes 1437704 | tf_op jit(solution)/shard_map/ppermute | solution.py:33
  68.5 17.0 %collective-permute-start.8 = (bf16[2,72,1024]{2,1,0:T(8,128)(2,1)}, bf16[2,72,1024]{2,1,0:T(8,128)(2,1)}, u32[]{:S(2)}, u32[]{:S(2)}) collective-permute-start(bf16[2,72,1024]{2,1,0:T(8,128)(2,1)} %maximum_select_fusion.5), channel_id=1, source_target_pairs={{32,0},{64,32},{96,64},{0,96},{33,1},{65,33},{97,65},{1,97},{34,2}... | collective-permute-start | bytes 884744 | tf_op jit(solution)/shard_map/ppermute | solution.py:33
  69.1 17.7 %collective-permute-start.9 = (bf16[2,72,1024]{2,1,0:T(8,128)(2,1)}, bf16[2,72,1024]{2,1,0:T(8,128)(2,1)}, u32[]{:S(2)}, u32[]{:S(2)}) collective-permute-start(bf16[2,72,1024]{2,1,0:T(8,128)(2,1)} %maximum_select_fusion.5), channel_id=1, source_target_pairs={{96,0},{0,32},{32,64},{64,96},{97,1},{1,33},{33,65},{65,97},{98,2}... | collective-permute-start | bytes 884744 | tf_op jit(solution)/shard_map/ppermute | solution.py:33
  70.6 28.0 %collective-permute-start.10 = (bf16[2,72,1024]{2,1,0:T(8,128)(2,1)}, bf16[2,72,1024]{2,1,0:T(8,128)(2,1)}, u32[]{:S(2)}, u32[]{:S(2)}) collective-permute-start(bf16[2,72,1024]{2,1,0:T(8,128)(2,1)} %maximum_select_fusion.5), channel_id=1, source_target_pairs={{64,0},{96,32},{0,64},{32,96},{65,1},{97,33},{1,65},{33,97},{66,2}... | collective-permute-start | bytes 884744 | tf_op jit(solution)/shard_map/ppermute | solution.py:33
  99.5 18.6 %collective-permute-start.11 = (bf16[4,2,72,1024]{3,2,1,0:T(8,128)(2,1)S(1)}, bf16[4,2,72,1024]{3,2,1,0:T(8,128)(2,1)S(1)}, u32[]{:S(2)}, u32[]{:S(2)}) collective-permute-start(bf16[4,2,72,1024]{3,2,1,0:T(8,128)(2,1)S(1)} %bitcast_dynamic-update-slice_fusion.3), channel_id=1, source_target_pairs={{0,8},{8,0},{1,9},{9,1},{2,10},{10,2},{3,11},{11,3},{4,12},{12,4},... | collective-permute-start | bytes 3538952 | tf_op jit(solution)/shard_map/ppermute | solution.py:38
  123.3 18.4 %collective-permute-start.16 = (bf16[256,1152]{1,0:T(8,128)(2,1)}, bf16[256,1152]{1,0:T(8,128)(2,1)}, u32[]{:S(2)}, u32[]{:S(2)}) collective-permute-start(bf16[256,1152]{1,0:T(8,128)(2,1)} %multiply_convert_fusion.12), channel_id=1, source_target_pairs={{2,0},{3,1},{0,2},{1,3},{6,4},{7,5},{4,6},{5,7},{10,8},{11,9},{8,1... | collective-permute-start | bytes 1769480 | tf_op jit(solution)/shard_map/ppermute | solution.py:33
  127.9 26.3 %collective-permute-start.13 = (bf16[256,1152]{1,0:T(8,128)(2,1)}, bf16[256,1152]{1,0:T(8,128)(2,1)S(1)}, u32[]{:S(2)}, u32[]{:S(2)}) collective-permute-start(bf16[256,1152]{1,0:T(8,128)(2,1)} %multiply_convert_fusion.12), channel_id=1, source_target_pairs={{3,0},{0,1},{1,2},{2,3},{7,4},{4,5},{5,6},{6,7},{11,8},{8,9},{9,10... | collective-permute-start | bytes 1769480 | tf_op jit(solution)/shard_map/ppermute | solution.py:33
  128.0 26.2 %collective-permute-start.12 = (bf16[256,1152]{1,0:T(8,128)(2,1)}, bf16[256,1152]{1,0:T(8,128)(2,1)S(1)}, u32[]{:S(2)}, u32[]{:S(2)}) collective-permute-start(bf16[256,1152]{1,0:T(8,128)(2,1)} %multiply_convert_fusion.12), channel_id=1, source_target_pairs={{1,0},{2,1},{3,2},{0,3},{5,4},{6,5},{7,6},{4,7},{9,8},{10,9},{11,1... | collective-permute-start | bytes 1769480 | tf_op jit(solution)/shard_map/ppermute | solution.py:33
  150.2 18.3 %collective-permute-start.17 = (bf16[256,1152]{1,0:T(8,128)(2,1)S(1)}, bf16[256,1152]{1,0:T(8,128)(2,1)S(1)}, u32[]{:S(2)}, u32[]{:S(2)}) collective-permute-start(bf16[256,1152]{1,0:T(8,128)(2,1)S(1)} %convolution_convert_fusion.5), channel_id=1, source_target_pairs={{0,2},{1,3},{2,0},{3,1},{4,6},{5,7},{6,4},{7,5},{8,10},{9,11},{10,... | collective-permute-start | bytes 1769480 | tf_op jit(solution)/shard_map/ppermute | solution.py:38
  185.0 17.8 %collective-permute-start.22 = (bf16[256,1152]{1,0:T(8,128)(2,1)S(1)}, bf16[256,1152]{1,0:T(8,128)(2,1)S(1)}, u32[]{:S(2)}, u32[]{:S(2)}) collective-permute-start(bf16[256,1152]{1,0:T(8,128)(2,1)S(1)} %get-tuple-element.120), channel_id=1, source_target_pairs={{2,0},{3,1},{0,2},{1,3},{6,4},{7,5},{4,6},{5,7},{10,8},{11,9},{8,1... | collective-permute-start | bytes 1769480 | tf_op jit(solution)/shard_map/ppermute | solution.py:33
  187.5 27.0 %collective-permute-start.19 = (bf16[256,1152]{1,0:T(8,128)(2,1)S(1)}, bf16[256,1152]{1,0:T(8,128)(2,1)S(1)}, u32[]{:S(2)}, u32[]{:S(2)}) collective-permute-start(bf16[256,1152]{1,0:T(8,128)(2,1)S(1)} %get-tuple-element.120), channel_id=1, source_target_pairs={{3,0},{0,1},{1,2},{2,3},{7,4},{4,5},{5,6},{6,7},{11,8},{8,9},{9,10... | collective-permute-start | bytes 1769480 | tf_op jit(solution)/shard_map/ppermute | solution.py:33
  187.7 26.8 %collective-permute-start.18 = (bf16[256,1152]{1,0:T(8,128)(2,1)S(1)}, bf16[256,1152]{1,0:T(8,128)(2,1)S(1)}, u32[]{:S(2)}, u32[]{:S(2)}) collective-permute-start(bf16[256,1152]{1,0:T(8,128)(2,1)S(1)} %get-tuple-element.120), channel_id=1, source_target_pairs={{1,0},{2,1},{3,2},{0,3},{5,4},{6,5},{7,6},{4,7},{9,8},{10,9},{11,1... | collective-permute-start | bytes 1769480 | tf_op jit(solution)/shard_map/ppermute | solution.py:33
  211.1 42.2 %collective-permute-start.23 = (bf16[256,1152]{1,0:T(8,128)(2,1)}, bf16[256,1152]{1,0:T(8,128)(2,1)}, u32[]{:S(2)}, u32[]{:S(2)}) collective-permute-start(bf16[256,1152]{1,0:T(8,128)(2,1)} %fusion.50), channel_id=1, source_target_pairs={{0,2},{1,3},{2,0},{3,1},{4,6},{5,7},{6,4},{7,5},{8,10},{9,11},{10,... | collective-permute-start | bytes 1769480 | tf_op jit(solution)/shard_map/ppermute | solution.py:38
  228.6 24.6 %collective-permute-start.21 = (bf16[256,1152]{1,0:T(8,128)(2,1)}, bf16[256,1152]{1,0:T(8,128)(2,1)}, u32[]{:S(2)}, u32[]{:S(2)}) collective-permute-start(bf16[256,1152]{1,0:T(8,128)(2,1)} %get-tuple-element.123), channel_id=1, source_target_pairs={{0,3},{1,0},{2,1},{3,2},{4,7},{5,4},{6,5},{7,6},{8,11},{9,8},{10,9... | collective-permute-start | bytes 1769480 | tf_op jit(solution)/shard_map/ppermute | solution.py:38
  229.7 23.5 %collective-permute-start.20 = (bf16[256,1152]{1,0:T(8,128)(2,1)}, bf16[256,1152]{1,0:T(8,128)(2,1)}, u32[]{:S(2)}, u32[]{:S(2)}) collective-permute-start(bf16[256,1152]{1,0:T(8,128)(2,1)} %get-tuple-element.122), channel_id=1, source_target_pairs={{0,1},{1,2},{2,3},{3,0},{4,5},{5,6},{6,7},{7,4},{8,9},{9,10},{10,1... | collective-permute-start | bytes 1769480 | tf_op jit(solution)/shard_map/ppermute | solution.py:38
  266.8 124.6 %all-gather.8.cloned.1.call-start = ((), (), s32[]{:S(2)}) async-start(), calls=%async_computation.2 | async-start | bytes 5570560 | tf_op jit(solution)/shard_map/all_gather | solution.py:537
  285.3 24.6 %collective-permute-start.27 = (bf16[2,72,1792]{2,1,0:T(8,128)(2,1)}, bf16[2,72,1792]{2,1,0:T(8,128)(2,1)}, u32[]{:S(2)}, u32[]{:S(2)}) collective-permute-start(bf16[2,72,1792]{2,1,0:T(8,128)(2,1)} %get-tuple-element.119), channel_id=1, source_target_pairs={{0,96},{32,0},{64,32},{96,64},{1,97},{33,1},{65,33},{97,65},{2,98}... | collective-permute-start | bytes 1548296 | tf_op jit(solution)/shard_map/ppermute | solution.py:38
  287.3 23.9 %collective-permute-start.26 = (bf16[2,72,1792]{2,1,0:T(8,128)(2,1)}, bf16[2,72,1792]{2,1,0:T(8,128)(2,1)}, u32[]{:S(2)}, u32[]{:S(2)}) collective-permute-start(bf16[2,72,1792]{2,1,0:T(8,128)(2,1)} %get-tuple-element.117), channel_id=1, source_target_pairs={{0,32},{32,64},{64,96},{96,0},{1,33},{33,65},{65,97},{97,1},{2,34}... | collective-permute-start | bytes 1548296 | tf_op jit(solution)/shard_map/ppermute | solution.py:38
  320.4 32.9 %collective-permute-start.33 = (bf16[2,72,3584]{2,1,0:T(8,128)(2,1)}, bf16[2,72,3584]{2,1,0:T(8,128)(2,1)}, u32[]{:S(2)}, u32[]{:S(2)}) collective-permute-start(bf16[2,72,3584]{2,1,0:T(8,128)(2,1)} %get-tuple-element.111), channel_id=1, source_target_pairs={{0,64},{32,96},{64,0},{96,32},{1,65},{33,97},{65,1},{97,33},{2,66}... | collective-permute-start | bytes 3096584 | tf_op jit(solution)/shard_map/ppermute | solution.py:38
  321.0 46.5 %collective-permute-start.32 = (bf16[2,72,3584]{2,1,0:T(8,128)(2,1)}, bf16[2,72,3584]{2,1,0:T(8,128)(2,1)}, u32[]{:S(2)}, u32[]{:S(2)}) collective-permute-start(bf16[2,72,3584]{2,1,0:T(8,128)(2,1)} %get-tuple-element.112), channel_id=1, source_target_pairs={{0,96},{32,0},{64,32},{96,64},{1,97},{33,1},{65,33},{97,65},{2,98}... | collective-permute-start | bytes 3096584 | tf_op jit(solution)/shard_map/ppermute | solution.py:38
  323.0 45.8 %collective-permute-start.31 = (bf16[2,72,3584]{2,1,0:T(8,128)(2,1)}, bf16[2,72,3584]{2,1,0:T(8,128)(2,1)}, u32[]{:S(2)}, u32[]{:S(2)}) collective-permute-start(bf16[2,72,3584]{2,1,0:T(8,128)(2,1)} %get-tuple-element.110), channel_id=1, source_target_pairs={{0,32},{32,64},{64,96},{96,0},{1,33},{33,65},{65,97},{97,1},{2,34}... | collective-permute-start | bytes 3096584 | tf_op jit(solution)/shard_map/ppermute | solution.py:38
  323.2 21.9 %collective-permute-start.29 = (bf16[256,512]{1,0:T(8,128)(2,1)}, bf16[256,512]{1,0:T(8,128)(2,1)S(1)}, u32[]{:S(2)}, u32[]{:S(2)}) collective-permute-start(bf16[256,512]{1,0:T(8,128)(2,1)} %copy-done.9), channel_id=1, source_target_pairs={{1,0},{2,1},{3,2},{4,3},{5,4},{6,5},{7,6},{9,8},{10,9},{11,10},{12... | collective-permute-start | bytes 786440 | tf_op jit(solution)/shard_map/ppermute | solution.py:28
  325.4 19.9 %collective-permute-start.30 = (bf16[256,512]{1,0:T(8,128)(2,1)}, bf16[256,512]{1,0:T(8,128)(2,1)S(1)}, u32[]{:S(2)}, u32[]{:S(2)}) collective-permute-start(bf16[256,512]{1,0:T(8,128)(2,1)} %copy-done.8), channel_id=1, source_target_pairs={{2,0},{3,1},{4,2},{5,3},{6,4},{7,5},{10,8},{11,9},{12,10},{13,11},... | collective-permute-start | bytes 786440 | tf_op jit(solution)/shard_map/ppermute | solution.py:28
  353.1 49.0 %collective-permute-start.53 = (bf16[72,1792]{1,0:T(8,128)(2,1)S(1)}, bf16[72,1792]{1,0:T(8,128)(2,1)}, u32[]{:S(2)}, u32[]{:S(2)}) collective-permute-start(bf16[72,1792]{1,0:T(8,128)(2,1)S(1)} %add_convert_fusion.1), channel_id=1, source_target_pairs={{2,0},{3,1},{0,2},{1,3},{6,4},{7,5},{4,6},{5,7},{10,8},{11,9},{8,1... | collective-permute-start | bytes 774152 | tf_op jit(solution)/shard_map/ppermute | solution.py:33
  353.2 48.9 %collective-permute-start.54 = (bf16[72,1792]{1,0:T(8,128)(2,1)S(1)}, bf16[72,1792]{1,0:T(8,128)(2,1)}, u32[]{:S(2)}, u32[]{:S(2)}) collective-permute-start(bf16[72,1792]{1,0:T(8,128)(2,1)S(1)} %add_convert_fusion.1), channel_id=1, source_target_pairs={{3,0},{0,1},{1,2},{2,3},{7,4},{4,5},{5,6},{6,7},{11,8},{8,9},{9,10... | collective-permute-start | bytes 774152 | tf_op jit(solution)/shard_map/ppermute | solution.py:33
  383.2 18.9 %collective-permute-start.55 = (bf16[72,1792]{1,0:T(8,128)(2,1)S(1)}, bf16[72,1792]{1,0:T(8,128)(2,1)}, u32[]{:S(2)}, u32[]{:S(2)}) collective-permute-start(bf16[72,1792]{1,0:T(8,128)(2,1)S(1)} %add_convert_fusion.1), channel_id=1, source_target_pairs={{1,0},{2,1},{3,2},{0,3},{5,4},{6,5},{7,6},{4,7},{9,8},{10,9},{11,1... | collective-permute-start | bytes 774152 | tf_op jit(solution)/shard_map/ppermute | solution.py:33
  415.0 22.6 %collective-permute-start.49 = (bf16[72,3584]{1,0:T(8,128)(2,1)S(1)}, bf16[72,3584]{1,0:T(8,128)(2,1)S(1)}, u32[]{:S(2)}, u32[]{:S(2)}) collective-permute-start(bf16[72,3584]{1,0:T(8,128)(2,1)S(1)} %add_convert_fusion), channel_id=1, source_target_pairs={{3,0},{0,1},{1,2},{2,3},{7,4},{4,5},{5,6},{6,7},{11,8},{8,9},{9,10... | collective-permute-start | bytes 1548296 | tf_op jit(solution)/shard_map/ppermute | solution.py:33
  416.1 22.4 %collective-permute-start.50 = (bf16[72,3584]{1,0:T(8,128)(2,1)S(1)}, bf16[72,3584]{1,0:T(8,128)(2,1)S(1)}, u32[]{:S(2)}, u32[]{:S(2)}) collective-permute-start(bf16[72,3584]{1,0:T(8,128)(2,1)S(1)} %add_convert_fusion), channel_id=1, source_target_pairs={{1,0},{2,1},{3,2},{0,3},{5,4},{6,5},{7,6},{4,7},{9,8},{10,9},{11,1... | collective-permute-start | bytes 1548296 | tf_op jit(solution)/shard_map/ppermute | solution.py:33
  (102 other events, 824.6 us)
Sparse Core Ops, SparseCore 0:
  11.8 107.1 all-gather.3
Sparse Core Ops, SparseCore 1:
  266.9 32.8 all-gather.5
  301.9 66.4 all-gather.7

commit v4 on v3

v4 whole, which is shorter than its diff:
```python
import functools
import math

import jax
import jax.numpy as jnp
from jax import lax
from jax.experimental import pallas as pl
from jax.experimental.pallas import tpu as pltpu
from jax.sharding import Mesh
from jax.sharding import PartitionSpec as P

EPSILON = 1e-06
GELU_COEFF = 0.044715
AXES = ("z", "xh", "core", "xl", "y")
SIZES = (4, 2, 2, 2, 4)
DP = ("z", "xh", "core")
SEQ = ("xl", "y")
FEED_SLICE = 1792
FEED_TILE = 896
HEADS = 4
HEAD = 256
SCALE = HEAD**-0.5
ROWS = 256
VMEM = 16 * 1024 * 1024
LONG = 12 * 10**9
SMALL = pl.CostEstimate(flops=1000, bytes_accessed=1000, transcendentals=0)


def from_behind(array, by):
    pairs = [(i, i + by) for i in range(8) if 0 <= i + by < 8]
    return lax.ppermute(array, SEQ, pairs)


def take(array, axis, by):
    count = lax.axis_size(axis)
    return lax.ppermute(array, axis, [((i + by) % count, i) for i in range(count)])


def give(array, axis, by):
    count = lax.axis_size(axis)
    return lax.ppermute(array, axis, [(i, (i + by) % count) for i in range(count)])


def swap_x(array):
    return lax.ppermute(array, ("xh", "xl"), [(0, 3), (3, 0), (1, 2), (2, 1)])


def ordered(value, *after):
    return lax.optimization_barrier((value,) + after)[0]


def pick(array, index, axis):
    return lax.dynamic_index_in_dim(array, index, axis, keepdims=False)


def with_other_x(block):
    xh = lax.axis_index("xh")
    beside = swap_x(block)
    return jnp.where(xh == 0, jnp.stack([block, beside]), jnp.stack([beside, block])), beside


def gather_rows(pair, wait=()):
    _, rows, width = pair.shape
    z = lax.axis_index("z")
    core = lax.axis_index("core")
    ring = [(take(pair, "z", by), by) for by in (1, 3, 2)]
    arrived = [piece for piece, _ in ring]
    own = jnp.zeros((4, 2, rows, width), pair.dtype)
    own = lax.dynamic_update_slice_in_dim(own, pair[None], z, 0)
    own = ordered(own, *wait)
    for piece, by in ring:
        own = lax.dynamic_update_slice_in_dim(own, piece[None], (z + by) % 4, 0)
    other = give(own, "core", 1)
    both = jnp.where(
        core == 0, jnp.stack([own, other], axis=2), jnp.stack([other, own], axis=2)
    )
    return both.reshape(16 * rows, width), arrived


def small_sum(chip):
    z = lax.axis_index("z")
    xh = lax.axis_index("xh")
    wide = jnp.float32
    total = pick(chip, z, 0).astype(wide)
    for by in (1, 3, 2):
        total = total + give(pick(chip, (z + by) % 4, 0), "z", by).astype(wide)
    column = total.astype(jnp.bfloat16)
    half = pick(column, xh, 0).astype(wide) + swap_x(pick(column, 1 - xh, 0)).astype(wide)
    half = half.astype(jnp.bfloat16)
    whole = (half.astype(wide) + give(half, "xl", 1).astype(wide)).astype(jnp.bfloat16)
    return whole, column


def in_order(blocks):
    y = lax.axis_index("y")
    placed = []
    for place in range(4):
        value = blocks[(place - 3) % 4]
        for at in range(3):
            value = jnp.where(y == at, blocks[(place - at) % 4], value)
        placed.append(value)
    return placed


def inverse_rms(values):
    return lax.rsqrt(jnp.mean(values * values, axis=-1, keepdims=True) + EPSILON)


def rms_backward(values, scaling, upstream):
    inner = jnp.mean(upstream * values, axis=-1, keepdims=True)
    return scaling * (upstream - values * (scaling * scaling) * inner)


def rotary_tables(positions, head_size):
    half_size = head_size // 2
    exponents = lax.iota(jnp.float32, half_size) * (2.0 / head_size)
    frequency = jnp.power(10000.0, -exponents)
    angles = positions.astype(jnp.float32)[:, None] * frequency[None, :]
    return (jnp.cos(angles), jnp.sin(angles))


def gelu_parts(values):
    root_coeff = math.sqrt(2.0 / math.pi)
    square = values * values
    bend = jnp.tanh(values * (root_coeff + (root_coeff * GELU_COEFF) * square))
    part = 0.5 + 0.5 * bend
    gelu_value = values * part
    inner = root_coeff + (3.0 * GELU_COEFF * root_coeff) * square
    gelu_slope = part + gelu_value * (1.0 - bend) * inner
    return (gelu_value, gelu_slope)


def dot(left, right, left_axis=1, right_axis=0):
    return lax.dot_general(
        left,
        right,
        (((left_axis,), (right_axis,)), ((), ())),
        preferred_element_type=jnp.float32,
    )


def turn(first, second, cosine, sine):
    return first * cosine - second * sine, second * cosine + first * sine


def turn_back(first, second, cosine, sine):
    return first * cosine + second * sine, second * cosine - first * sine


def rows_call(body, outs, name):
    def call(*operands):
        specs = [
            pl.BlockSpec(memory_space=pltpu.SMEM)
            if operand.dtype == jnp.int32
            else pl.BlockSpec(memory_space=pltpu.VMEM)
            for operand in operands
        ]
        return pl.pallas_call(
            body,
            out_shape=[jax.ShapeDtypeStruct(shape, dtype) for shape, dtype in outs],
            in_specs=specs,
            out_specs=[pl.BlockSpec(memory_space=pltpu.VMEM) for _ in outs],
            compiler_params=pltpu.CompilerParams(vmem_limit_bytes=VMEM),
            cost_estimate=SMALL,
            name=name,
        )(*operands)

    return call


def prepare_body(raw, gain, cosine, sine, query, pair):
    cos, sin = cosine[...], sine[...]
    half = HEAD // 2

    def finish(block, gains):
        hat = block * inverse_rms(block) * gains
        first, second = turn(hat[:, :half], hat[:, half:], cos, sin)
        return jnp.concatenate([first, second], axis=1).astype(jnp.bfloat16)

    for head in range(HEADS):
        at = slice(head * HEAD, (head + 1) * HEAD)
        query[:, at] = finish(raw[:, at], gain[0:1, :])
    keys = HEADS * HEAD
    pair[:, :HEAD] = finish(raw[:, keys : keys + HEAD], gain[1:2, :])
    pair[:, HEAD:] = raw[:, keys + HEAD : keys + 2 * HEAD].astype(jnp.bfloat16)


def attend_body(place, query, far, near, own, context, log_total):
    row = lax.broadcasted_iota(jnp.int32, (ROWS, ROWS), 0)
    column = lax.broadcasted_iota(jnp.int32, (ROWS, ROWS), 1)
    seq = place[0]
    allowed = (
        (row < column) & (seq >= 2),
        jnp.full((ROWS, ROWS), seq >= 1),
        column <= row,
    )
    blocks = (far, near, own)
    lane = lax.broadcasted_iota(jnp.int32, (ROWS, 128), 1)
    logs = jnp.zeros((ROWS, 128), jnp.float32)
    for head in range(HEADS):
        at = slice(head * HEAD, (head + 1) * HEAD)
        scores = [
            jnp.where(ok, dot(query[:, at], block[:, :HEAD], 1, 1) * SCALE, -1e30)
            for ok, block in zip(allowed, blocks)
        ]
        top = jnp.max(jnp.maximum(jnp.maximum(scores[0], scores[1]), scores[2]), 1, keepdims=True)
        terms = [jnp.exp(score - top) for score in scores]
        total = jnp.sum(terms[0] + terms[1] + terms[2], 1, keepdims=True)
        share = 1.0 / total
        out = sum(
            dot((term * share).astype(jnp.bfloat16), block[:, HEAD:])
            for term, block in zip(terms, blocks)
        )
        context[:, at] = out.astype(jnp.bfloat16)
        logs = jnp.where(lane == head, top + jnp.log(total), logs)
    log_total[...] = logs.T[:8]


def attend_back_body(
    place,
    upstream,
    out_weight,
    query,
    far,
    near,
    own,
    log_total,
    raw,
    gain,
    cosine,
    sine,
    far_grad,
    near_grad,
    own_grad,
    query_grad,
    gain_grad,
):
    low = jnp.bfloat16
    half = HEAD // 2
    key_at = lax.broadcasted_iota(jnp.int32, (ROWS, ROWS), 0)
    query_at = lax.broadcasted_iota(jnp.int32, (ROWS, ROWS), 1)
    seq = place[0]
    allowed = (
        (query_at < key_at) & (seq >= 2),
        jnp.full((ROWS, ROWS), seq >= 1),
        key_at <= query_at,
    )
    blocks = (far, near, own)
    cos, sin = cosine[...], sine[...]
    key_grads = [0.0, 0.0, 0.0]
    value_grads = [0.0, 0.0, 0.0]
    gain_sum = jnp.zeros((1, HEAD), jnp.float32)
    for head in range(HEADS):
        at = slice(head * HEAD, (head + 1) * HEAD)
        context_grad = dot(upstream[...], out_weight[:, at]).astype(low)
        queries = query[:, at]
        logs = log_total[head : head + 1, :]
        probs = [
            jnp.where(ok, jnp.exp(dot(block[:, :HEAD], queries, 1, 1) * SCALE - logs), 0.0)
            for ok, block in zip(allowed, blocks)
        ]
        prob_grads = [dot(block[:, HEAD:], context_grad, 1, 1) for block in blocks]
        inner = jnp.sum(
            probs[0] * prob_grads[0] + probs[1] * prob_grads[1] + probs[2] * prob_grads[2],
            0,
            keepdims=True,
        )
        query_rot = 0.0
        for at_block, block in enumerate(blocks):
            score_grad = (probs[at_block] * (prob_grads[at_block] - inner)).astype(low)
            query_rot = query_rot + dot(score_grad, block[:, :HEAD], 0, 0)
            key_grads[at_block] = key_grads[at_block] + dot(score_grad, queries)
            value_grads[at_block] = value_grads[at_block] + dot(
                probs[at_block].astype(low), context_grad
            )
        query_rot = query_rot * SCALE
        first, second = turn_back(query_rot[:, :half], query_rot[:, half:], cos, sin)
        upper = jnp.concatenate([first, second], axis=1)
        block = raw[:, at]
        scaling = inverse_rms(block)
        gain_sum = gain_sum + jnp.sum(upper * (block * scaling), 0, keepdims=True)
        query_grad[:, at] = rms_backward(block, scaling, upper * gain[0:1, :]).astype(low)
    gain_grad[...] = jnp.broadcast_to(gain_sum, (8, HEAD))
    far_grad[:, :HEAD] = (key_grads[0] * SCALE).astype(low)
    far_grad[:, HEAD:] = value_grads[0].astype(low)
    near_grad[:, :HEAD] = (key_grads[1] * SCALE).astype(low)
    near_grad[:, HEAD:] = value_grads[1].astype(low)
    own_grad[:, :HEAD] = key_grads[2] * SCALE
    own_grad[:, HEAD:] = value_grads[2]


def pair_back_body(query, own, near, far, raw, gain, cosine, sine, pair_grad, cut, gain_grad):
    half = HEAD // 2
    low = jnp.bfloat16
    total = own[...] + near[...].astype(jnp.float32) + far[...].astype(jnp.float32)
    first, second = turn_back(total[:, :half], total[:, half:HEAD], cosine[...], sine[...])
    upper = jnp.concatenate([first, second], axis=1)
    block = raw[:, HEADS * HEAD : (HEADS + 1) * HEAD]
    scaling = inverse_rms(block)
    gain_sum = jnp.sum(upper * (block * scaling), 0, keepdims=True)
    gain_grad[...] = jnp.broadcast_to(gain_sum, (8, HEAD))
    keys = rms_backward(block, scaling, upper * gain[1:2, :]).astype(low)
    values = total[:, HEAD:].astype(low)
    pair_grad[:, :HEAD] = keys
    pair_grad[:, HEAD:] = values
    size = cut.shape[2]
    cut[0] = query[:, :size]
    cut[1] = query[:, size : 2 * size]
    cut[2] = jnp.concatenate([query[:, 2 * size :], keys[:, :half]], axis=1)
    cut[3] = jnp.concatenate([keys[:, half:], values], axis=1)


def residual_body(
    context, out_weight, tokens, attention_gain, feed_gain, raw, state, feed_input
):
    value = dot(context[...], out_weight[...], 1, 1)
    raw[...] = value
    hidden = tokens[...].astype(jnp.float32) + value * inverse_rms(value) * attention_gain[...]
    state[...] = hidden
    feed_input[...] = (hidden * inverse_rms(hidden) * feed_gain[...]).astype(jnp.bfloat16)


def down_body(
    part, near, across, behind, state, cotangent, valid, gain, layer, down_grad, gain_grad
):
    wide = jnp.float32
    raw = (
        part[...].astype(wide)
        + near[...].astype(wide)
        + across[...].astype(wide)
        + behind[...].astype(wide)
    )
    scaling = inverse_rms(raw)
    hat = raw * scaling
    ok = valid[:, :1]
    layer[...] = (ok * (state[...] + hat * gain[...])).astype(jnp.bfloat16)
    upstream = cotangent[...].astype(wide) * ok
    gain_grad[...] = jnp.broadcast_to(
        jnp.sum(upstream * hat, 0, keepdims=True), (8, hat.shape[1])
    )
    down_grad[...] = rms_backward(raw, scaling, upstream * gain[...]).astype(jnp.bfloat16)


def state_body(
    part,
    near,
    across,
    behind,
    state,
    raw,
    cotangent,
    valid,
    feed_gain,
    attention_gain,
    attention_grad,
    state_grad,
    gain_grads,
):
    wide = jnp.float32
    feed_grad = (
        part[...].astype(wide)
        + near[...].astype(wide)
        + across[...].astype(wide)
        + behind[...].astype(wide)
    )
    hidden = state[...]
    scaling = inverse_rms(hidden)
    upstream = cotangent[...].astype(wide) * valid[:, :1]
    total = upstream + rms_backward(hidden, scaling, feed_grad * feed_gain[...])
    state_grad[...] = total
    value = raw[...]
    value_scaling = inverse_rms(value)
    width = value.shape[1]
    gain_grads[:8] = jnp.broadcast_to(
        jnp.sum(feed_grad * (hidden * scaling), 0, keepdims=True), (8, width)
    )
    gain_grads[8:] = jnp.broadcast_to(
        jnp.sum(total * (value * value_scaling), 0, keepdims=True), (8, width)
    )
    attention_grad[...] = rms_backward(value, value_scaling, total * attention_gain[...]).astype(
        jnp.bfloat16
    )


def input_body(
    query_grad, pair_grad, weight, tokens, state_grad, gain, tokens_grad, gain_grad
):
    queries = query_grad.shape[1]
    pairs = pair_grad.shape[1]
    grad = dot(query_grad[...], weight[:, :queries], 1, 1) + dot(
        pair_grad[...], weight[:, queries : queries + pairs], 1, 1
    )
    value = tokens[...].astype(jnp.float32)
    scaling = inverse_rms(value)
    gain_grad[...] = jnp.broadcast_to(
        jnp.sum(grad * (value * scaling), 0, keepdims=True), (8, value.shape[1])
    )
    tokens_grad[...] = (
        state_grad[...] + rms_backward(value, scaling, grad * gain[...])
    ).astype(jnp.bfloat16)


def feed_body(place, rows, weights, *refs):
    hidden_out, value_out, slope_out, part, total = refs[-5:]
    low = jnp.bfloat16
    total[...] = jnp.zeros_like(total)

    @pl.loop(0, FEED_SLICE // FEED_TILE)
    def _(tile):
        gate_at, up_at, down_at = (
            pl.ds(pl.multiple_of(start + tile * FEED_TILE, 128), FEED_TILE)
            for start in (0, FEED_SLICE, 2 * FEED_SLICE)
        )
        to = slice(place, place + rows.shape[0])
        gate_raw = dot(rows[...], weights[:, gate_at])
        up_raw = dot(rows[...], weights[:, up_at])
        value, slope = gelu_parts(gate_raw)
        hidden = (value * up_raw).astype(low)
        hidden_out[to, gate_at] = hidden
        value_out[to, gate_at] = value.astype(low)
        slope_out[to, gate_at] = (slope * up_raw).astype(low)
        total[...] += dot(hidden, weights[:, down_at], 1, 1)

    part[...] = total[...].astype(low)


def feed_back_body(place, rows, weights, value, slope, *refs):
    gate_out, up_out, part, total = refs[-4:]
    low = jnp.bfloat16
    total[...] = jnp.zeros_like(total)

    @pl.loop(0, FEED_SLICE // FEED_TILE)
    def _(tile):
        gate_at, up_at, down_at = (
            pl.ds(pl.multiple_of(start + tile * FEED_TILE, 128), FEED_TILE)
            for start in (0, FEED_SLICE, 2 * FEED_SLICE)
        )
        to = slice(place, place + rows.shape[0])
        hidden_grad = dot(rows[...], weights[:, down_at])
        gate_grad = (hidden_grad * slope[to, gate_at].astype(jnp.float32)).astype(low)
        up_grad = (hidden_grad * value[to, gate_at].astype(jnp.float32)).astype(low)
        gate_out[to, gate_at] = gate_grad
        up_out[to, gate_at] = up_grad
        total[...] += dot(gate_grad, weights[:, gate_at], 1, 1) + dot(
            up_grad, weights[:, up_at], 1, 1
        )

    part[...] = total[...].astype(low)


def feed_call(body, rows, weights, read, kept, place, outs, cost, name):
    count, width = rows.shape
    operands = [rows, weights, *read, *kept]
    whole = pl.BlockSpec(memory_space=pltpu.VMEM)
    first_kept = 2 + len(read)
    return pl.pallas_call(
        functools.partial(body, place),
        in_specs=[whole] * first_kept + [pl.BlockSpec(memory_space=pl.ANY)] * len(kept),
        out_specs=[whole] * (outs + 1),
        out_shape=[jax.ShapeDtypeStruct((4 * ROWS, FEED_SLICE), jnp.bfloat16)] * outs
        + [jax.ShapeDtypeStruct((count, width), jnp.bfloat16)],
        scratch_shapes=[pltpu.VMEM((count, width), jnp.float32)],
        input_output_aliases={first_kept + i: i for i in range(len(kept))},
        compiler_params=pltpu.CompilerParams(vmem_limit_bytes=VMEM),
        cost_estimate=pl.CostEstimate(flops=cost, bytes_accessed=1000, transcendentals=0),
        name=name,
    )(*operands)


def product_body(core, left, right, *refs):
    away, here, total = refs[-3:]
    rows = left.shape[1] // 16
    width = right.shape[1]

    def split(to, first, columns):
        for two in range(4):
            pieces = [
                total[pl.ds(pl.multiple_of((4 * two + 2 * i + first) * rows, 8), rows), :columns]
                for i in (0, 1)
            ]
            yield slice(two * 2 * rows, (two + 1) * 2 * rows), jnp.concatenate(pieces, axis=0)

    for start in range(0, width, total.shape[1]):
        size = min(total.shape[1], width - start)
        at = slice(start, start + size)
        total[:, :size] = dot(left[...], right[:, at], 0, 0)
        for to, first in ((away, 1 - core[0]), (here, core[0])):
            for place, value in split(to, first, size):
                to[place, at] = value.astype(to.dtype)
    if len(refs) > 3:
        extra = refs[0]
        at = slice(width, width + extra.shape[1])
        total[:, : extra.shape[1]] = extra[...]
        for to, first in ((away, 1 - core[0]), (here, core[0])):
            for place, value in split(to, first, extra.shape[1]):
                to[place, at] = value.astype(to.dtype)


def product(core, left, right, *extra):
    width = right.shape[1] + sum(block.shape[1] for block in extra)
    out = jax.ShapeDtypeStruct((left.shape[1] // 2, width), jnp.bfloat16)
    whole = pl.BlockSpec(memory_space=pltpu.VMEM)
    away, here = pl.pallas_call(
        product_body,
        in_specs=[pl.BlockSpec(memory_space=pltpu.SMEM)] + [whole] * (2 + len(extra)),
        out_specs=[whole, whole],
        out_shape=[out, out],
        scratch_shapes=[pltpu.VMEM((left.shape[1], 512), jnp.float32)],
        compiler_params=pltpu.CompilerParams(vmem_limit_bytes=VMEM),
        cost_estimate=SMALL,
        name="product",
    )(core, left, right, *extra)
    return here, give(away, "core", 1)


def added(halves):
    here, got = halves
    return (here.astype(jnp.float32) + got.astype(jnp.float32)).astype(jnp.bfloat16)


def spread_in_body(gate, gate_got, up, up_got, down, down_got, spread):
    rows = spread.shape[1]
    half = FEED_SLICE // 2
    for two in range(4):
        at = slice(two * 2 * rows, (two + 1) * 2 * rows)
        gates, ups, downs = (
            here[at].astype(jnp.float32) + got[at].astype(jnp.float32)
            for here, got in ((gate, gate_got), (up, up_got), (down, down_got))
        )
        for block in range(2):
            of = slice(block * rows, (block + 1) * rows)
            to = 4 * two + 2 * block
            spread[to, :, :FEED_SLICE] = gates[of].astype(spread.dtype)
            spread[to, :, FEED_SLICE:] = downs[of, :half].astype(spread.dtype)
            spread[to + 1, :, :FEED_SLICE] = ups[of].astype(spread.dtype)
            spread[to + 1, :, FEED_SLICE:] = downs[of, half:].astype(spread.dtype)


def spread_out_body(sums, gate, up, down):
    width = gate.shape[1]
    half = FEED_SLICE // 2
    for y in range(4):
        start = y * FEED_SLICE
        size = min(FEED_SLICE, width - start)
        gate[:, start : start + size] = sums[y, :, :size].astype(jnp.float32)
        up[:, start : start + size] = sums[4 + y, :, :size].astype(jnp.float32)
        for xl in range(2):
            first = start + xl * half
            size = min(half, width - first)
            down[:, first : first + size] = sums[
                4 * xl + y, :, FEED_SLICE : FEED_SLICE + size
            ].astype(jnp.float32)


def feed_slice(weight):
    y = lax.axis_index("y")
    padded = jnp.pad(weight, ((0, 0), (0, 4 * FEED_SLICE - weight.shape[1])))
    return lax.dynamic_slice_in_dim(padded, y * FEED_SLICE, FEED_SLICE, 1)


def local(
    tokens,
    cotangent,
    lengths,
    query_weight,
    key_weight,
    value_weight,
    out_weight,
    gate_weight,
    up_weight,
    down_weight,
    input_gain,
    query_gain,
    key_gain,
    attention_gain,
    feedforward_gain,
    output_gain,
):
    low = jnp.bfloat16
    wide = jnp.float32
    row_count, model_width = tokens.shape
    head_size = key_weight.shape[1]
    head_count = query_weight.shape[1] // head_size
    query_width = head_count * head_size
    qkv_width = query_width + 2 * head_size
    feed_width = gate_weight.shape[1]
    gain_shard = input_gain.shape[0]
    head_shard = query_gain.shape[0]
    y = lax.axis_index("y")
    seq_index = lax.axis_index("xl") * 4 + y
    place = seq_index.reshape(1).astype(jnp.int32)
    core = lax.axis_index("core").reshape(1).astype(jnp.int32)
    positions = seq_index * row_count + lax.iota(jnp.int32, row_count)
    valid = jnp.broadcast_to((positions < lengths[0]).astype(wide)[:, None], (row_count, 128))
    cosine, sine = rotary_tables(positions, head_size)

    def spread(vector):
        return jnp.pad(vector, (0, gain_shard - head_shard))

    gain_columns = jnp.stack(
        [
            input_gain,
            attention_gain,
            feedforward_gain,
            output_gain,
            spread(query_gain),
            spread(key_gain),
        ],
        axis=1,
    )
    gain_columns = jnp.pad(gain_columns, ((0, 0), (0, 122)))
    feed_weights = lax.all_gather(
        jnp.concatenate(
            [feed_slice(gate_weight), feed_slice(up_weight), feed_slice(down_weight)], axis=1
        ),
        DP,
        axis=0,
        tiled=True,
    )
    pairs, beside = with_other_x(
        jnp.concatenate([query_weight, key_weight, value_weight, gain_columns, out_weight], axis=1)
    )
    qkv_columns = qkv_width + gain_columns.shape[1]
    full_qkv, arrived = gather_rows(pairs[:, :, :qkv_columns])
    tokens_ring = [take(ordered(tokens, beside), "y", by) for by in (1, 2, 3)]
    gains = 1.0 + full_qkv[:, qkv_width : qkv_width + 8].astype(wide).T
    one_input, one_attention, one_feed, one_output = (gains[i : i + 1] for i in range(4))
    head_gain = gains.reshape(8, 16, gain_shard)[4:6, :, :head_shard].reshape(2, head_size)
    head_gain = jnp.pad(head_gain, ((0, 6), (0, 0)))

    def attention_input_of(rows):
        values = rows.astype(wide)
        return (values * inverse_rms(values) * one_input).astype(low)

    attention_input = attention_input_of(tokens)
    qkv_raw = jnp.dot(attention_input, full_qkv[:, :qkv_width], preferred_element_type=wide)
    prepare = rows_call(
        prepare_body,
        [((row_count, query_width), low), ((row_count, 2 * head_size), low)],
        "prepare",
    )
    query_low, local_pair = prepare(qkv_raw, head_gain, cosine, sine)
    near_pair, far_pair = (from_behind(local_pair, distance) for distance in (1, 2))
    full_out, _ = gather_rows(ordered(pairs[:, :, qkv_columns:], *arrived), (local_pair,))
    input_ring = attention_input_of(jnp.concatenate([tokens] + tokens_ring, axis=0))
    near_pair, far_pair, input_ring = lax.optimization_barrier((near_pair, far_pair, input_ring))
    attend = rows_call(
        attend_body,
        [((row_count, query_width), low), ((8, row_count), wide)],
        "attend",
    )
    context_low, log_total = attend(place, query_low, far_pair, near_pair, local_pair)
    residual = rows_call(
        residual_body,
        [
            ((row_count, model_width), wide),
            ((row_count, model_width), wide),
            ((row_count, model_width), low),
        ],
        "residual",
    )
    attention_raw, state, feed_input = residual(
        context_low, full_out, tokens, one_attention, one_feed
    )

    weights, feed_input = lax.optimization_barrier((feed_weights, feed_input))

    def exchange(rows, run):
        two, one, three = (take(rows, "y", by) for by in (2, 1, 3))
        kept, two_part = run(two, [], 3 * row_count, 1000)
        across = give(two_part, "y", 2)
        both = jnp.concatenate([one, three], axis=0)
        kept, both_part = run(both, kept, 0, LONG)
        from_one = give(both_part[:row_count], "y", 1)
        from_three = give(both_part[row_count:], "y", 3)
        *kept, across, both = lax.optimization_barrier((*kept, across, both))
        kept, own_part = run(rows, kept, 2 * row_count, LONG)
        ring = jnp.concatenate([ordered(both, own_part, from_one, from_three), rows, two], axis=0)
        return kept, [own_part, from_one, across, from_three], ring

    def forward(rows, kept, at, cost):
        *kept, part = feed_call(feed_body, rows, weights, [], kept, at, 3, cost, "feed")
        return kept, part

    kept, terms, feed_ring = exchange(feed_input, forward)
    hidden, value, slope = kept
    finish = rows_call(
        down_body,
        [
            ((row_count, model_width), low),
            ((row_count, model_width), low),
            ((8, model_width), wide),
        ],
        "finish",
    )
    layer_output, down_grad, output_gain_rows = finish(
        *terms, state, cotangent, valid, one_output
    )

    def backward(rows, kept, at, cost):
        *kept, part = feed_call(
            feed_back_body, rows, weights, [value, slope], kept, at, 2, cost, "feed_back"
        )
        return kept, part

    rows72 = gain_shard
    (gate_grad, up_grad), terms, down_ring = exchange(down_grad, backward)
    halves = [
        half
        for left, right in ((feed_ring, gate_grad), (feed_ring, up_grad), (down_ring, hidden))
        for half in product(core, left, right)
    ]
    (spread_in,) = rows_call(
        spread_in_body, [((16, rows72, FEED_SLICE * 3 // 2), low)], "spread_in"
    )(*halves)
    feed_sum = lax.psum_scatter(spread_in, ("z", "xh", "xl"), scatter_dimension=0, tiled=False)
    back = rows_call(
        state_body,
        [
            ((row_count, model_width), low),
            ((row_count, model_width), wide),
            ((16, model_width), wide),
        ],
        "state_back",
    )
    attention_grad, state_grad, state_gain_rows = back(
        *terms, state, attention_raw, cotangent, valid, one_feed, one_attention
    )

    attend_back = rows_call(
        attend_back_body,
        [
            ((row_count, 2 * head_size), low),
            ((row_count, 2 * head_size), low),
            ((row_count, 2 * head_size), wide),
            ((row_count, query_width), low),
            ((8, head_size), wide),
        ],
        "attend_back",
    )
    far_grad, near_grad, own_grad, query_grad, query_gain_rows = attend_back(
        place,
        attention_grad,
        full_out,
        query_low,
        far_pair,
        near_pair,
        local_pair,
        log_total,
        qkv_raw,
        head_gain,
        cosine,
        sine,
    )
    near_back = from_behind(near_grad, -1)
    far_back = from_behind(far_grad, -2)
    out_chip = added(product(core, ordered(attention_grad, near_grad), context_low))
    out_cut = out_chip.reshape(model_width // 2, 4, query_width // 4)
    out_sum = pick(out_cut, y, 1).astype(wide)
    for by in (1, 3, 2):
        out_sum = out_sum + give(pick(out_cut, (y + by) % 4, 1), "y", by).astype(wide)
    pair_back = rows_call(
        pair_back_body,
        [
            ((row_count, 2 * head_size), low),
            ((4, row_count, qkv_width // 4), low),
            ((8, head_size), wide),
        ],
        "pair_back",
    )
    pair_grad, qkv_cut, key_gain_rows = pair_back(
        query_grad, own_grad, near_back, far_back, qkv_raw, head_gain, cosine, sine
    )
    qkv_pieces = [give(pick(qkv_cut, (y + by) % 4, 0), "y", by) for by in (3, 2, 1)]
    qkv_ring = jnp.concatenate([pick(qkv_cut, y, 0)] + qkv_pieces, axis=0)
    input_back = rows_call(
        input_body,
        [((row_count, model_width), low), ((8, model_width), wide)],
        "input_back",
    )
    tokens_grad, input_gain_rows = input_back(
        query_grad, pair_grad, full_qkv, tokens, state_grad, one_input
    )

    def spread_head(vector):
        return jnp.pad(
            vector.reshape(16, head_shard), ((0, 0), (0, gain_shard - head_shard))
        ).reshape(model_width)

    gain_block = jnp.stack(
        [
            input_gain_rows[0],
            state_gain_rows[8],
            state_gain_rows[0],
            output_gain_rows[0],
            spread_head(query_gain_rows[0]),
            spread_head(key_gain_rows[0]),
        ],
        axis=1,
    )
    gain_block = jnp.pad(gain_block, ((0, 0), (0, 122)))
    chip = jnp.concatenate(
        [added(product(core, input_ring, qkv_ring, gain_block)), out_sum.astype(low)], axis=1
    )
    attention_sum, attention_column = small_sum(chip.reshape(4, 2, rows72, chip.shape[1]))
    attention_blocks = in_order(
        [attention_sum] + [take(attention_sum, "y", by) for by in (1, 2, 3)]
    )
    feed_sums = lax.all_gather(ordered(feed_sum, attention_column), SEQ, axis=0, tiled=False)
    gate_weight_grad, up_weight_grad, down_weight_grad = rows_call(
        spread_out_body, [((rows72, feed_width), wide)] * 3, "spread_out"
    )(feed_sums)
    qkv_cols = qkv_width // 4
    out_cols = query_width // 4
    qkv_weight_grad = jnp.concatenate([b[:, :qkv_cols] for b in attention_blocks], axis=1)
    out_weight_grad = jnp.concatenate([b[:, qkv_cols + 128 :] for b in attention_blocks], axis=1)
    gain_sum = sum(b[:, qkv_cols : qkv_cols + 128].astype(wide) for b in attention_blocks)
    return (
        layer_output,
        tokens_grad,
        qkv_weight_grad[:, :query_width].astype(wide),
        qkv_weight_grad[:, query_width : query_width + head_size].astype(wide),
        qkv_weight_grad[:, query_width + head_size :].astype(wide),
        out_weight_grad.astype(wide),
        gate_weight_grad,
        up_weight_grad,
        down_weight_grad,
        gain_sum[:, 0],
        gain_sum[:head_shard, 4],
        gain_sum[:head_shard, 5],
        gain_sum[:, 1],
        gain_sum[:, 2],
        gain_sum[:, 3],
    )


def solution(mesh):
    fine = Mesh(mesh.devices.reshape(SIZES), AXES)
    rows = P(AXES, None)
    matrix = P(DP, None)
    vector = P(DP)
    return jax.shard_map(
        local,
        mesh=fine,
        in_specs=(rows, rows, vector) + (matrix,) * 7 + (vector,) * 6,
        out_specs=(rows, rows) + (matrix,) * 7 + (vector,) * 6,
        check_vma=False,
    )
```

time: 474 us -> 443 us (0.935)
  matrix products: 87.4 us -> 3.24 us
  Pallas kernels: 8.74 us -> 75.6 us
  local copies, waits for them, and re-layouts: 37.6 us -> 65 us
  other arithmetic: 48.3 us -> 22.8 us
  waiting for transfers between devices: 187 us -> 172 us
    dot_general x19 -> x1, matrix products: 87.4 us -> 3.24 us  [local(): jnp.dot(attention_input, full_qkv[:, :qkv_width], preferred_element_type=...]
    pallas_call x0 -> x11, Pallas kernels: none -> 56.8 us  [the longest x6 37.7 us: feed_call(): pl.pallas_call(functools.partial(body, place), in_specs=[whole] * first_k...]
    unnamed x154 -> x159, local copies, waits for them, and re-layouts: 9.34 us -> 37.5 us
    ppermute x21 -> x18, waiting for transfers between devices: 77.2 us -> 98 us  [take(): lax.ppermute(array, axis, [((i + by) % count, i) for i in range(count)])]
    ppermute x26 -> x23, waiting for transfers between devices: 70.5 us -> 50.9 us  [give(): lax.ppermute(array, axis, [(i, (i + by) % count) for i in range(count)])]
    convert_element_type x24 -> x8, other arithmetic: 28.1 us -> 9.18 us  [the longest x1 5.9 us: attention_input_of(): return (values * inverse_rms(values) * one_input).astype(low)]
    ppermute x4, waiting for transfers between devices: 25.9 us -> 8.2 us  [from_behind(): return lax.ppermute(array, SEQ, pairs)]
    ppermute x26 -> x23, starting transfers between devices: 24.8 us -> 40.1 us  [give(): lax.ppermute(array, axis, [(i, (i + by) % count) for i in range(count)])]
  transfers between devices with their start and end apart: 59 -> 50, of which waited for: 36 -> 26; matrix products, arithmetic and copies ran while one was open for 30% -> 12% of each run, Pallas kernels for 2% -> 15%
where the time goes in v4:
time: 443 us; the launch traced here: 434 us
  waiting for transfers between devices  172 us (39%)
  starting transfers between devices  79.5 us (18%)
  Pallas kernels  75.6 us (17%)
  local copies, waits for them, and re-layouts  65 us (15%)
  other arithmetic  22.8 us (5%)
  between operations  16.2 us (4%)
    ppermute x18, waiting for transfers between devices, take(): lax.ppermute(array, axis, [((i + by) % count, i) for i in range(count)])  98 us
    ppermute x23, waiting for transfers between devices, give(): lax.ppermute(array, axis, [(i, (i + by) % count) for i in range(count)])  50.9 us
    ppermute x23, starting transfers between devices, give(): lax.ppermute(array, axis, [(i, (i + by) % count) for i in range(count)])  40.1 us
    pallas_call x6, Pallas kernels, feed_call(): pl.pallas_call(functools.partial(body, place), in_specs=[whole] * first_k...  37.7 us
    unnamed x159, local copies, waits for them, and re-layouts  37.5 us
    ppermute x18, starting transfers between devices, take(): lax.ppermute(array, axis, [((i + by) % count, i) for i in range(count)])  28.2 us
    pallas_call x5, Pallas kernels, product(): pl.pallas_call(product_body, in_specs=[pl.BlockSpec(memory_space=pltpu.SM...  19.1 us
    pallas_call x10, Pallas kernels, call(): pl.pallas_call(body, out_shape=[jax.ShapeDtypeStruct(shape, dtype) for sh...  18.8 us
  transfers between devices with their start and end apart: 50, of which 26 were waited for; matrix products, arithmetic and copies ran while one was open for 12% of the time, Pallas kernels for 15%

profile of v4, /device:TPU:0, one launch (start us, length us, event | category | flops | bytes accessed | tf_op | source)
XLA Modules:
  0.0 433.8 jit_solution(18185065502518513104)
XLA Ops:
  13.8 9.0 %collective-permute-done = bf16[72,2688]{1,0:T(8,128)(2,1)S(1)} collective-permute-done((bf16[72,2688]{1,0:T(8,128)(2,1)S(1)}, bf16[72,2688]{1,0:T(8,128)(2,1)S(1)}, u32[]{:S(2)}, u32[]{:S(2)}) %collective-permute-start) | collective-permute-done | bytes 387104 | tf_op jit(solution)/shard_map/ppermute | solution.py:45
  25.8 4.2 collective-permute-start.1
  33.2 16.9 %collective-permute-done.1 = bf16[2,72,1664]{2,1,0:T(8,128)(2,1)S(1)} collective-permute-done((bf16[2,72,1664]{2,1,0:T(8,128)(2,1)}, bf16[2,72,1664]{2,1,0:T(8,128)(2,1)S(1)}, u32[]{:S(2)}, u32[]{:S(2)}) %collective-permute-start.1) | collective-permute-done | bytes 479264 | tf_op jit(solution)/shard_map/ppermute | solution.py:36
  50.1 11.5 %collective-permute-done.2 = bf16[2,72,1664]{2,1,0:T(8,128)(2,1)S(1)} collective-permute-done((bf16[2,72,1664]{2,1,0:T(8,128)(2,1)}, bf16[2,72,1664]{2,1,0:T(8,128)(2,1)S(1)}, u32[]{:S(2)}, u32[]{:S(2)}) %collective-permute-start.2) | collective-permute-done | bytes 479264 | tf_op jit(solution)/shard_map/ppermute | solution.py:36
  89.6 8.2 %collective-permute-done.12 = bf16[2,72,1024]{2,1,0:T(8,128)(2,1)S(1)} collective-permute-done((bf16[2,72,1024]{2,1,0:T(8,128)(2,1)}, bf16[2,72,1024]{2,1,0:T(8,128)(2,1)S(1)}, u32[]{:S(2)}, u32[]{:S(2)}) %collective-permute-start.12) | collective-permute-done | bytes 294944 | tf_op jit(solution)/shard_map/ppermute | solution.py:36
  105.0 5.9 %fusion.2.left = bf16[1024,1152]{1,0:T(8,128)(2,1)} fusion(f32[1152]{0:T(1024)S(1)} %copy-done.66, f32[1024]{0:T(1024)S(1)} %add_rsqrt_fusion, bf16[256,1152]{1,0:T(8,128)(2,1)S(1)} %collective-permute-done.9, bf16[256,1152]{1,0:T(8,128)(2,1)} %collective-permute-done.8, bf16[256,1152]{1,0:T(8,128)(2,1)} %collective-permute-done.7, ...), kind=kLoop, calls=%fused_computation.4 | loop fusion | flops 12976128 | bytes 4727296 | tf_op jit(solution)/shard_map/convert_element_type | solution.py:633
  121.0 4.0 collective-permute-start.16
  127.6 11.5 %collective-permute-done.16.rows = bf16[256,1152]{1,0:T(8,128)(2,1)S(1)} collective-permute-done((bf16[256,1152]{1,0:T(8,128)(2,1)S(1)}, bf16[256,1152]{1,0:T(8,128)(2,1)S(1)}, u32[]{:S(2)}, u32[]{:S(2)}) %collective-permute-start.16) | collective-permute-done | bytes 589856 | tf_op jit(solution)/shard_map/ppermute | solution.py:36
  139.1 4.5 %copy-done = bf16[1152,5376]{1,0:T(8,128)(2,1)S(1)} copy-done((bf16[1152,5376]{1,0:T(8,128)(2,1)S(1)}, bf16[1152,5376]{1,0:T(8,128)(2,1)}, u32[]{:S(2)}) %copy-start) | copy-done | bytes 12386328
  143.6 5.1 %feed.3 = (bf16[1024,1792]{1,0:T(8,128)(2,1)S(1)}, bf16[1024,1792]{1,0:T(8,128)(2,1)S(1)}, bf16[1024,1792]{1,0:T(8,128)(2,1)S(1)}, bf16[256,1152]{1,0:T(8,128)(2,1)S(1)}) custom-call(bf16[256,1152]{1,0:T(8,128)(2,1)S(1)} %collective-permute-done.16.rows, bf16[1152,5376]{1,0:T(8,128)(2,1)S(1)} %copy-done), custom_call_target="tpu_custom_call" | custom-call | flops 1000 | bytes 1000 | tf_op jit(solution)/shard_map/feed/pallas_call | solution.py:456
  152.7 9.2 %feed.4 = (bf16[1024,1792]{1,0:T(8,128)(2,1)S(1)}, bf16[1024,1792]{1,0:T(8,128)(2,1)S(1)}, bf16[1024,1792]{1,0:T(8,128)(2,1)S(1)}, bf16[512,1152]{1,0:T(8,128)(2,1)S(1)}) custom-call(bf16[512,1152]{1,0:T(8,128)(2,1)S(1)} %constant_dynamic-update-slice_fusion.5.rows, ...), custom_call_target="tpu_custom_call", output_to_operand_aliasing={{0}: (2, {}), {1}: (3, {}), {2}: (4, {})} | custom-call | flops 12000000000 | bytes 1000 | tf_op jit(solution)/shard_map/feed/pallas_call | solution.py:456
  164.7 5.0 %feed.5 = (bf16[1024,1792]{1,0:T(8,128)(2,1)S(1)}, bf16[1024,1792]{1,0:T(8,128)(2,1)S(1)}, bf16[1024,1792]{1,0:T(8,128)(2,1)S(1)}, bf16[256,1152]{1,0:T(8,128)(2,1)S(1)}) custom-call(bf16[256,1152]{1,0:T(8,128)(2,1)S(1)} %get-tuple-element.102.rows, bf16[1152,5376]{1,0:T(8,128)(2,1)S(1)} %copy-done.1, ...), custom_call_target="tpu_custom_call", output_to_operand_aliasing={{0}: (2, {}), {1}: (3, {}), {2}: (4, {})} | custom-call | flops 12000000000 | bytes 1000 | tf_op jit(solution)/shard_map/feed/pallas_call | solution.py:456
  169.7 7.1 %collective-permute-done.19.behind = bf16[256,1152]{1,0:T(8,128)(2,1)S(1)} collective-permute-done((bf16[256,1152]{1,0:T(8,128)(2,1)S(1)}, bf16[256,1152]{1,0:T(8,128)(2,1)S(1)}, u32[]{:S(2)}, u32[]{:S(2)}) %collective-permute-start.19) | collective-permute-done | bytes 589856 | tf_op jit(solution)/shard_map/ppermute | solution.py:41
  186.2 13.8 %collective-permute-done.22.rows = bf16[256,1152]{1,0:T(8,128)(2,1)S(1)} collective-permute-done((bf16[256,1152]{1,0:T(8,128)(2,1)S(1)}, bf16[256,1152]{1,0:T(8,128)(2,1)S(1)}, u32[]{:S(2)}, u32[]{:S(2)}) %collective-permute-start.22) | collective-permute-done | bytes 589856 | tf_op jit(solution)/shard_map/ppermute | solution.py:36
  200.0 4.8 %feed_back.3 = (bf16[1024,1792]{1,0:T(8,128)(2,1)S(1)}, bf16[1024,1792]{1,0:T(8,128)(2,1)S(1)}, bf16[256,1152]{1,0:T(8,128)(2,1)S(1)}) custom-call(bf16[256,1152]{1,0:T(8,128)(2,1)S(1)} %collective-permute-done.22.rows, bf16[1152,5376]{1,0:T(8,128)(2,1)S(1)} %copy-done.1, bf16[1024,1792]{1,0:T(8,128)(2,1)S(1)} %get-tuple-element.120.value, ...), custom_call_target="tpu_custom_call" | custom-call | flops 1000 | bytes 1000 | tf_op jit(solution)/shard_map/feed_back/pallas_call | solution.py:456
  205.8 4.6 %collective-permute-done.20 = bf16[256,1152]{1,0:T(8,128)(2,1)S(1)} collective-permute-done((bf16[256,1152]{1,0:T(8,128)(2,1)S(1)}, bf16[256,1152]{1,0:T(8,128)(2,1)S(1)}, u32[]{:S(2)}, u32[]{:S(2)}) %collective-permute-start.20) | collective-permute-done | bytes 589856 | tf_op jit(solution)/shard_map/ppermute | solution.py:36
  212.6 8.9 %feed_back.4 = (bf16[1024,1792]{1,0:T(8,128)(2,1)S(1)}, bf16[1024,1792]{1,0:T(8,128)(2,1)S(1)}, bf16[512,1152]{1,0:T(8,128)(2,1)S(1)}) custom-call(bf16[512,1152]{1,0:T(8,128)(2,1)S(1)} %constant_dynamic-update-slice_fusion.7.rows, bf16[1152,5376]{1,0:T(8,128)(2,1)S(1)} %copy-done.1, ...), custom_call_target="tpu_custom_call", output_to_operand_aliasing={{0}: (4, {}), {1}: (5, {})} | custom-call | flops 12000000000 | bytes 1000 | tf_op jit(solution)/shard_map/feed_back/pallas_call | solution.py:456
  224.6 4.8 %feed_back.5 = (bf16[1024,1792]{1,0:T(8,128)(2,1)S(1)}, bf16[1024,1792]{1,0:T(8,128)(2,1)S(1)}, bf16[256,1152]{1,0:T(8,128)(2,1)S(1)}) custom-call(bf16[256,1152]{1,0:T(8,128)(2,1)S(1)} %get-tuple-element.119.rows, bf16[1152,5376]{1,0:T(8,128)(2,1)S(1)} %copy-done.1, ...), custom_call_target="tpu_custom_call", output_to_operand_aliasing={{0}: (4, {}), {1}: (5, {})} | custom-call | flops 12000000000 | bytes 1000 | tf_op jit(solution)/shard_map/feed_back/pallas_call | solution.py:456
  229.4 7.4 %collective-permute-done.25.behind = bf16[256,1152]{1,0:T(8,128)(2,1)S(1)} collective-permute-done((bf16[256,1152]{1,0:T(8,128)(2,1)S(1)}, bf16[256,1152]{1,0:T(8,128)(2,1)S(1)}, u32[]{:S(2)}, u32[]{:S(2)}) %collective-permute-start.25) | collective-permute-done | bytes 589856 | tf_op jit(solution)/shard_map/ppermute | solution.py:41
  239.2 5.1 %product.9 = (bf16[576,1792]{1,0:T(8,128)(2,1)S(1)}, bf16[576,1792]{1,0:T(8,128)(2,1)S(1)}) custom-call(s32[1]{0:T(128)} %bitcast.25.core, bf16[1024,1152]{1,0:T(8,128)(2,1)S(1)} %pad_maximum_fusion.1.left, bf16[1024,1792]{1,0:T(8,128)(2,1)S(1)} %get-tuple-element.164.right), custom_call_target="tpu_custom_call" | custom-call | flops 1000 | bytes 1000 | tf_op jit(solution)/shard_map/product/pallas_call | solution.py:503
  244.6 5.1 %product.7 = (bf16[576,1792]{1,0:T(8,128)(2,1)S(1)}, bf16[576,1792]{1,0:T(8,128)(2,1)S(1)}) custom-call(s32[1]{0:T(128)} %bitcast.25.core, bf16[1024,1152]{1,0:T(8,128)(2,1)S(1)} %constant_dynamic-update-slice_fusion.9.left, bf16[1024,1792]{1,0:T(8,128)(2,1)S(1)} %get-tuple-element.156.right), custom_call_target="tpu_custom_call" | custom-call | flops 1000 | bytes 1000 | tf_op jit(solution)/shard_map/product/pallas_call | solution.py:503
  250.3 5.1 %product.8 = (bf16[576,1792]{1,0:T(8,128)(2,1)S(1)}, bf16[576,1792]{1,0:T(8,128)(2,1)S(1)}) custom-call(s32[1]{0:T(128)} %bitcast.25.core, bf16[1024,1152]{1,0:T(8,128)(2,1)S(1)} %constant_dynamic-update-slice_fusion.9.left, bf16[1024,1792]{1,0:T(8,128)(2,1)S(1)} %get-tuple-element.159.right), custom_call_target="tpu_custom_call" | custom-call | flops 1000 | bytes 1000 | tf_op jit(solution)/shard_map/product/pallas_call | solution.py:503
  255.5 4.1 collective-permute-done.45.up_got
  277.5 5.3 %attend_back.1 = (bf16[256,512]{1,0:T(8,128)(2,1)S(1)}, bf16[256,512]{1,0:T(8,128)(2,1)}, f32[256,512]{1,0:T(8,128)S(1)}, bf16[256,1024]{1,0:T(8,128)(2,1)S(1)}, f32[8,256]{1,0:T(8,128)S(1)}) custom-call(s32[1]{0:T(128)} %bitcast.place, bf16[256,1152]{1,0:T(8,128)(2,1)S(1)} %get-tuple-element.151.upstream.left, bf16[1152,1024]{1,0:T(8,128)(2,1)S(1)} %bitcast.87, ...), custom_call_target="tpu_custom_call" | custom-call | flops 1000 | bytes 1000 | tf_op jit(solution)/shard_map/attend_back/pallas_call | solution.py:158
  293.5 5.0 %collective-permute-done.27.far = bf16[256,512]{1,0:T(8,128)(2,1)S(1)} collective-permute-done((bf16[256,512]{1,0:T(8,128)(2,1)}, bf16[256,512]{1,0:T(8,128)(2,1)S(1)}, u32[]{:S(2)}, u32[]{:S(2)}) %collective-permute-start.27) | collective-permute-done | bytes 262176 | tf_op jit(solution)/shard_map/ppermute | solution.py:31
  307.8 14.3 %collective-permute-start.29 = (bf16[256,384]{1,0:T(8,128)(2,1)}, bf16[256,384]{1,0:T(8,128)(2,1)}, u32[]{:S(2)}, u32[]{:S(2)}) collective-permute-start(bf16[256,384]{1,0:T(8,128)(2,1)} %get-tuple-element.190), channel_id=1, source_target_pairs={{0,2},{1,3},{2,0},{3,1},{4,6},{5,7},{6,4},{7,5},{8,10},{9,11},{10,... | collective-permute-start | bytes 589832 | tf_op jit(solution)/shard_map/ppermute | solution.py:41
  351.4 6.1 %collective-permute-done.33 = bf16[576,256]{1,0:T(8,128)(2,1)S(1)} collective-permute-done((bf16[576,256]{1,0:T(8,128)(2,1)S(1)}, bf16[576,256]{1,0:T(8,128)(2,1)S(1)}, u32[]{:S(2)}, u32[]{:S(2)}) %collective-permute-start.33) | collective-permute-done | bytes 294944 | tf_op jit(solution)/shard_map/ppermute | solution.py:41
  361.1 10.1 %collective-permute-done.36 = bf16[2,72,768]{2,1,0:T(8,128)(2,1)S(1)} collective-permute-done((bf16[2,72,768]{2,1,0:T(8,128)(2,1)S(1)}, bf16[2,72,768]{2,1,0:T(8,128)(2,1)S(1)}, u32[]{:S(2)}, u32[]{:S(2)}) %collective-permute-start.36) | collective-permute-done | bytes 221216 | tf_op jit(solution)/shard_map/ppermute | solution.py:41
  372.7 5.3 %collective-permute-done.39 = bf16[72,768]{1,0:T(8,128)(2,1)S(1)} collective-permute-done((bf16[72,768]{1,0:T(8,128)(2,1)S(1)}, bf16[72,768]{1,0:T(8,128)(2,1)S(1)}, u32[]{:S(2)}, u32[]{:S(2)}) %collective-permute-start.39) | collective-permute-done | bytes 110624 | tf_op jit(solution)/shard_map/ppermute | solution.py:45
  378.1 6.9 %collective-permute-done.40 = bf16[72,768]{1,0:T(8,128)(2,1)S(1)} collective-permute-done((bf16[72,768]{1,0:T(8,128)(2,1)S(1)}, bf16[72,768]{1,0:T(8,128)(2,1)S(1)}, u32[]{:S(2)}, u32[]{:S(2)}) %collective-permute-start.40) | collective-permute-done | bytes 110624 | tf_op jit(solution)/shard_map/ppermute | solution.py:41
  388.2 14.3 %collective-permute-done.43 = bf16[72,768]{1,0:T(8,128)(2,1)S(1)} collective-permute-done((bf16[72,768]{1,0:T(8,128)(2,1)S(1)}, bf16[72,768]{1,0:T(8,128)(2,1)S(1)}, u32[]{:S(2)}, u32[]{:S(2)}) %collective-permute-start.43) | collective-permute-done | bytes 110624 | tf_op jit(solution)/shard_map/ppermute | solution.py:36
  402.5 15.2 %collective-permute-done.42 = bf16[72,768]{1,0:T(8,128)(2,1)S(1)} collective-permute-done((bf16[72,768]{1,0:T(8,128)(2,1)S(1)}, bf16[72,768]{1,0:T(8,128)(2,1)S(1)}, u32[]{:S(2)}, u32[]{:S(2)}) %collective-permute-start.42) | collective-permute-done | bytes 110624 | tf_op jit(solution)/shard_map/ppermute | solution.py:36
  (339 shorter events, 169.4 us)
Async XLA Ops:
  7.2 113.8 %all-gather.4.cloned.1.call-start = ((), (), s32[]{:S(2)}) async-start(), calls=%async_computation.1 | async-start | bytes 13160448 | tf_op jit(solution)/shard_map/all_gather | solution.py:612
  10.5 361.4 %reduce-scatter.4.cloned.1.call-start = ((), (), s32[]{:S(2)}) async-start(), calls=%async_computation.3 | async-start | bytes 6580224
  25.8 24.2 %collective-permute-start.1 = (bf16[2,72,1664]{2,1,0:T(8,128)(2,1)}, bf16[2,72,1664]{2,1,0:T(8,128)(2,1)S(1)}, u32[]{:S(2)}, u32[]{:S(2)}) collective-permute-start(bf16[2,72,1664]{2,1,0:T(8,128)(2,1)} %slice.163), channel_id=1, source_target_pairs={{32,0},{64,32},{96,64},{0,96},{33,1},{65,33},{97,65},{1,97},{34,2}... | collective-permute-start | bytes 1437704 | tf_op jit(solution)/shard_map/ppermute | solution.py:36
  30.0 31.5 %collective-permute-start.2 = (bf16[2,72,1664]{2,1,0:T(8,128)(2,1)}, bf16[2,72,1664]{2,1,0:T(8,128)(2,1)S(1)}, u32[]{:S(2)}, u32[]{:S(2)}) collective-permute-start(bf16[2,72,1664]{2,1,0:T(8,128)(2,1)} %slice.163), channel_id=1, source_target_pairs={{96,0},{0,32},{32,64},{64,96},{97,1},{1,33},{33,65},{65,97},{98,2}... | collective-permute-start | bytes 1437704 | tf_op jit(solution)/shard_map/ppermute | solution.py:36
  30.0 31.6 %collective-permute-start.3 = (bf16[2,72,1664]{2,1,0:T(8,128)(2,1)}, bf16[2,72,1664]{2,1,0:T(8,128)(2,1)S(1)}, u32[]{:S(2)}, u32[]{:S(2)}) collective-permute-start(bf16[2,72,1664]{2,1,0:T(8,128)(2,1)} %slice.163), channel_id=1, source_target_pairs={{64,0},{96,32},{0,64},{32,96},{65,1},{97,33},{1,65},{33,97},{66,2}... | collective-permute-start | bytes 1437704 | tf_op jit(solution)/shard_map/ppermute | solution.py:36
  64.4 34.1 %collective-permute-start.9 = (bf16[256,1152]{1,0:T(8,128)(2,1)S(1)}, bf16[256,1152]{1,0:T(8,128)(2,1)S(1)}, u32[]{:S(2)}, u32[]{:S(2)}) collective-permute-start(bf16[256,1152]{1,0:T(8,128)(2,1)S(1)} %copy-done.5), channel_id=1, source_target_pairs={{3,0},{0,1},{1,2},{2,3},{7,4},{4,5},{5,6},{6,7},{11,8},{8,9},{9,10... | collective-permute-start | bytes 1769480 | tf_op jit(solution)/shard_map/ppermute | solution.py:36
  66.0 32.5 %collective-permute-start.8 = (bf16[256,1152]{1,0:T(8,128)(2,1)S(1)}, bf16[256,1152]{1,0:T(8,128)(2,1)}, u32[]{:S(2)}, u32[]{:S(2)}) collective-permute-start(bf16[256,1152]{1,0:T(8,128)(2,1)S(1)} %copy-done.5), channel_id=1, source_target_pairs={{2,0},{3,1},{0,2},{1,3},{6,4},{7,5},{4,6},{5,7},{10,8},{11,9},{8,1... | collective-permute-start | bytes 1769480 | tf_op jit(solution)/shard_map/ppermute | solution.py:36
  68.9 29.6 %collective-permute-start.7 = (bf16[256,1152]{1,0:T(8,128)(2,1)S(1)}, bf16[256,1152]{1,0:T(8,128)(2,1)}, u32[]{:S(2)}, u32[]{:S(2)}) collective-permute-start(bf16[256,1152]{1,0:T(8,128)(2,1)S(1)} %copy-done.5), channel_id=1, source_target_pairs={{1,0},{2,1},{3,2},{0,3},{5,4},{6,5},{7,6},{4,7},{9,8},{10,9},{11,1... | collective-permute-start | bytes 1769480 | tf_op jit(solution)/shard_map/ppermute | solution.py:36
  70.3 17.6 %collective-permute-start.11 = (bf16[2,72,1024]{2,1,0:T(8,128)(2,1)}, bf16[2,72,1024]{2,1,0:T(8,128)(2,1)}, u32[]{:S(2)}, u32[]{:S(2)}) collective-permute-start(bf16[2,72,1024]{2,1,0:T(8,128)(2,1)} %slice.168), channel_id=1, source_target_pairs={{96,0},{0,32},{32,64},{64,96},{97,1},{1,33},{33,65},{65,97},{98,2}... | collective-permute-start | bytes 884744 | tf_op jit(solution)/shard_map/ppermute | solution.py:36
  98.5 17.0 %collective-permute-start.13 = (bf16[4,2,72,1024]{3,2,1,0:T(8,128)(2,1)}, bf16[4,2,72,1024]{3,2,1,0:T(8,128)(2,1)S(1)}, u32[]{:S(2)}, u32[]{:S(2)}) collective-permute-start(bf16[4,2,72,1024]{3,2,1,0:T(8,128)(2,1)} %bitcast_dynamic-update-slice_fusion.4), channel_id=1, source_target_pairs={{0,8},{8,0},{1,9},{9,1},{2,10},{10,2},{3,11},{11,3},{4,12},{12,4},... | collective-permute-start | bytes 3538952 | tf_op jit(solution)/shard_map/ppermute | solution.py:41
  121.0 18.2 %collective-permute-start.16 = (bf16[256,1152]{1,0:T(8,128)(2,1)S(1)}, bf16[256,1152]{1,0:T(8,128)(2,1)S(1)}, u32[]{:S(2)}, u32[]{:S(2)}) collective-permute-start(bf16[256,1152]{1,0:T(8,128)(2,1)S(1)} %get-tuple-element.102.rows), channel_id=1, source_target_pairs={{2,0},{3,1},{0,2},{1,3},{6,4},{7,5},{4,6},{5,7},{10,8},{11,9},{8,1... | collective-permute-start | bytes 1769480 | tf_op jit(solution)/shard_map/ppermute | solution.py:36
  124.9 27.6 %collective-permute-start.14 = (bf16[256,1152]{1,0:T(8,128)(2,1)S(1)}, bf16[256,1152]{1,0:T(8,128)(2,1)S(1)}, u32[]{:S(2)}, u32[]{:S(2)}) collective-permute-start(bf16[256,1152]{1,0:T(8,128)(2,1)S(1)} %get-tuple-element.102.rows), channel_id=1, source_target_pairs={{1,0},{2,1},{3,2},{0,3},{5,4},{6,5},{7,6},{4,7},{9,8},{10,9},{11,1... | collective-permute-start | bytes 1769480 | tf_op jit(solution)/shard_map/ppermute | solution.py:36
  126.1 26.5 %collective-permute-start.15 = (bf16[256,1152]{1,0:T(8,128)(2,1)S(1)}, bf16[256,1152]{1,0:T(8,128)(2,1)S(1)}, u32[]{:S(2)}, u32[]{:S(2)}) collective-permute-start(bf16[256,1152]{1,0:T(8,128)(2,1)S(1)} %get-tuple-element.102.rows), channel_id=1, source_target_pairs={{3,0},{0,1},{1,2},{2,3},{7,4},{4,5},{5,6},{6,7},{11,8},{8,9},{9,10... | collective-permute-start | bytes 1769480 | tf_op jit(solution)/shard_map/ppermute | solution.py:36
  148.7 16.0 %collective-permute-start.17 = (bf16[256,1152]{1,0:T(8,128)(2,1)S(1)}, bf16[256,1152]{1,0:T(8,128)(2,1)S(1)}, u32[]{:S(2)}, u32[]{:S(2)}) collective-permute-start(bf16[256,1152]{1,0:T(8,128)(2,1)S(1)} %get-tuple-element.110), channel_id=1, source_target_pairs={{0,2},{1,3},{2,0},{3,1},{4,6},{5,7},{6,4},{7,5},{8,10},{9,11},{10,... | collective-permute-start | bytes 1769480 | tf_op jit(solution)/shard_map/ppermute | solution.py:41
  162.1 14.7 %collective-permute-start.19 = (bf16[256,1152]{1,0:T(8,128)(2,1)S(1)}, bf16[256,1152]{1,0:T(8,128)(2,1)S(1)}, u32[]{:S(2)}, u32[]{:S(2)}) collective-permute-start(bf16[256,1152]{1,0:T(8,128)(2,1)S(1)} %get-tuple-element.183), channel_id=1, source_target_pairs={{0,3},{1,0},{2,1},{3,2},{4,7},{5,4},{6,5},{7,6},{8,11},{9,8},{10,9... | collective-permute-start | bytes 1769480 | tf_op jit(solution)/shard_map/ppermute | solution.py:41
  163.6 16.2 %collective-permute-start.18 = (bf16[256,1152]{1,0:T(8,128)(2,1)S(1)}, bf16[256,1152]{1,0:T(8,128)(2,1)S(1)}, u32[]{:S(2)}, u32[]{:S(2)}) collective-permute-start(bf16[256,1152]{1,0:T(8,128)(2,1)S(1)} %get-tuple-element.184), channel_id=1, source_target_pairs={{0,1},{1,2},{2,3},{3,0},{4,5},{5,6},{6,7},{7,4},{8,9},{9,10},{10,1... | collective-permute-start | bytes 1769480 | tf_op jit(solution)/shard_map/ppermute | solution.py:41
  182.2 17.8 %collective-permute-start.22 = (bf16[256,1152]{1,0:T(8,128)(2,1)S(1)}, bf16[256,1152]{1,0:T(8,128)(2,1)S(1)}, u32[]{:S(2)}, u32[]{:S(2)}) collective-permute-start(bf16[256,1152]{1,0:T(8,128)(2,1)S(1)} %get-tuple-element.119.rows), channel_id=1, source_target_pairs={{2,0},{3,1},{0,2},{1,3},{6,4},{7,5},{4,6},{5,7},{10,8},{11,9},{8,1... | collective-permute-start | bytes 1769480 | tf_op jit(solution)/shard_map/ppermute | solution.py:36
  182.7 29.8 %collective-permute-start.21 = (bf16[256,1152]{1,0:T(8,128)(2,1)S(1)}, bf16[256,1152]{1,0:T(8,128)(2,1)S(1)}, u32[]{:S(2)}, u32[]{:S(2)}) collective-permute-start(bf16[256,1152]{1,0:T(8,128)(2,1)S(1)} %get-tuple-element.119.rows), channel_id=1, source_target_pairs={{3,0},{0,1},{1,2},{2,3},{7,4},{4,5},{5,6},{6,7},{11,8},{8,9},{9,10... | collective-permute-start | bytes 1769480 | tf_op jit(solution)/shard_map/ppermute | solution.py:36
  183.5 26.9 %collective-permute-start.20 = (bf16[256,1152]{1,0:T(8,128)(2,1)S(1)}, bf16[256,1152]{1,0:T(8,128)(2,1)S(1)}, u32[]{:S(2)}, u32[]{:S(2)}) collective-permute-start(bf16[256,1152]{1,0:T(8,128)(2,1)S(1)} %get-tuple-element.119.rows), channel_id=1, source_target_pairs={{1,0},{2,1},{3,2},{0,3},{5,4},{6,5},{7,6},{4,7},{9,8},{10,9},{11,1... | collective-permute-start | bytes 1769480 | tf_op jit(solution)/shard_map/ppermute | solution.py:36
  204.8 19.0 %collective-permute-start.23 = (bf16[256,1152]{1,0:T(8,128)(2,1)S(1)}, bf16[256,1152]{1,0:T(8,128)(2,1)S(1)}, u32[]{:S(2)}, u32[]{:S(2)}) collective-permute-start(bf16[256,1152]{1,0:T(8,128)(2,1)S(1)} %get-tuple-element.126), channel_id=1, source_target_pairs={{0,2},{1,3},{2,0},{3,1},{4,6},{5,7},{6,4},{7,5},{8,10},{9,11},{10,... | collective-permute-start | bytes 1769480 | tf_op jit(solution)/shard_map/ppermute | solution.py:41
  221.6 15.2 %collective-permute-start.25 = (bf16[256,1152]{1,0:T(8,128)(2,1)S(1)}, bf16[256,1152]{1,0:T(8,128)(2,1)S(1)}, u32[]{:S(2)}, u32[]{:S(2)}) collective-permute-start(bf16[256,1152]{1,0:T(8,128)(2,1)S(1)} %get-tuple-element.181), channel_id=1, source_target_pairs={{0,3},{1,0},{2,1},{3,2},{4,7},{5,4},{6,5},{7,6},{8,11},{9,8},{10,9... | collective-permute-start | bytes 1769480 | tf_op jit(solution)/shard_map/ppermute | solution.py:41
  222.4 15.9 %collective-permute-start.24 = (bf16[256,1152]{1,0:T(8,128)(2,1)S(1)}, bf16[256,1152]{1,0:T(8,128)(2,1)S(1)}, u32[]{:S(2)}, u32[]{:S(2)}) collective-permute-start(bf16[256,1152]{1,0:T(8,128)(2,1)S(1)} %get-tuple-element.182), channel_id=1, source_target_pairs={{0,1},{1,2},{2,3},{3,0},{4,5},{5,6},{6,7},{7,4},{8,9},{9,10},{10,1... | collective-permute-start | bytes 1769480 | tf_op jit(solution)/shard_map/ppermute | solution.py:41
  263.6 158.5 %all-gather.6.cloned.1.call-start = ((), (), s32[]{:S(2)}) async-start(), calls=%async_computation.2 | async-start | bytes 3483648 | tf_op jit(solution)/shard_map/all_gather | solution.py:809
  285.1 13.8 %collective-permute-start.26 = (bf16[256,512]{1,0:T(8,128)(2,1)}, bf16[256,512]{1,0:T(8,128)(2,1)S(1)}, u32[]{:S(2)}, u32[]{:S(2)}) collective-permute-start(bf16[256,512]{1,0:T(8,128)(2,1)} %get-tuple-element.137), channel_id=1, source_target_pairs={{1,0},{2,1},{3,2},{4,3},{5,4},{6,5},{7,6},{9,8},{10,9},{11,10},{12... | collective-permute-start | bytes 786440 | tf_op jit(solution)/shard_map/ppermute | solution.py:31
  291.9 42.6 %collective-permute-start.32 = (bf16[576,1024]{1,0:T(8,128)(2,1)}, bf16[576,1024]{1,0:T(8,128)(2,1)}, u32[]{:S(2)}, u32[]{:S(2)}) collective-permute-start(bf16[576,1024]{1,0:T(8,128)(2,1)} %get-tuple-element.153), channel_id=1, source_target_pairs={{0,8},{8,0},{1,9},{9,1},{2,10},{10,2},{3,11},{11,3},{4,12},{12,4},... | collective-permute-start | bytes 3538952 | tf_op jit(solution)/shard_map/ppermute | solution.py:41
  305.5 25.7 %collective-permute-start.30 = (bf16[256,384]{1,0:T(8,128)(2,1)}, bf16[256,384]{1,0:T(8,128)(2,1)S(1)}, u32[]{:S(2)}, u32[]{:S(2)}) collective-permute-start(bf16[256,384]{1,0:T(8,128)(2,1)} %get-tuple-element.189), channel_id=1, source_target_pairs={{0,1},{1,2},{2,3},{3,0},{4,5},{5,6},{6,7},{7,4},{8,9},{9,10},{10,1... | collective-permute-start | bytes 589832 | tf_op jit(solution)/shard_map/ppermute | solution.py:41
  307.8 23.6 %collective-permute-start.29 = (bf16[256,384]{1,0:T(8,128)(2,1)}, bf16[256,384]{1,0:T(8,128)(2,1)}, u32[]{:S(2)}, u32[]{:S(2)}) collective-permute-start(bf16[256,384]{1,0:T(8,128)(2,1)} %get-tuple-element.190), channel_id=1, source_target_pairs={{0,2},{1,3},{2,0},{3,1},{4,6},{5,7},{6,4},{7,5},{8,10},{9,11},{10,... | collective-permute-start | bytes 589832 | tf_op jit(solution)/shard_map/ppermute | solution.py:41
  343.5 14.0 %collective-permute-start.33 = (bf16[576,256]{1,0:T(8,128)(2,1)S(1)}, bf16[576,256]{1,0:T(8,128)(2,1)S(1)}, u32[]{:S(2)}, u32[]{:S(2)}) collective-permute-start(bf16[576,256]{1,0:T(8,128)(2,1)S(1)} %bitcast.100), channel_id=1, source_target_pairs={{0,1},{1,2},{2,3},{3,0},{4,5},{5,6},{6,7},{7,4},{8,9},{9,10},{10,1... | collective-permute-start | bytes 884744 | tf_op jit(solution)/shard_map/ppermute | solution.py:41
  343.5 14.0 %collective-permute-start.34 = (bf16[576,256]{1,0:T(8,128)(2,1)S(1)}, bf16[576,256]{1,0:T(8,128)(2,1)S(1)}, u32[]{:S(2)}, u32[]{:S(2)}) collective-permute-start(bf16[576,256]{1,0:T(8,128)(2,1)S(1)} %bitcast.99), channel_id=1, source_target_pairs={{0,3},{1,0},{2,1},{3,2},{4,7},{5,4},{6,5},{7,6},{8,11},{9,8},{10,9... | collective-permute-start | bytes 884744 | tf_op jit(solution)/shard_map/ppermute | solution.py:41
  385.1 17.5 %collective-permute-start.43 = (bf16[72,768]{1,0:T(8,128)(2,1)S(1)}, bf16[72,768]{1,0:T(8,128)(2,1)S(1)}, u32[]{:S(2)}, u32[]{:S(2)}) collective-permute-start(bf16[72,768]{1,0:T(8,128)(2,1)S(1)} %add_convert_fusion.2), channel_id=1, source_target_pairs={{1,0},{2,1},{3,2},{0,3},{5,4},{6,5},{7,6},{4,7},{9,8},{10,9},{11,1... | collective-permute-start | bytes 331784 | tf_op jit(solution)/shard_map/ppermute | solution.py:36
  386.7 31.1 %collective-permute-start.42 = (bf16[72,768]{1,0:T(8,128)(2,1)S(1)}, bf16[72,768]{1,0:T(8,128)(2,1)S(1)}, u32[]{:S(2)}, u32[]{:S(2)}) collective-permute-start(bf16[72,768]{1,0:T(8,128)(2,1)S(1)} %add_convert_fusion.2), channel_id=1, source_target_pairs={{3,0},{0,1},{1,2},{2,3},{7,4},{4,5},{5,6},{6,7},{11,8},{8,9},{9,10... | collective-permute-start | bytes 331784 | tf_op jit(solution)/shard_map/ppermute | solution.py:36
  387.2 30.6 %collective-permute-start.41 = (bf16[72,768]{1,0:T(8,128)(2,1)S(1)}, bf16[72,768]{1,0:T(8,128)(2,1)S(1)}, u32[]{:S(2)}, u32[]{:S(2)}) collective-permute-start(bf16[72,768]{1,0:T(8,128)(2,1)S(1)} %add_convert_fusion.2), channel_id=1, source_target_pairs={{2,0},{3,1},{0,2},{1,3},{6,4},{7,5},{4,6},{5,7},{10,8},{11,9},{8,1... | collective-permute-start | bytes 331784 | tf_op jit(solution)/shard_map/ppermute | solution.py:36
  (91 other events, 572.0 us)
Sparse Core Ops, SparseCore 0:
  10.6 100.1 all-gather.3
  263.7 80.6 reduce-scatter.3
  372.1 45.0 all-gather.5
